TPU v7x, 32 devices: a whole 2x2x4 slice. The times are simulated.
32 devices in a mesh: groups: 2 (over y), expert: 8 (over z, core), section: 2 (over x).
Axes of the slice: x: 2, y: 2, z: 4, core: 2. Of those that a mesh axis runs over, the one named last changes fastest.
Arguments:
- activations: bfloat16 [2, 64, 128, 6144], P('section', 'groups', 'expert'), parts along dimension 1, may hold values from -6 to 6
- block_expert: int32 [2, 64, 1], P('section', 'groups'), parts along dimension 1, may hold values from 0 to 7; in each aligned block of 32 rows (0 to 31, 32 to 63, ..., all dimensions but the last counted through in order) at most 8 rows name the same one
- seq_task: int32 [2, 16], P('section', 'groups'), parts along dimension 1, may hold values from 0 to 7
- norm_gain: bfloat16 [2, 6144], P('section'), may hold values from 0.099609375 to 1.8984375
- task_embed: bfloat16 [8, 256], replicated, may hold values from -6 to 6
- expert_embed: bfloat16 [2, 8, 256], P('section'), may hold values from -6 to 6
- gen_down: bfloat16 [2, 256, 16, 6144], P('section', None, None, 'expert'), may hold values from -0.0048828125 to 0.0048828125
- gen_up: bfloat16 [2, 256, 16, 6144], P('section', None, None, 'expert'), may hold values from -0.09375 to 0.09375
Outputs:
- handoff: bfloat16 [2, 64, 128, 6144], P('section', 'groups', 'expert'), parts along dimension 1
There are 2 independent parts, one for each index of `groups`. A program takes and returns all parts, laid end to end along the dimension named above; an argument that names none is the same for every part. Nothing has to cross between parts.
Inputs may be any that keep to these rules, and one draw needn't show every extreme that they name: `block_expert`: within each layer's 32 blocks no expert is named more than 8 times, and one expert exactly 8 times.
All inputs are finite; a program needn't handle non-finite values.
Results may differ from a plain program's by a relative error of at most 0.0065.
Values may be sent and summed in bfloat16 or wider, within the bound.
No kernel may reach another device: no remote copies, remote signals or barrier semaphores. Data moves between devices by JAX's collectives and lax.ppermute only.
A program may use at most 192 MiB of HBM per device.

v0:
```python
import jax
import jax.numpy as jnp
from jax import lax
from jax.sharding import PartitionSpec as P


def passed_along(block, axis, distance):
    devices = range(lax.axis_size(axis))
    route = [((i - distance) % len(devices), i) for i in devices]
    return lax.ppermute(block, axis, route)


def norm_rows(block_rows, gain):
    values = block_rows.astype(jnp.float32)
    scale = lax.rsqrt(jnp.mean(values * values, axis=-1, keepdims=True) + 1e-05)
    return (values * scale * gain.astype(jnp.float32)).astype(jnp.bfloat16)


def apply_adapter(block_rows, gain, down_maps, up_maps):
    values = block_rows.astype(jnp.float32)
    normed = norm_rows(block_rows, gain)
    low = jnp.einsum("bnd,brd->bnr", normed, down_maps, preferred_element_type=jnp.float32).astype(
        jnp.bfloat16
    )
    update = jnp.einsum("bnr,brd->bnd", low, up_maps, preferred_element_type=jnp.float32)
    return (values + update).astype(jnp.bfloat16)


def on_device(
    activations, block_expert, seq_task, norm_gain, task_embed, expert_embed, gen_down, gen_up
):
    tokens_in = activations[0]
    expert_ids = block_expert[0, :, 0]
    n_blocks = expert_ids.shape[0]
    per_seq = n_blocks // seq_task.shape[1]
    task_ids = seq_task[0][jnp.arange(n_blocks, dtype=jnp.int32) // per_seq]
    gain = norm_gain[0]
    code_all = jax.nn.silu(
        task_embed.astype(jnp.float32)[:, None, :] + expert_embed[0].astype(jnp.float32)[None]
    ).astype(jnp.bfloat16)
    code_rows = code_all[task_ids, expert_ids]
    down_part = jnp.einsum(
        "bh,hrd->brd", code_rows, gen_down[0], preferred_element_type=jnp.float32
    ).astype(jnp.bfloat16)
    up_part = jnp.einsum(
        "bh,hrd->brd", code_rows, gen_up[0], preferred_element_type=jnp.float32
    ).astype(jnp.bfloat16)
    down_full, up_full = (
        lax.all_gather(down_part, "expert", axis=2, tiled=True),
        lax.all_gather(up_part, "expert", axis=2, tiled=True),
    )
    result = apply_adapter(tokens_in, gain, down_full, up_full)
    return passed_along(result[None], "section", 1)


def solution(mesh):
    in_specs = (
        P("section", "groups", "expert", None),
        P("section", "groups", None),
        P("section", "groups"),
        P("section", None),
        P(),
        P("section", None, None),
        P("section", None, None, "expert"),
        P("section", None, None, "expert"),
    )
    out_specs = P("section", "groups", "expert", None)
    return jax.shard_map(
        on_device, mesh=mesh, in_specs=in_specs, out_specs=out_specs, check_vma=False
    )
```

profile of v0, /device:TPU:0, one launch (start us, length us, event | category | flops | bytes accessed | tf_op | source)
XLA Modules:
  0.0 313.5 jit_solution(6102342258807756337)
XLA Ops:
  6.5 0.0 copy-start
  6.5 0.0 all-gather.5.cloned.1.call-start
  6.6 0.7 convert_element_type.45
  7.3 0.7 bitcast_convert_fusion
  7.9 0.0 copy-done
  7.9 0.7 gather_fusion
  8.6 0.7 fusion.31
  9.3 0.7 gather_fusion.1
  10.0 6.4 %fusion.8 = bf16[32,16,768]{2,0,1:T(8,128)(2,1)S(1)} fusion(bf16[256,16,768]{2,1,0:T(8,128)(2,1)} %bitcast.41, bf16[32,256]{1,0:T(8,128)(2,1)S(1)} %gather_fusion.1), kind=kOutput, calls=%fused_computation.12 | convolution fusion | flops 201326592 | bytes 7094272 | tf_op jit(solution)/shard_map/bh,hrd->brd/dot_general | solution.py:45
  16.5 0.0 copy-start.1
  16.5 1.3 copy.19
  17.8 0.0 all-gather.5.cloned.1.call-update
  17.8 0.2 all-gather.3.cloned.1.call-start
  18.0 6.4 %fusion.10 = bf16[32,16,768]{2,0,1:T(8,128)(2,1)S(1)} fusion(bf16[256,16,768]{2,1,0:T(8,128)(2,1)} %bitcast.42, bf16[32,256]{1,0:T(8,128)(2,1)S(1)} %gather_fusion.1), kind=kOutput, calls=%fused_computation.14 | convolution fusion | flops 201326592 | bytes 7094272 | tf_op jit(solution)/shard_map/bh,hrd->brd/dot_general | solution.py:42
  24.5 1.4 copy.20
  25.9 0.0 all-gather.3.cloned.1.call-update
  25.9 0.0 copy-done.1
  25.9 4.5 %fusion = f32[32,16]{1,0:T(8,128)S(1)} fusion(bf16[1,32,16,6144]{3,2,1,0:T(8,128)(2,1)} %param.8), kind=kLoop, calls=%fused_computation.5 | loop fusion | flops 9436672 | bytes 6293504 | tf_op jit(solution)/shard_map/reduce_sum | solution.py:15
  30.5 54.9 %all-gather.5.cloned.1.call-done = bf16[32,16,6144]{2,1,0:T(8,128)(2,1)} async-done(((bf16[32,16,768]{2,1,0:T(8,128)(2,1)}), bf16[32,16,6144]{2,1,0:T(8,128)(2,1)}) %all-gather.5.cloned.1.call-update) | async-done | bytes 6291472 | tf_op jit(solution)/shard_map/all_gather | solution.py:50
  85.4 65.0 %all-gather.3.cloned.1.call-done = bf16[32,16,6144]{2,1,0:T(8,128)(2,1)} async-done(((bf16[32,16,768]{2,1,0:T(8,128)(2,1)}), bf16[32,16,6144]{2,1,0:T(8,128)(2,1)}) %all-gather.3.cloned.1.call-update) | async-done | bytes 6291472 | tf_op jit(solution)/shard_map/all_gather | solution.py:49
  150.4 15.6 %fusion.4 = bf16[1,32,16,6144]{3,2,1,0:T(8,128)(2,1)} fusion(bf16[32,16,6144]{2,1,0:T(8,128)(2,1)} %all-gather.5.cloned.1.call-done, bf16[1,32,16,6144]{3,2,1,0:T(8,128)(2,1)} %param.8, bf16[32,16,6144]{2,1,0:T(8,128)(2,1)} %all-gather.3.cloned.1.call-done, f32[6144]{0:T(1024)S(1)} %bitcast.43, f32[32,16]{1,0:T(8,128)S(1)} %add_rsqrt_fusion), kind=kOutput, calls=%fused_computation.9 | convolution fusion | flops 223354880 | bytes 25192448 | tf_op jit(solution)/shard_map/bnr,brd->bnd/dot_general | solution.py:25
  166.1 1.5 collective-permute-start
  167.5 136.4 %collective-permute-done = bf16[1,32,16,6144]{3,2,1,0:T(8,128)(2,1)S(1)} collective-permute-done((bf16[1,32,16,6144]{3,2,1,0:T(8,128)(2,1)}, bf16[1,32,16,6144]{3,2,1,0:T(8,128)(2,1)S(1)}, u32[]{:S(2)}, u32[]{:S(2)}) %collective-permute-start) | collective-permute-done | bytes 6291488 | tf_op jit(solution)/shard_map/ppermute | solution.py:10
  303.9 2.7 copy.22
  (5 shorter events, 0.1 us)
Async XLA Ops:
  6.5 1.4 copy-start
  6.5 78.8 %all-gather.5.cloned.1.call-start = ((), (), s32[]{:S(2)}) async-start(), calls=%async_computation.1 | async-start | bytes 7077888 | tf_op jit(solution)/shard_map/all_gather | solution.py:50
  16.5 9.4 %copy-start.1 = (bf16[1,6144]{1,0:T(2,128)(2,1)S(1)}, bf16[1,6144]{1,0:T(2,128)(2,1)}, u32[]{:S(2)}) copy-start(bf16[1,6144]{1,0:T(2,128)(2,1)} %param.11) | copy-start | bytes 36868
  17.8 132.6 %all-gather.3.cloned.1.call-start = ((), (), s32[]{:S(2)}) async-start(), calls=%async_computation | async-start | bytes 7077888 | tf_op jit(solution)/shard_map/all_gather | solution.py:49
  166.1 137.9 %collective-permute-start = (bf16[1,32,16,6144]{3,2,1,0:T(8,128)(2,1)}, bf16[1,32,16,6144]{3,2,1,0:T(8,128)(2,1)S(1)}, u32[]{:S(2)}, u32[]{:S(2)}) collective-permute-start(bf16[1,32,16,6144]{3,2,1,0:T(8,128)(2,1)} %fusion.4), channel_id=1, source_target_pairs={{1,0},{0,1},{3,2},{2,3},{5,4},{4,5},{7,6},{6,7},{9,8},{8,9},{11,10... | collective-permute-start | bytes 18874376 | tf_op jit(solution)/shard_map/ppermute | solution.py:10
Sparse Core Ops, SparseCore 0:
  17.9 67.4 all-gather.4
  87.0 63.3 all-gather.2
where the time goes:
time: 314 us; the launch traced here: 313 us
  waiting for transfers between devices  256 us (82%)
  matrix products  28.5 us (9%)
  between operations  13.5 us (4%)
  local copies, waits for them, and re-layouts  6.78 us (2%)
  other arithmetic  6.7 us (2%)
    ppermute x1, waiting for transfers between devices, passed_along(): return lax.ppermute(block, axis, route)  136 us
    all_gather x1, waiting for transfers between devices, on_device(): lax.all_gather(down_part, 'expert', axis=2, tiled=True)  65 us
    all_gather x1, waiting for transfers between devices, on_device(): lax.all_gather(up_part, 'expert', axis=2, tiled=True)  54.9 us
    dot_general x1, matrix products, apply_adapter(): jnp.einsum('bnr,brd->bnd', low, up_maps, preferred_element_type=jnp.float32)  15.6 us
    dot_general x1, matrix products, on_device(): jnp.einsum('bh,hrd->brd', code_rows, gen_down[0], preferred_element_type=...  6.44 us
    dot_general x1, matrix products, on_device(): jnp.einsum('bh,hrd->brd', code_rows, gen_up[0], preferred_element_type=jn...  6.44 us
  transfers between devices with their start and end apart: 3, of which 3 were waited for; matrix products, arithmetic and copies ran while one was open for 4% of the time, Pallas kernels for 0%

commit v1 on v0

--- a/solution.py
+++ b/solution.py
@@ -1,13 +1,212 @@
+import functools
+
 import jax
 import jax.numpy as jnp
 from jax import lax
+from jax.experimental import pallas as pl
+from jax.experimental.pallas import tpu as pltpu
 from jax.sharding import PartitionSpec as P
+
+CORES = 2
+VMEM_BYTES = 40 * 1024 * 1024
 
 
 def passed_along(block, axis, distance):
     devices = range(lax.axis_size(axis))
     route = [((i - distance) % len(devices), i) for i in devices]
     return lax.ppermute(block, axis, route)
+
+
+def chip_ring(n_chips):
+    return list(range(0, n_chips, 2)) + list(range(1, n_chips, 2))[::-1]
+
+
+def ring_step(block):
+    order = chip_ring(lax.axis_size("expert") // CORES)
+    route = []
+    for at, chip in enumerate(order):
+        after = order[(at + 1) % len(order)]
+        route += [(chip * CORES + core, after * CORES + core) for core in range(CORES)]
+    return lax.ppermute(block, "expert", route)
+
+
+def core_swap(block):
+    route = [(i, i ^ 1) for i in range(lax.axis_size("expert"))]
+    return lax.ppermute(block, "expert", route)
+
+
+def piece_owners(n_devices):
+    order = chip_ring(n_devices // CORES)
+    owners = []
+    for device in range(n_devices):
+        chip, core = divmod(device, CORES)
+        at = order.index(chip)
+        row = []
+        for step in range(len(order)):
+            source = order[(at - step) % len(order)]
+            row += [source * CORES + core, source * CORES + 1 - core]
+        owners.append(row)
+    return jnp.asarray(owners, jnp.int32)
+
+
+def tied(value, *after):
+    return lax.optimization_barrier((value, *after))[0]
+
+
+def ring_gather(block):
+    pieces, held = [], block
+    for step in range(lax.axis_size("expert") // CORES):
+        if step:
+            held = ring_step(held)
+        pieces += [held, core_swap(held)]
+    return pieces
+
+
+def columns(owners_ref, piece, width):
+    return pl.ds(pl.multiple_of(owners_ref[piece] * width, 128), width)
+
+
+def normed_into(normed_ref, rows_ref, gain_ref):
+    values = rows_ref[0].astype(jnp.float32)
+    scale = lax.rsqrt(jnp.mean(values * values, axis=-1, keepdims=True) + 1e-05)
+    normed_ref[...] = (values * scale * gain_ref[...].astype(jnp.float32)).astype(jnp.bfloat16)
+
+
+def low_of(owners_ref, normed_ref, maps, width):
+    total = None
+    for piece, down in enumerate(maps):
+        part = lax.dot_general(
+            normed_ref[:, columns(owners_ref, piece, width)],
+            down,
+            (((1,), (1,)), ((), ())),
+            preferred_element_type=jnp.float32,
+        )
+        total = part if total is None else total + part
+    return total.astype(jnp.bfloat16)
+
+
+def add_update(owners_ref, out_ref, rows_ref, low, maps, width):
+    for piece, up in enumerate(maps):
+        at = columns(owners_ref, piece, width)
+        update = jnp.dot(low, up, preferred_element_type=jnp.float32)
+        out_ref[0, :, at] = (rows_ref[0, :, at].astype(jnp.float32) + update).astype(jnp.bfloat16)
+
+
+def layer_kernel(n, width, owners_ref, rows_ref, gain_ref, *refs):
+    pieces, out_ref, normed_ref = refs[:n], refs[n], refs[n + 1]
+    normed_into(normed_ref, rows_ref, gain_ref)
+    low = low_of(owners_ref, normed_ref, [p[0, 0] for p in pieces], width)
+    add_update(owners_ref, out_ref, rows_ref, low, [p[1, 0] for p in pieces], width)
+
+
+def low_kernel(n, width, owners_ref, rows_ref, gain_ref, *refs):
+    pieces, out_ref, normed_ref = refs[:n], refs[n], refs[n + 1]
+    normed_into(normed_ref, rows_ref, gain_ref)
+    out_ref[0] = low_of(owners_ref, normed_ref, [p[0] for p in pieces], width)
+
+
+def update_kernel(n, width, owners_ref, rows_ref, low_ref, *refs):
+    pieces, out_ref = refs[:n], refs[-1]
+    add_update(owners_ref, out_ref, rows_ref, low_ref[0], [p[0] for p in pieces], width)
+
+
+def place_kernel(block_ref, held_ref, out_ref):
+    out_ref[...] = block_ref[...]
+
+
+def params():
+    return pltpu.CompilerParams(vmem_limit_bytes=VMEM_BYTES)
+
+
+def cost(count, rows, dim, rank, passes):
+    return pl.CostEstimate(
+        flops=4 * count * rows * dim * rank,
+        bytes_accessed=2 * count * dim * (passes * rows + 2 * rank),
+        transcendentals=0,
+    )
+
+
+def layer_blocks(owners, rows, first, gain, pieces):
+    n, (_, count, rank, width) = len(pieces), pieces[0].shape
+    held, dim = rows.shape[1:]
+    return pl.pallas_call(
+        functools.partial(layer_kernel, n, width),
+        out_shape=jax.ShapeDtypeStruct((count, held, dim), jnp.bfloat16),
+        grid_spec=pltpu.PrefetchScalarGridSpec(
+            num_scalar_prefetch=1,
+            grid=(count,),
+            in_specs=[
+                pl.BlockSpec((1, held, dim), lambda b, s: (b + first, 0, 0)),
+                pl.BlockSpec((1, dim), lambda b, s: (0, 0)),
+            ]
+            + [pl.BlockSpec((2, 1, rank, width), lambda b, s: (0, b, 0, 0))] * n,
+            out_specs=pl.BlockSpec((1, held, dim), lambda b, s: (b, 0, 0)),
+            scratch_shapes=[pltpu.VMEM((held, dim), jnp.bfloat16)],
+        ),
+        compiler_params=params(),
+        cost_estimate=cost(count, held, dim, rank, 2),
+    )(owners, rows, gain, *pieces)
+
+
+def low_blocks(owners, rows, gain, pieces):
+    n, (count, rank, width) = len(pieces), pieces[0].shape
+    held, dim = rows.shape[1:]
+    return pl.pallas_call(
+        functools.partial(low_kernel, n, width),
+        out_shape=jax.ShapeDtypeStruct((count, held, rank), jnp.bfloat16),
+        grid_spec=pltpu.PrefetchScalarGridSpec(
+            num_scalar_prefetch=1,
+            grid=(count,),
+            in_specs=[
+                pl.BlockSpec((1, held, dim), lambda b, s: (b, 0, 0)),
+                pl.BlockSpec((1, dim), lambda b, s: (0, 0)),
+            ]
+            + [pl.BlockSpec((1, rank, width), lambda b, s: (b, 0, 0))] * n,
+            out_specs=pl.BlockSpec((1, held, rank), lambda b, s: (b, 0, 0)),
+            scratch_shapes=[pltpu.VMEM((held, dim), jnp.bfloat16)],
+        ),
+        compiler_params=params(),
+        cost_estimate=cost(count, held, dim, rank, 1),
+    )(owners, rows, gain, *pieces)
+
+
+def update_blocks(owners, rows, low, pieces, result):
+    n, (count, rank, width) = len(pieces), pieces[0].shape
+    held, dim = rows.shape[1:]
+    return pl.pallas_call(
+        functools.partial(update_kernel, n, width),
+        out_shape=jax.ShapeDtypeStruct(result.shape, result.dtype),
+        grid_spec=pltpu.PrefetchScalarGridSpec(
+            num_scalar_prefetch=1,
+            grid=(count,),
+            in_specs=[
+                pl.BlockSpec((1, held, dim), lambda b, s: (b, 0, 0)),
+                pl.BlockSpec((1, held, rank), lambda b, s: (b, 0, 0)),
+            ]
+            + [pl.BlockSpec((1, rank, width), lambda b, s: (b, 0, 0))] * n
+            + [pl.BlockSpec(memory_space=pl.ANY)],
+            out_specs=pl.BlockSpec((1, held, dim), lambda b, s: (b, 0, 0)),
+        ),
+        input_output_aliases={3 + n: 0},
+        compiler_params=params(),
+        cost_estimate=cost(count, held, dim, rank, 2),
+    )(owners, rows, low, *pieces, result)
+
+
+def place_blocks(block, first, result, total):
+    count, held, dim = block.shape
+    spec = pl.BlockSpec((1, held, dim), lambda b: (b, 0, 0))
+    kernel = place_kernel if result is not None else (lambda b, o: place_kernel(b, None, o))
+    return pl.pallas_call(
+        kernel,
+        out_shape=jax.ShapeDtypeStruct((total, held, dim), jnp.bfloat16),
+        grid=(count,),
+        in_specs=[spec] + ([pl.BlockSpec(memory_space=pl.ANY)] if result is not None else []),
+        out_specs=pl.BlockSpec((1, held, dim), lambda b: (b + first, 0, 0)),
+        input_output_aliases={1: 0} if result is not None else {},
+        compiler_params=params(),
+        cost_estimate=cost(count, held, dim, 0, 2),
+    )(block, *([] if result is None else [result]))
 
 
 def norm_rows(block_rows, gain):
@@ -26,15 +225,30 @@
     return (values + update).astype(jnp.bfloat16)
 
 
+def cuts(n_blocks):
+    raw = n_blocks * 3 // 8
+    sizes = [n_blocks // 8]
+    while raw + sum(sizes) < n_blocks:
+        left = n_blocks - raw - sum(sizes)
+        sizes.append(left if left <= n_blocks // 5 else -(-left // -(-left // (n_blocks // 5))))
+    starts = [raw + sum(sizes[:i]) for i in range(len(sizes))]
+    return raw, [(a, a + s) for a, s in zip(starts, sizes)]
+
+
 def on_device(
     activations, block_expert, seq_task, norm_gain, task_embed, expert_embed, gen_down, gen_up
 ):
-    tokens_in = activations[0]
+    rows = activations[0]
+    n_blocks = rows.shape[0]
+    raw, chunks = cuts(n_blocks)
+    tiled = rows.shape[1] % 16 == 0 and gen_down.shape[3] % 128 == 0 and raw > 0
+
+    if tiled:
+        raw_rows = passed_along(rows[:raw], "section", 1)
+
     expert_ids = block_expert[0, :, 0]
-    n_blocks = expert_ids.shape[0]
     per_seq = n_blocks // seq_task.shape[1]
     task_ids = seq_task[0][jnp.arange(n_blocks, dtype=jnp.int32) // per_seq]
-    gain = norm_gain[0]
     code_all = jax.nn.silu(
         task_embed.astype(jnp.float32)[:, None, :] + expert_embed[0].astype(jnp.float32)[None]
     ).astype(jnp.bfloat16)
@@ -45,12 +259,37 @@
     up_part = jnp.einsum(
         "bh,hrd->brd", code_rows, gen_up[0], preferred_element_type=jnp.float32
     ).astype(jnp.bfloat16)
-    down_full, up_full = (
-        lax.all_gather(down_part, "expert", axis=2, tiled=True),
-        lax.all_gather(up_part, "expert", axis=2, tiled=True),
-    )
-    result = apply_adapter(tokens_in, gain, down_full, up_full)
-    return passed_along(result[None], "section", 1)
+
+    if not tiled:
+        down_full, up_full = (
+            lax.all_gather(down_part, "expert", axis=2, tiled=True),
+            lax.all_gather(up_part, "expert", axis=2, tiled=True),
+        )
+        result = apply_adapter(rows, norm_gain[0], down_full, up_full)
+        return passed_along(result[None], "section", 1)
+
+    owners = piece_owners(lax.axis_size("expert"))[lax.axis_index("expert")]
+    raw_up = passed_along(tied(up_part[:raw], down_part), "section", 1)
+    raw_down = ring_gather(down_part[:raw])
+    raw_low = passed_along(low_blocks(owners, rows, norm_gain, raw_down), "section", 1)
+
+    gathered = [raw_down]
+    arrived = []
+    for first, last in chunks:
+        mine = jnp.stack([down_part[first:last], up_part[first:last]])
+        if len(gathered) > 1:
+            mine = tied(mine, gathered[-2][-2])
+        gathered.append(ring_gather(mine))
+        done = layer_blocks(owners, rows, first, norm_gain, gathered[-1])
+        arrived.append(passed_along(done, "section", 1))
+    raw_ups = ring_gather(tied(raw_up, gathered[-2][-2]))
+
+    result = None
+    for (first, last), block in zip(chunks[:-1], arrived[:-1]):
+        result = place_blocks(block, first, result, n_blocks)
+    result = update_blocks(owners, raw_rows, raw_low, raw_ups, result)
+    result = place_blocks(arrived[-1], chunks[-1][0], result, n_blocks)
+    return result[None]
 
 
 def solution(mesh):

time: 314 us -> 246 us (0.78)
  waiting for transfers between devices: 256 us -> 129 us
  starting transfers between devices: 1.7 us -> 51.4 us
  Pallas kernels: 0 us -> 36.3 us
  matrix products: 28.5 us -> 10.3 us
  between operations: 13.5 us -> 0.34 us
  local copies, waits for them, and re-layouts: 6.78 us -> 15.9 us
  other arithmetic: 6.7 us -> 2.19 us
    all_gather x2 -> x0, waiting for transfers between devices: 120 us -> none  [the longest x1 65 us: on_device(): lax.all_gather(down_part, 'expert', axis=2, tiled=True)]
    ppermute x1 -> x7, waiting for transfers between devices: 136 us -> 79.2 us  [passed_along(): return lax.ppermute(block, axis, route)]
    ppermute x0 -> x42, waiting for transfers between devices: none -> 50.2 us  [the longest x18 50.2 us: ring_step(): return lax.ppermute(block, 'expert', route)]
    ppermute x0 -> x42, starting transfers between devices: none -> 43.5 us  [the longest x18 39.2 us: ring_step(): return lax.ppermute(block, 'expert', route)]
    pallas_call x0 -> x10, Pallas kernels: none -> 36.3 us  [the longest x4 17.6 us: layer_blocks(): pl.pallas_call(functools.partial(layer_kernel, n, width), out_shape=jax.S...]
    dot_general x1 -> x0, matrix products: 15.6 us -> none  [apply_adapter(): jnp.einsum('bnr,brd->bnd', low, up_maps, preferred_element_type=jnp.float32)]
    unnamed x5 -> x42, local copies, waits for them, and re-layouts: 2.71 us -> 12 us
    ppermute x1 -> x7, starting transfers between devices: 1.48 us -> 7.91 us  [passed_along(): return lax.ppermute(block, axis, route)]
  transfers between devices with their start and end apart: 3 -> 49, of which waited for: 3 -> 16; matrix products, arithmetic and copies ran while one was open for 4% -> 2% of each run, Pallas kernels for 0% -> 14%
where the time goes in v1:
time: 246 us
  waiting for transfers between devices  129 us (52%)
  starting transfers between devices  51.4 us (21%)
  Pallas kernels  36.3 us (15%)
  local copies, waits for them, and re-layouts  15.9 us (6%)
  matrix products  10.3 us (4%)
    ppermute x7, waiting for transfers between devices, passed_along(): return lax.ppermute(block, axis, route)  79.2 us
    ppermute x18, waiting for transfers between devices, ring_step(): return lax.ppermute(block, 'expert', route)  50.2 us
    ppermute x18, starting transfers between devices, ring_step(): return lax.ppermute(block, 'expert', route)  39.2 us
    pallas_call x4, Pallas kernels, layer_blocks(): pl.pallas_call(functools.partial(layer_kernel, n, width), out_shape=jax.S...  17.6 us
    unnamed x42, local copies, waits for them, and re-layouts  12 us
    ppermute x7, starting transfers between devices, passed_along(): return lax.ppermute(block, axis, route)  7.91 us
    pallas_call x4, Pallas kernels, place_blocks(): pl.pallas_call(kernel, out_shape=jax.ShapeDtypeStruct((total, held, dim),...  7.71 us
    dot_general x1, matrix products, on_device(): jnp.einsum('bh,hrd->brd', code_rows, gen_down[0], preferred_element_type=...  6.59 us
  transfers between devices with their start and end apart: 49, of which 16 were waited for; matrix products, arithmetic and copies ran while one was open for 2% of the time, Pallas kernels for 14%

profile of v1, /device:TPU:0, one launch (start us, length us, event | category | flops | bytes accessed | tf_op | source)
XLA Modules:
  0.0 245.8 jit_solution(9134303706137377851)
XLA Ops:
  0.0 0.7 bitcast_convert_fusion
  0.7 0.7 convert_element_type.14
  1.4 0.7 gather_fusion
  2.1 0.7 fusion.16
  2.8 0.7 gather_fusion.1
  3.5 6.6 %fusion.2 = bf16[32,16,768]{2,0,1:T(8,128)(2,1)S(1)} fusion(bf16[256,16,768]{2,1,0:T(8,128)(2,1)} %bitcast.51, bf16[32,256]{1,0:T(8,128)(2,1)S(1)} %gather_fusion.1), kind=kOutput, calls=%fused_computation.4 | convolution fusion | flops 201326592 | bytes 7094272 | tf_op jit(solution)/shard_map/bh,hrd->brd/dot_general | solution.py:256
  10.6 4.1 %collective-permute-start = (bf16[12,16,768]{2,1,0:T(8,128)(2,1)S(1)}, bf16[12,16,768]{2,1,0:T(8,128)(2,1)S(1)}, u32[]{:S(2)}, u32[]{:S(2)}) collective-permute-start(bf16[12,16,768]{2,1,0:T(8,128)(2,1)S(1)} %slice.56.refs_0_), channel_id=1, source_target_pairs={{0,8},{2,10},{8,12},{10,14},{12,4},{14,6},{4,0},{6,2},{1,9},{3,11}... | collective-permute-start | bytes 884744 | tf_op jit(solution)/shard_map/ppermute | solution.py:30
  14.7 3.7 %fusion = bf16[32,16,768]{2,0,1:T(8,128)(2,1)S(1)} fusion(bf16[256,16,768]{2,1,0:T(8,128)(2,1)S(1)} %bitcast.52, bf16[32,256]{1,0:T(8,128)(2,1)S(1)} %gather_fusion.1), kind=kOutput, calls=%fused_computation.2 | convolution fusion | flops 201326592 | bytes 7094272 | tf_op jit(solution)/shard_map/bh,hrd->brd/dot_general | solution.py:259
  18.8 1.6 collective-permute-start.21
  21.0 1.6 collective-permute-start.20
  22.5 2.5 %collective-permute-start.1 = (bf16[12,16,768]{2,1,0:T(8,128)(2,1)S(1)}, bf16[12,16,768]{2,1,0:T(8,128)(2,1)S(1)}, u32[]{:S(2)}, u32[]{:S(2)}) collective-permute-start(bf16[12,16,768]{2,1,0:T(8,128)(2,1)S(1)} %collective-permute-done.refs_2_), channel_id=1, source_target_pairs={{0,8},{2,10},{8,12},{10,14},{12,4},{14,6},{4,0},{6,2},{1,9},{3,11}... | collective-permute-start | bytes 884744 | tf_op jit(solution)/shard_map/ppermute | solution.py:30
  25.8 3.4 %collective-permute-start.22 = (bf16[2,4,16,768]{3,2,1,0:T(8,128)(2,1)S(1)}, bf16[2,4,16,768]{3,2,1,0:T(8,128)(2,1)S(1)}, u32[]{:S(2)}, u32[]{:S(2)}) collective-permute-start(bf16[2,4,16,768]{3,2,1,0:T(8,128)(2,1)S(1)} %collective-permute-done.21.refs_2_), channel_id=1, source_target_pairs={{0,8},{2,10},{8,12},{10,14},{12,4},{14,6},{4,0},{6,2},{1,9},{3,11}... | collective-permute-start | bytes 589832 | tf_op jit(solution)/shard_map/ppermute | solution.py:30
  29.2 3.2 %collective-permute-done.1.refs_4_ = bf16[12,16,768]{2,1,0:T(8,128)(2,1)S(1)} collective-permute-done((bf16[12,16,768]{2,1,0:T(8,128)(2,1)S(1)}, bf16[12,16,768]{2,1,0:T(8,128)(2,1)S(1)}, u32[]{:S(2)}, u32[]{:S(2)}) %collective-permute-start.1) | collective-permute-done | bytes 294944 | tf_op jit(solution)/shard_map/ppermute | solution.py:30
  32.5 3.4 %collective-permute-start.2 = (bf16[12,16,768]{2,1,0:T(8,128)(2,1)S(1)}, bf16[12,16,768]{2,1,0:T(8,128)(2,1)S(1)}, u32[]{:S(2)}, u32[]{:S(2)}) collective-permute-start(bf16[12,16,768]{2,1,0:T(8,128)(2,1)S(1)} %collective-permute-done.1.refs_4_), channel_id=1, source_target_pairs={{0,8},{2,10},{8,12},{10,14},{12,4},{14,6},{4,0},{6,2},{1,9},{3,11}... | collective-permute-start | bytes 884744 | tf_op jit(solution)/shard_map/ppermute | solution.py:30
  35.9 0.8 collective-permute-done.22.refs_4_
  36.7 3.4 %collective-permute-start.23 = (bf16[2,4,16,768]{3,2,1,0:T(8,128)(2,1)S(1)}, bf16[2,4,16,768]{3,2,1,0:T(8,128)(2,1)S(1)}, u32[]{:S(2)}, u32[]{:S(2)}) collective-permute-start(bf16[2,4,16,768]{3,2,1,0:T(8,128)(2,1)S(1)} %collective-permute-done.22.refs_4_), channel_id=1, source_target_pairs={{0,8},{2,10},{8,12},{10,14},{12,4},{14,6},{4,0},{6,2},{1,9},{3,11}... | collective-permute-start | bytes 589832 | tf_op jit(solution)/shard_map/ppermute | solution.py:30
  40.1 3.2 %collective-permute-done.2.refs_6_ = bf16[12,16,768]{2,1,0:T(8,128)(2,1)S(1)} collective-permute-done((bf16[12,16,768]{2,1,0:T(8,128)(2,1)S(1)}, bf16[12,16,768]{2,1,0:T(8,128)(2,1)S(1)}, u32[]{:S(2)}, u32[]{:S(2)}) %collective-permute-start.2) | collective-permute-done | bytes 294944 | tf_op jit(solution)/shard_map/ppermute | solution.py:30
  44.6 1.7 collective-permute-done.23.refs_6_
  46.3 3.3 %collective-permute-start.3 = (bf16[2,6,16,768]{3,2,1,0:T(8,128)(2,1)S(1)}, bf16[2,6,16,768]{3,2,1,0:T(8,128)(2,1)S(1)}, u32[]{:S(2)}, u32[]{:S(2)}) collective-permute-start(bf16[2,6,16,768]{3,2,1,0:T(8,128)(2,1)S(1)} %pad_maximum_fusion.refs_0_), channel_id=1, source_target_pairs={{0,8},{2,10},{8,12},{10,14},{12,4},{14,6},{4,0},{6,2},{1,9},{3,11}... | collective-permute-start | bytes 884744 | tf_op jit(solution)/shard_map/ppermute | solution.py:30
  49.7 0.7 collective-permute-start.24
  50.4 0.7 copy-done.13
  51.3 0.7 copy-done.15
  52.3 4.7 %collective-permute-done.3.refs_2_ = bf16[2,6,16,768]{3,2,1,0:T(8,128)(2,1)S(1)} collective-permute-done((bf16[2,6,16,768]{3,2,1,0:T(8,128)(2,1)S(1)}, bf16[2,6,16,768]{3,2,1,0:T(8,128)(2,1)S(1)}, u32[]{:S(2)}, u32[]{:S(2)}) %collective-permute-start.3) | collective-permute-done | bytes 294944 | tf_op jit(solution)/shard_map/ppermute | solution.py:30
  57.0 3.4 %collective-permute-start.4 = (bf16[2,6,16,768]{3,2,1,0:T(8,128)(2,1)S(1)}, bf16[2,6,16,768]{3,2,1,0:T(8,128)(2,1)S(1)}, u32[]{:S(2)}, u32[]{:S(2)}) collective-permute-start(bf16[2,6,16,768]{3,2,1,0:T(8,128)(2,1)S(1)} %collective-permute-done.3.refs_2_), channel_id=1, source_target_pairs={{0,8},{2,10},{8,12},{10,14},{12,4},{14,6},{4,0},{6,2},{1,9},{3,11}... | collective-permute-start | bytes 884744 | tf_op jit(solution)/shard_map/ppermute | solution.py:30
  60.4 1.9 collective-permute-done.24.refs_2_
  62.3 3.5 %collective-permute-start.25 = (bf16[2,5,16,768]{3,2,1,0:T(8,128)(2,1)}, bf16[2,5,16,768]{3,2,1,0:T(8,128)(2,1)}, u32[]{:S(2)}, u32[]{:S(2)}) collective-permute-start(bf16[2,5,16,768]{3,2,1,0:T(8,128)(2,1)} %collective-permute-done.24.refs_2_), channel_id=1, source_target_pairs={{0,8},{2,10},{8,12},{10,14},{12,4},{14,6},{4,0},{6,2},{1,9},{3,11}... | collective-permute-start | bytes 737288 | tf_op jit(solution)/shard_map/ppermute | solution.py:30
  65.8 0.7 copy-done.17
  66.5 0.7 dynamic-slice_bitcast_fusion.owners_ref
  67.2 2.8 %copy-done.1 = bf16[1,32,16,6144]{3,2,1,0:T(8,128)(2,1)S(1)} copy-done((bf16[1,32,16,6144]{3,2,1,0:T(8,128)(2,1)S(1)}, bf16[1,32,16,6144]{3,2,1,0:T(8,128)(2,1)}, u32[]{:S(2)}) %copy-start.1) | copy-done | bytes 6291480
  70.0 0.9 copy-done.6
  70.9 0.9 copy-done.8
  71.8 0.9 copy-done.10
  72.7 0.9 copy-done.12
  73.7 0.9 copy-done.14
  74.6 0.9 copy-done.16
  75.5 0.9 copy-done.18
  76.5 3.4 %shard_map.95 = bf16[4,16,6144]{2,1,0:T(8,128)(2,1)S(1)} custom-call(s32[8]{0:T(128)S(1)} %dynamic-slice_bitcast_fusion.owners_ref, bf16[32,16,6144]{2,1,0:T(8,128)(2,1)S(1)} %bitcast.46, bf16[1,6144]{1,0:T(2,128)(2,1)S(1)} %copy-done.2, bf16[2,4,16,768]{3,2,1,0:T(8,128)(2,1)S(1)} %pad_maximum_fusion.3.refs_0_, bf16[2,4,16,768]{3,2,1,0:T(8,128)(2,1)S(1)} %copy-done.8, ...), custom_call_target="tpu_custom_call" | custom-call | flops 25165824 | bytes 3145728 | tf_op jit(solution)/shard_map/pallas_call | solution.py:132
  79.9 1.6 collective-permute-start.48
  82.0 1.9 collective-permute-start.5
  84.7 5.0 %shard_map.92 = bf16[12,16,16]{2,1,0:T(8,128)(2,1)S(1)} custom-call(s32[8]{0:T(128)S(1)} %dynamic-slice_bitcast_fusion.owners_ref, bf16[32,16,6144]{2,1,0:T(8,128)(2,1)S(1)} %bitcast.47, bf16[1,6144]{1,0:T(2,128)(2,1)S(1)} %copy-done.2, bf16[12,16,768]{2,1,0:T(8,128)(2,1)S(1)} %slice.56.refs_0_, bf16[12,16,768]{2,1,0:T(8,128)(2,1)S(1)} %collective-permute-done.15.refs_1_, ...), custom_call_target="tpu_custom_call" | custom-call | flops 75497472 | bytes 7077888 | tf_op jit(solution)/shard_map/pallas_call | solution.py:154
  89.8 6.8 %collective-permute-done.5.refs_6_ = bf16[2,6,16,768]{3,2,1,0:T(8,128)(2,1)S(1)} collective-permute-done((bf16[2,6,16,768]{3,2,1,0:T(8,128)(2,1)S(1)}, bf16[2,6,16,768]{3,2,1,0:T(8,128)(2,1)S(1)}, u32[]{:S(2)}, u32[]{:S(2)}) %collective-permute-start.5) | collective-permute-done | bytes 294944 | tf_op jit(solution)/shard_map/ppermute | solution.py:30
  97.2 54.4 %collective-permute-done.19.low_ref = bf16[12,16,16]{2,1,0:T(8,128)(2,1)S(1)} collective-permute-done((bf16[12,16,16]{2,1,0:T(8,128)(2,1)S(1)}, bf16[12,16,16]{2,1,0:T(8,128)(2,1)S(1)}, u32[]{:S(2)}, u32[]{:S(2)}) %collective-permute-start.19) | collective-permute-done | bytes 6176 | tf_op jit(solution)/shard_map/ppermute | solution.py:17
  152.1 7.0 %collective-permute-done.7.refs_2_ = bf16[2,5,16,768]{3,2,1,0:T(8,128)(2,1)S(1)} collective-permute-done((bf16[2,5,16,768]{3,2,1,0:T(8,128)(2,1)S(1)}, bf16[2,5,16,768]{3,2,1,0:T(8,128)(2,1)S(1)}, u32[]{:S(2)}, u32[]{:S(2)}) %collective-permute-start.7) | collective-permute-done | bytes 245792 | tf_op jit(solution)/shard_map/ppermute | solution.py:30
  159.1 1.2 collective-permute-start.9
  160.9 4.9 %collective-permute-done.9.refs_4_ = bf16[2,5,16,768]{3,2,1,0:T(8,128)(2,1)S(1)} collective-permute-done((bf16[2,5,16,768]{3,2,1,0:T(8,128)(2,1)S(1)}, bf16[2,5,16,768]{3,2,1,0:T(8,128)(2,1)S(1)}, u32[]{:S(2)}, u32[]{:S(2)}) %collective-permute-start.9) | collective-permute-done | bytes 245792 | tf_op jit(solution)/shard_map/ppermute | solution.py:30
  165.8 2.4 collective-permute-start.11
  168.7 4.8 %shard_map.94 = bf16[6,16,6144]{2,1,0:T(8,128)(2,1)S(1)} custom-call(s32[8]{0:T(128)S(1)} %dynamic-slice_bitcast_fusion.owners_ref, bf16[32,16,6144]{2,1,0:T(8,128)(2,1)S(1)} %bitcast.48, bf16[1,6144]{1,0:T(2,128)(2,1)S(1)} %copy-done.2, bf16[2,6,16,768]{3,2,1,0:T(8,128)(2,1)S(1)} %pad_maximum_fusion.refs_0_, ...), custom_call_target="tpu_custom_call" | custom-call | flops 37748736 | bytes 4718592 | tf_op jit(solution)/shard_map/pallas_call | solution.py:132
  173.6 1.6 collective-permute-start.43
  175.1 5.2 %shard_map.93 = bf16[5,16,6144]{2,1,0:T(8,128)(2,1)S(1)} custom-call(s32[8]{0:T(128)S(1)} %dynamic-slice_bitcast_fusion.owners_ref, bf16[32,16,6144]{2,1,0:T(8,128)(2,1)S(1)} %bitcast.49, bf16[1,6144]{1,0:T(2,128)(2,1)S(1)} %copy-done.2, bf16[2,5,16,768]{3,2,1,0:T(8,128)(2,1)S(1)} %pad_maximum_fusion.2.refs_0_, ...), custom_call_target="tpu_custom_call" | custom-call | flops 31457280 | bytes 3932160 | tf_op jit(solution)/shard_map/pallas_call | solution.py:132
  181.0 1.1 collective-permute-start.28
  182.1 4.1 %shard_map.91 = bf16[5,16,6144]{2,1,0:T(8,128)(2,1)S(1)} custom-call(s32[8]{0:T(128)S(1)} %dynamic-slice_bitcast_fusion.owners_ref, bf16[32,16,6144]{2,1,0:T(8,128)(2,1)S(1)} %bitcast.50, bf16[1,6144]{1,0:T(2,128)(2,1)S(1)} %copy-done.2, bf16[2,5,16,768]{3,2,1,0:T(8,128)(2,1)S(1)} %pad_maximum_fusion.1.refs_0_, ...), custom_call_target="tpu_custom_call" | custom-call | flops 31457280 | bytes 3932160 | tf_op jit(solution)/shard_map/pallas_call | solution.py:132
  186.2 3.9 %collective-permute-done.28.refs_2_ = bf16[12,16,768]{2,1,0:T(8,128)(2,1)S(1)} collective-permute-done((bf16[12,16,768]{2,1,0:T(8,128)(2,1)S(1)}, bf16[12,16,768]{2,1,0:T(8,128)(2,1)S(1)}, u32[]{:S(2)}, u32[]{:S(2)}) %collective-permute-start.28) | collective-permute-done | bytes 294944 | tf_op jit(solution)/shard_map/ppermute | solution.py:30
  190.1 1.5 collective-permute-start.13
  191.6 1.2 collective-permute-start.30
  192.8 6.9 %collective-permute-done.30.refs_4_ = bf16[12,16,768]{2,1,0:T(8,128)(2,1)S(1)} collective-permute-done((bf16[12,16,768]{2,1,0:T(8,128)(2,1)S(1)}, bf16[12,16,768]{2,1,0:T(8,128)(2,1)S(1)}, u32[]{:S(2)}, u32[]{:S(2)}) %collective-permute-start.30) | collective-permute-done | bytes 294944 | tf_op jit(solution)/shard_map/ppermute | solution.py:30
  199.7 2.2 collective-permute-start.32
  201.9 4.9 %collective-permute-done.32.refs_6_ = bf16[12,16,768]{2,1,0:T(8,128)(2,1)S(1)} collective-permute-done((bf16[12,16,768]{2,1,0:T(8,128)(2,1)S(1)}, bf16[12,16,768]{2,1,0:T(8,128)(2,1)S(1)}, u32[]{:S(2)}, u32[]{:S(2)}) %collective-permute-start.32) | collective-permute-done | bytes 294944 | tf_op jit(solution)/shard_map/ppermute | solution.py:30
  206.8 16.7 %collective-permute-done.38.block_ref = bf16[5,16,6144]{2,1,0:T(8,128)(2,1)S(1)} collective-permute-done((bf16[5,16,6144]{2,1,0:T(8,128)(2,1)S(1)}, bf16[5,16,6144]{2,1,0:T(8,128)(2,1)S(1)}, u32[]{:S(2)}, u32[]{:S(2)}) %collective-permute-start.38) | collective-permute-done | bytes 983072 | tf_op jit(solution)/shard_map/ppermute | solution.py:17
  224.0 1.4 shard_map.96.held_ref
  225.5 2.1 shard_map.97.held_ref
  227.6 2.1 shard_map.98.refs_8_
  229.7 5.9 %shard_map.99.held_ref = bf16[32,16,6144]{2,1,0:T(8,128)(2,1)} custom-call(s32[8]{0:T(128)S(1)} %dynamic-slice_bitcast_fusion.owners_ref, bf16[12,16,6144]{2,1,0:T(8,128)(2,1)S(1)} %collective-permute-done.14.rows_ref, bf16[12,16,16]{2,1,0:T(8,128)(2,1)S(1)} %collective-permute-done.19.low_ref, ...), custom_call_target="tpu_custom_call", output_to_operand_aliasing={{}: (11, {})} | custom-call | flops 75497472 | bytes 9437184 | tf_op jit(solution)/shard_map/pallas_call | solution.py:176
  235.6 8.1 %collective-permute-done.13.block_ref = bf16[5,16,6144]{2,1,0:T(8,128)(2,1)S(1)} collective-permute-done((bf16[5,16,6144]{2,1,0:T(8,128)(2,1)S(1)}, bf16[5,16,6144]{2,1,0:T(8,128)(2,1)S(1)}, u32[]{:S(2)}, u32[]{:S(2)}) %collective-permute-start.13) | collective-permute-done | bytes 983072 | tf_op jit(solution)/shard_map/ppermute | solution.py:17
  243.7 2.1 shard_map.100
  (112 shorter events, 9.0 us)
Async XLA Ops:
  0.0 1.4 copy-start
  3.5 11.2 %copy-start.19 = (bf16[1,256,16,768]{3,2,1,0:T(8,128)(2,1)S(1)}, bf16[1,256,16,768]{3,2,1,0:T(8,128)(2,1)}, u32[]{:S(2)}) copy-start(bf16[1,256,16,768]{3,2,1,0:T(8,128)(2,1)} %param.16) | copy-start | bytes 18874372
  10.6 12.0 %collective-permute-start = (bf16[12,16,768]{2,1,0:T(8,128)(2,1)S(1)}, bf16[12,16,768]{2,1,0:T(8,128)(2,1)S(1)}, u32[]{:S(2)}, u32[]{:S(2)}) collective-permute-start(bf16[12,16,768]{2,1,0:T(8,128)(2,1)S(1)} %slice.56.refs_0_), channel_id=1, source_target_pairs={{0,8},{2,10},{8,12},{10,14},{12,4},{14,6},{4,0},{6,2},{1,9},{3,11}... | collective-permute-start | bytes 884744 | tf_op jit(solution)/shard_map/ppermute | solution.py:30
  14.7 52.5 %copy-start.2 = (bf16[1,6144]{1,0:T(2,128)(2,1)S(1)}, bf16[1,6144]{1,0:T(2,128)(2,1)}, u32[]{:S(2)}) copy-start(bf16[1,6144]{1,0:T(2,128)(2,1)} %gain_ref.9) | copy-start | bytes 36868
  18.8 7.0 %collective-permute-start.21 = (bf16[2,4,16,768]{3,2,1,0:T(8,128)(2,1)S(1)}, bf16[2,4,16,768]{3,2,1,0:T(8,128)(2,1)S(1)}, u32[]{:S(2)}, u32[]{:S(2)}) collective-permute-start(bf16[2,4,16,768]{3,2,1,0:T(8,128)(2,1)S(1)} %pad_maximum_fusion.3.refs_0_), channel_id=1, source_target_pairs={{0,8},{2,10},{8,12},{10,14},{12,4},{14,6},{4,0},{6,2},{1,9},{3,11}... | collective-permute-start | bytes 589832 | tf_op jit(solution)/shard_map/ppermute | solution.py:30
  20.4 22.9 %collective-permute-start.44 = (bf16[2,4,16,768]{3,2,1,0:T(8,128)(2,1)S(1)}, bf16[2,4,16,768]{3,2,1,0:T(8,128)(2,1)S(1)}, u32[]{:S(2)}, u32[]{:S(2)}) collective-permute-start(bf16[2,4,16,768]{3,2,1,0:T(8,128)(2,1)S(1)} %pad_maximum_fusion.3.refs_0_), channel_id=1, source_target_pairs={{0,2},{2,0},{4,6},{6,4},{8,10},{10,8},{12,14},{14,12},{1,3},{3,1},... | collective-permute-start | bytes 589832 | tf_op jit(solution)/shard_map/ppermute | solution.py:35
  20.5 29.2 %collective-permute-start.15 = (bf16[12,16,768]{2,1,0:T(8,128)(2,1)S(1)}, bf16[12,16,768]{2,1,0:T(8,128)(2,1)S(1)}, u32[]{:S(2)}, u32[]{:S(2)}) collective-permute-start(bf16[12,16,768]{2,1,0:T(8,128)(2,1)S(1)} %slice.56.refs_0_), channel_id=1, source_target_pairs={{0,2},{2,0},{4,6},{6,4},{8,10},{10,8},{12,14},{14,12},{1,3},{3,1},... | collective-permute-start | bytes 884744 | tf_op jit(solution)/shard_map/ppermute | solution.py:35
  21.0 28.7 %collective-permute-start.20 = (bf16[12,16,768]{2,1,0:T(8,128)(2,1)S(1)}, bf16[12,16,768]{2,1,0:T(8,128)(2,1)S(1)}, u32[]{:S(2)}, u32[]{:S(2)}) collective-permute-start(bf16[12,16,768]{2,1,0:T(8,128)(2,1)S(1)} %slice.57), channel_id=1, source_target_pairs={{1,0},{0,1},{3,2},{2,3},{5,4},{4,5},{7,6},{6,7},{9,8},{8,9},{11,10... | collective-permute-start | bytes 884744 | tf_op jit(solution)/shard_map/ppermute | solution.py:17
  22.5 9.9 %collective-permute-start.1 = (bf16[12,16,768]{2,1,0:T(8,128)(2,1)S(1)}, bf16[12,16,768]{2,1,0:T(8,128)(2,1)S(1)}, u32[]{:S(2)}, u32[]{:S(2)}) collective-permute-start(bf16[12,16,768]{2,1,0:T(8,128)(2,1)S(1)} %collective-permute-done.refs_2_), channel_id=1, source_target_pairs={{0,8},{2,10},{8,12},{10,14},{12,4},{14,6},{4,0},{6,2},{1,9},{3,11}... | collective-permute-start | bytes 884744 | tf_op jit(solution)/shard_map/ppermute | solution.py:30
  25.8 36.5 %copy-start.5 = (bf16[2,4,16,768]{3,2,1,0:T(8,128)(2,1)}, bf16[2,4,16,768]{3,2,1,0:T(8,128)(2,1)S(1)}, u32[]{:S(2)}) copy-start(bf16[2,4,16,768]{3,2,1,0:T(8,128)(2,1)S(1)} %collective-permute-done.21.refs_2_) | copy-start | bytes 589828
  25.8 10.8 %collective-permute-start.22 = (bf16[2,4,16,768]{3,2,1,0:T(8,128)(2,1)S(1)}, bf16[2,4,16,768]{3,2,1,0:T(8,128)(2,1)S(1)}, u32[]{:S(2)}, u32[]{:S(2)}) collective-permute-start(bf16[2,4,16,768]{3,2,1,0:T(8,128)(2,1)S(1)} %collective-permute-done.21.refs_2_), channel_id=1, source_target_pairs={{0,8},{2,10},{8,12},{10,14},{12,4},{14,6},{4,0},{6,2},{1,9},{3,11}... | collective-permute-start | bytes 589832 | tf_op jit(solution)/shard_map/ppermute | solution.py:30
  32.5 10.8 %collective-permute-start.2 = (bf16[12,16,768]{2,1,0:T(8,128)(2,1)S(1)}, bf16[12,16,768]{2,1,0:T(8,128)(2,1)S(1)}, u32[]{:S(2)}, u32[]{:S(2)}) collective-permute-start(bf16[12,16,768]{2,1,0:T(8,128)(2,1)S(1)} %collective-permute-done.1.refs_4_), channel_id=1, source_target_pairs={{0,8},{2,10},{8,12},{10,14},{12,4},{14,6},{4,0},{6,2},{1,9},{3,11}... | collective-permute-start | bytes 884744 | tf_op jit(solution)/shard_map/ppermute | solution.py:30
  36.7 29.1 %copy-start.9 = (bf16[2,4,16,768]{3,2,1,0:T(8,128)(2,1)}, bf16[2,4,16,768]{3,2,1,0:T(8,128)(2,1)S(1)}, u32[]{:S(2)}) copy-start(bf16[2,4,16,768]{3,2,1,0:T(8,128)(2,1)S(1)} %collective-permute-done.22.refs_4_) | copy-start | bytes 589828
  36.7 9.6 %collective-permute-start.23 = (bf16[2,4,16,768]{3,2,1,0:T(8,128)(2,1)S(1)}, bf16[2,4,16,768]{3,2,1,0:T(8,128)(2,1)S(1)}, u32[]{:S(2)}, u32[]{:S(2)}) collective-permute-start(bf16[2,4,16,768]{3,2,1,0:T(8,128)(2,1)S(1)} %collective-permute-done.22.refs_4_), channel_id=1, source_target_pairs={{0,8},{2,10},{8,12},{10,14},{12,4},{14,6},{4,0},{6,2},{1,9},{3,11}... | collective-permute-start | bytes 589832 | tf_op jit(solution)/shard_map/ppermute | solution.py:30
  43.3 7.1 %collective-permute-start.45 = (bf16[2,4,16,768]{3,2,1,0:T(8,128)(2,1)S(1)}, bf16[2,4,16,768]{3,2,1,0:T(8,128)(2,1)S(1)}, u32[]{:S(2)}, u32[]{:S(2)}) collective-permute-start(bf16[2,4,16,768]{3,2,1,0:T(8,128)(2,1)S(1)} %collective-permute-done.21.refs_2_), channel_id=1, source_target_pairs={{0,2},{2,0},{4,6},{6,4},{8,10},{10,8},{12,14},{14,12},{1,3},{3,1},... | collective-permute-start | bytes 589832 | tf_op jit(solution)/shard_map/ppermute | solution.py:35
  44.0 16.4 %collective-permute-start.16 = (bf16[12,16,768]{2,1,0:T(8,128)(2,1)S(1)}, bf16[12,16,768]{2,1,0:T(8,128)(2,1)S(1)}, u32[]{:S(2)}, u32[]{:S(2)}) collective-permute-start(bf16[12,16,768]{2,1,0:T(8,128)(2,1)S(1)} %collective-permute-done.refs_2_), channel_id=1, source_target_pairs={{0,2},{2,0},{4,6},{6,4},{8,10},{10,8},{12,14},{14,12},{1,3},{3,1},... | collective-permute-start | bytes 884744 | tf_op jit(solution)/shard_map/ppermute | solution.py:35
  46.3 19.5 %copy-start.11 = (bf16[2,4,16,768]{3,2,1,0:T(8,128)(2,1)}, bf16[2,4,16,768]{3,2,1,0:T(8,128)(2,1)S(1)}, u32[]{:S(2)}) copy-start(bf16[2,4,16,768]{3,2,1,0:T(8,128)(2,1)S(1)} %collective-permute-done.23.refs_6_) | copy-start | bytes 589828
  46.3 10.7 %collective-permute-start.3 = (bf16[2,6,16,768]{3,2,1,0:T(8,128)(2,1)S(1)}, bf16[2,6,16,768]{3,2,1,0:T(8,128)(2,1)S(1)}, u32[]{:S(2)}, u32[]{:S(2)}) collective-permute-start(bf16[2,6,16,768]{3,2,1,0:T(8,128)(2,1)S(1)} %pad_maximum_fusion.refs_0_), channel_id=1, source_target_pairs={{0,8},{2,10},{8,12},{10,14},{12,4},{14,6},{4,0},{6,2},{1,9},{3,11}... | collective-permute-start | bytes 884744 | tf_op jit(solution)/shard_map/ppermute | solution.py:30
  49.6 1.7 collective-permute-start.46
  49.7 2.6 %copy-start.3 = (bf16[12,16,768]{2,1,0:T(8,128)(2,1)}, bf16[12,16,768]{2,1,0:T(8,128)(2,1)S(1)}, u32[]{:S(2)}) copy-start(bf16[12,16,768]{2,1,0:T(8,128)(2,1)S(1)} %collective-permute-done.20.refs_0_) | copy-start | bytes 884740
  49.7 12.6 %collective-permute-start.24 = (bf16[2,5,16,768]{3,2,1,0:T(8,128)(2,1)S(1)}, bf16[2,5,16,768]{3,2,1,0:T(8,128)(2,1)}, u32[]{:S(2)}, u32[]{:S(2)}) collective-permute-start(bf16[2,5,16,768]{3,2,1,0:T(8,128)(2,1)S(1)} %pad_maximum_fusion.2.refs_0_), channel_id=1, source_target_pairs={{0,8},{2,10},{8,12},{10,14},{12,4},{14,6},{4,0},{6,2},{1,9},{3,11}... | collective-permute-start | bytes 737288 | tf_op jit(solution)/shard_map/ppermute | solution.py:30
  51.1 14.7 %collective-permute-start.47 = (bf16[2,4,16,768]{3,2,1,0:T(8,128)(2,1)S(1)}, bf16[2,4,16,768]{3,2,1,0:T(8,128)(2,1)S(1)}, u32[]{:S(2)}, u32[]{:S(2)}) collective-permute-start(bf16[2,4,16,768]{3,2,1,0:T(8,128)(2,1)S(1)} %collective-permute-done.23.refs_6_), channel_id=1, source_target_pairs={{0,2},{2,0},{4,6},{6,4},{8,10},{10,8},{12,14},{14,12},{1,3},{3,1},... | collective-permute-start | bytes 589832 | tf_op jit(solution)/shard_map/ppermute | solution.py:35
  52.0 29.5 %collective-permute-start.17 = (bf16[12,16,768]{2,1,0:T(8,128)(2,1)S(1)}, bf16[12,16,768]{2,1,0:T(8,128)(2,1)S(1)}, u32[]{:S(2)}, u32[]{:S(2)}) collective-permute-start(bf16[12,16,768]{2,1,0:T(8,128)(2,1)S(1)} %collective-permute-done.1.refs_4_), channel_id=1, source_target_pairs={{0,2},{2,0},{4,6},{6,4},{8,10},{10,8},{12,14},{14,12},{1,3},{3,1},... | collective-permute-start | bytes 884744 | tf_op jit(solution)/shard_map/ppermute | solution.py:35
  57.0 25.0 %collective-permute-start.4 = (bf16[2,6,16,768]{3,2,1,0:T(8,128)(2,1)S(1)}, bf16[2,6,16,768]{3,2,1,0:T(8,128)(2,1)S(1)}, u32[]{:S(2)}, u32[]{:S(2)}) collective-permute-start(bf16[2,6,16,768]{3,2,1,0:T(8,128)(2,1)S(1)} %collective-permute-done.3.refs_2_), channel_id=1, source_target_pairs={{0,8},{2,10},{8,12},{10,14},{12,4},{14,6},{4,0},{6,2},{1,9},{3,11}... | collective-permute-start | bytes 884744 | tf_op jit(solution)/shard_map/ppermute | solution.py:30
  60.4 19.5 %collective-permute-start.34 = (bf16[2,5,16,768]{3,2,1,0:T(8,128)(2,1)S(1)}, bf16[2,5,16,768]{3,2,1,0:T(8,128)(2,1)}, u32[]{:S(2)}, u32[]{:S(2)}) collective-permute-start(bf16[2,5,16,768]{3,2,1,0:T(8,128)(2,1)S(1)} %pad_maximum_fusion.2.refs_0_), channel_id=1, source_target_pairs={{0,2},{2,0},{4,6},{6,4},{8,10},{10,8},{12,14},{14,12},{1,3},{3,1},... | collective-permute-start | bytes 737288 | tf_op jit(solution)/shard_map/ppermute | solution.py:35
  62.3 19.4 %collective-permute-start.25 = (bf16[2,5,16,768]{3,2,1,0:T(8,128)(2,1)}, bf16[2,5,16,768]{3,2,1,0:T(8,128)(2,1)}, u32[]{:S(2)}, u32[]{:S(2)}) collective-permute-start(bf16[2,5,16,768]{3,2,1,0:T(8,128)(2,1)} %collective-permute-done.24.refs_2_), channel_id=1, source_target_pairs={{0,8},{2,10},{8,12},{10,14},{12,4},{14,6},{4,0},{6,2},{1,9},{3,11}... | collective-permute-start | bytes 737288 | tf_op jit(solution)/shard_map/ppermute | solution.py:30
  66.5 15.5 %collective-permute-start.35 = (bf16[2,5,16,768]{3,2,1,0:T(8,128)(2,1)}, bf16[2,5,16,768]{3,2,1,0:T(8,128)(2,1)}, u32[]{:S(2)}, u32[]{:S(2)}) collective-permute-start(bf16[2,5,16,768]{3,2,1,0:T(8,128)(2,1)} %collective-permute-done.24.refs_2_), channel_id=1, source_target_pairs={{0,2},{2,0},{4,6},{6,4},{8,10},{10,8},{12,14},{14,12},{1,3},{3,1},... | collective-permute-start | bytes 737288 | tf_op jit(solution)/shard_map/ppermute | solution.py:35
  67.2 2.8 %copy-start.1 = (bf16[1,32,16,6144]{3,2,1,0:T(8,128)(2,1)S(1)}, bf16[1,32,16,6144]{3,2,1,0:T(8,128)(2,1)}, u32[]{:S(2)}) copy-start(bf16[1,32,16,6144]{3,2,1,0:T(8,128)(2,1)} %param.9) | copy-start | bytes 18874372
  70.0 0.9 copy-start.6
  70.9 0.9 copy-start.8
  71.8 0.9 copy-start.10
  72.7 0.9 copy-start.12
  73.7 0.9 copy-start.14
  79.9 17.3 %copy-start.20 = (bf16[1,5,16,768]{3,2,1,0:T(8,128)(2,1)S(1)}, bf16[1,5,16,768]{3,2,1,0:T(8,128)(2,1)}, u32[]{:S(2)}) copy-start(bf16[1,5,16,768]{3,2,1,0:T(8,128)(2,1)} %get-tuple-element.18) | copy-start | bytes 368644
  79.9 80.4 %collective-permute-start.48 = (bf16[4,16,6144]{2,1,0:T(8,128)(2,1)S(1)}, bf16[4,16,6144]{2,1,0:T(8,128)(2,1)S(1)}, u32[]{:S(2)}, u32[]{:S(2)}) collective-permute-start(bf16[4,16,6144]{2,1,0:T(8,128)(2,1)S(1)} %shard_map.95), channel_id=1, source_target_pairs={{1,0},{0,1},{3,2},{2,3},{5,4},{4,5},{7,6},{6,7},{9,8},{8,9},{11,10... | collective-permute-start | bytes 2359304 | tf_op jit(solution)/shard_map/ppermute | solution.py:17
  81.4 8.3 %collective-permute-start.39 = (bf16[2,6,16,768]{3,2,1,0:T(8,128)(2,1)S(1)}, bf16[2,6,16,768]{3,2,1,0:T(8,128)(2,1)S(1)}, u32[]{:S(2)}, u32[]{:S(2)}) collective-permute-start(bf16[2,6,16,768]{3,2,1,0:T(8,128)(2,1)S(1)} %pad_maximum_fusion.refs_0_), channel_id=1, source_target_pairs={{0,2},{2,0},{4,6},{6,4},{8,10},{10,8},{12,14},{14,12},{1,3},{3,1},... | collective-permute-start | bytes 884744 | tf_op jit(solution)/shard_map/ppermute | solution.py:35
  81.7 2.4 collective-permute-start.18
  82.0 69.6 %collective-permute-start.26 = (bf16[2,5,16,768]{3,2,1,0:T(8,128)(2,1)}, bf16[2,5,16,768]{3,2,1,0:T(8,128)(2,1)S(1)}, u32[]{:S(2)}, u32[]{:S(2)}) collective-permute-start(bf16[2,5,16,768]{3,2,1,0:T(8,128)(2,1)} %collective-permute-done.25.refs_4_), channel_id=1, source_target_pairs={{0,8},{2,10},{8,12},{10,14},{12,4},{14,6},{4,0},{6,2},{1,9},{3,11}... | collective-permute-start | bytes 737288 | tf_op jit(solution)/shard_map/ppermute | solution.py:30
  82.0 14.6 %collective-permute-start.5 = (bf16[2,6,16,768]{3,2,1,0:T(8,128)(2,1)S(1)}, bf16[2,6,16,768]{3,2,1,0:T(8,128)(2,1)S(1)}, u32[]{:S(2)}, u32[]{:S(2)}) collective-permute-start(bf16[2,6,16,768]{3,2,1,0:T(8,128)(2,1)S(1)} %collective-permute-done.4.refs_4_), channel_id=1, source_target_pairs={{0,8},{2,10},{8,12},{10,14},{12,4},{14,6},{4,0},{6,2},{1,9},{3,11}... | collective-permute-start | bytes 884744 | tf_op jit(solution)/shard_map/ppermute | solution.py:30
  84.1 145.6 %collective-permute-start.14 = (bf16[12,16,6144]{2,1,0:T(8,128)(2,1)S(1)}, bf16[12,16,6144]{2,1,0:T(8,128)(2,1)S(1)}, u32[]{:S(2)}, u32[]{:S(2)}) collective-permute-start(bf16[12,16,6144]{2,1,0:T(8,128)(2,1)S(1)} %slice_bitcast_fusion), channel_id=1, source_target_pairs={{1,0},{0,1},{3,2},{2,3},{5,4},{4,5},{7,6},{6,7},{9,8},{8,9},{11,10... | collective-permute-start | bytes 7077896 | tf_op jit(solution)/shard_map/ppermute | solution.py:17
  89.8 61.8 %collective-permute-start.36 = (bf16[2,5,16,768]{3,2,1,0:T(8,128)(2,1)}, bf16[2,5,16,768]{3,2,1,0:T(8,128)(2,1)S(1)}, u32[]{:S(2)}, u32[]{:S(2)}) collective-permute-start(bf16[2,5,16,768]{3,2,1,0:T(8,128)(2,1)} %collective-permute-done.25.refs_4_), channel_id=1, source_target_pairs={{0,2},{2,0},{4,6},{6,4},{8,10},{10,8},{12,14},{14,12},{1,3},{3,1},... | collective-permute-start | bytes 737288 | tf_op jit(solution)/shard_map/ppermute | solution.py:35
  96.6 54.9 %collective-permute-start.19 = (bf16[12,16,16]{2,1,0:T(8,128)(2,1)S(1)}, bf16[12,16,16]{2,1,0:T(8,128)(2,1)S(1)}, u32[]{:S(2)}, u32[]{:S(2)}) collective-permute-start(bf16[12,16,16]{2,1,0:T(8,128)(2,1)S(1)} %shard_map.92), channel_id=1, source_target_pairs={{1,0},{0,1},{3,2},{2,3},{5,4},{4,5},{7,6},{6,7},{9,8},{8,9},{11,10... | collective-permute-start | bytes 18440 | tf_op jit(solution)/shard_map/ppermute | solution.py:17
  151.5 7.6 %collective-permute-start.7 = (bf16[2,5,16,768]{3,2,1,0:T(8,128)(2,1)S(1)}, bf16[2,5,16,768]{3,2,1,0:T(8,128)(2,1)S(1)}, u32[]{:S(2)}, u32[]{:S(2)}) collective-permute-start(bf16[2,5,16,768]{3,2,1,0:T(8,128)(2,1)S(1)} %pad_maximum_fusion.1.refs_0_), channel_id=1, source_target_pairs={{0,8},{2,10},{8,12},{10,14},{12,4},{14,6},{4,0},{6,2},{1,9},{3,11}... | collective-permute-start | bytes 737288 | tf_op jit(solution)/shard_map/ppermute | solution.py:30
  151.5 8.8 %collective-permute-start.40 = (bf16[2,6,16,768]{3,2,1,0:T(8,128)(2,1)S(1)}, bf16[2,6,16,768]{3,2,1,0:T(8,128)(2,1)S(1)}, u32[]{:S(2)}, u32[]{:S(2)}) collective-permute-start(bf16[2,6,16,768]{3,2,1,0:T(8,128)(2,1)S(1)} %collective-permute-done.3.refs_2_), channel_id=1, source_target_pairs={{0,2},{2,0},{4,6},{6,4},{8,10},{10,8},{12,14},{14,12},{1,3},{3,1},... | collective-permute-start | bytes 884744 | tf_op jit(solution)/shard_map/ppermute | solution.py:35
  151.6 9.3 %collective-permute-start.37 = (bf16[2,5,16,768]{3,2,1,0:T(8,128)(2,1)S(1)}, bf16[2,5,16,768]{3,2,1,0:T(8,128)(2,1)S(1)}, u32[]{:S(2)}, u32[]{:S(2)}) collective-permute-start(bf16[2,5,16,768]{3,2,1,0:T(8,128)(2,1)S(1)} %collective-permute-done.26.refs_6_), channel_id=1, source_target_pairs={{0,2},{2,0},{4,6},{6,4},{8,10},{10,8},{12,14},{14,12},{1,3},{3,1},... | collective-permute-start | bytes 737288 | tf_op jit(solution)/shard_map/ppermute | solution.py:35
  159.1 6.7 %collective-permute-start.9 = (bf16[2,5,16,768]{3,2,1,0:T(8,128)(2,1)S(1)}, bf16[2,5,16,768]{3,2,1,0:T(8,128)(2,1)S(1)}, u32[]{:S(2)}, u32[]{:S(2)}) collective-permute-start(bf16[2,5,16,768]{3,2,1,0:T(8,128)(2,1)S(1)} %collective-permute-done.7.refs_2_), channel_id=1, source_target_pairs={{0,8},{2,10},{8,12},{10,14},{12,4},{14,6},{4,0},{6,2},{1,9},{3,11}... | collective-permute-start | bytes 737288 | tf_op jit(solution)/shard_map/ppermute | solution.py:30
  160.3 7.9 %collective-permute-start.41 = (bf16[2,6,16,768]{3,2,1,0:T(8,128)(2,1)S(1)}, bf16[2,6,16,768]{3,2,1,0:T(8,128)(2,1)S(1)}, u32[]{:S(2)}, u32[]{:S(2)}) collective-permute-start(bf16[2,6,16,768]{3,2,1,0:T(8,128)(2,1)S(1)} %collective-permute-done.4.refs_4_), channel_id=1, source_target_pairs={{0,2},{2,0},{4,6},{6,4},{8,10},{10,8},{12,14},{14,12},{1,3},{3,1},... | collective-permute-start | bytes 884744 | tf_op jit(solution)/shard_map/ppermute | solution.py:35
  160.3 7.9 %collective-permute-start.42 = (bf16[2,6,16,768]{3,2,1,0:T(8,128)(2,1)S(1)}, bf16[2,6,16,768]{3,2,1,0:T(8,128)(2,1)S(1)}, u32[]{:S(2)}, u32[]{:S(2)}) collective-permute-start(bf16[2,6,16,768]{3,2,1,0:T(8,128)(2,1)S(1)} %collective-permute-done.5.refs_6_), channel_id=1, source_target_pairs={{0,2},{2,0},{4,6},{6,4},{8,10},{10,8},{12,14},{14,12},{1,3},{3,1},... | collective-permute-start | bytes 884744 | tf_op jit(solution)/shard_map/ppermute | solution.py:35
  160.8 12.7 %collective-permute-start.6 = (bf16[2,5,16,768]{3,2,1,0:T(8,128)(2,1)S(1)}, bf16[2,5,16,768]{3,2,1,0:T(8,128)(2,1)S(1)}, u32[]{:S(2)}, u32[]{:S(2)}) collective-permute-start(bf16[2,5,16,768]{3,2,1,0:T(8,128)(2,1)S(1)} %pad_maximum_fusion.1.refs_0_), channel_id=1, source_target_pairs={{0,2},{2,0},{4,6},{6,4},{8,10},{10,8},{12,14},{14,12},{1,3},{3,1},... | collective-permute-start | bytes 737288 | tf_op jit(solution)/shard_map/ppermute | solution.py:35
  165.8 9.3 %collective-permute-start.11 = (bf16[2,5,16,768]{3,2,1,0:T(8,128)(2,1)S(1)}, bf16[2,5,16,768]{3,2,1,0:T(8,128)(2,1)S(1)}, u32[]{:S(2)}, u32[]{:S(2)}) collective-permute-start(bf16[2,5,16,768]{3,2,1,0:T(8,128)(2,1)S(1)} %collective-permute-done.9.refs_4_), channel_id=1, source_target_pairs={{0,8},{2,10},{8,12},{10,14},{12,4},{14,6},{4,0},{6,2},{1,9},{3,11}... | collective-permute-start | bytes 737288 | tf_op jit(solution)/shard_map/ppermute | solution.py:30
  168.2 12.2 %collective-permute-start.8 = (bf16[2,5,16,768]{3,2,1,0:T(8,128)(2,1)S(1)}, bf16[2,5,16,768]{3,2,1,0:T(8,128)(2,1)S(1)}, u32[]{:S(2)}, u32[]{:S(2)}) collective-permute-start(bf16[2,5,16,768]{3,2,1,0:T(8,128)(2,1)S(1)} %collective-permute-done.7.refs_2_), channel_id=1, source_target_pairs={{0,2},{2,0},{4,6},{6,4},{8,10},{10,8},{12,14},{14,12},{1,3},{3,1},... | collective-permute-start | bytes 737288 | tf_op jit(solution)/shard_map/ppermute | solution.py:35
  168.2 12.8 %collective-permute-start.10 = (bf16[2,5,16,768]{3,2,1,0:T(8,128)(2,1)S(1)}, bf16[2,5,16,768]{3,2,1,0:T(8,128)(2,1)S(1)}, u32[]{:S(2)}, u32[]{:S(2)}) collective-permute-start(bf16[2,5,16,768]{3,2,1,0:T(8,128)(2,1)S(1)} %collective-permute-done.9.refs_4_), channel_id=1, source_target_pairs={{0,2},{2,0},{4,6},{6,4},{8,10},{10,8},{12,14},{14,12},{1,3},{3,1},... | collective-permute-start | bytes 737288 | tf_op jit(solution)/shard_map/ppermute | solution.py:35
  173.5 7.4 %copy-start.4 = (bf16[12,16,768]{2,1,0:T(8,128)(2,1)S(1)}, bf16[12,16,768]{2,1,0:T(8,128)(2,1)}, u32[]{:S(2)}) copy-start(bf16[12,16,768]{2,1,0:T(8,128)(2,1)} %copy-done.3) | copy-start | bytes 884740
  173.6 50.0 %collective-permute-start.43 = (bf16[6,16,6144]{2,1,0:T(8,128)(2,1)S(1)}, bf16[6,16,6144]{2,1,0:T(8,128)(2,1)S(1)}, u32[]{:S(2)}, u32[]{:S(2)}) collective-permute-start(bf16[6,16,6144]{2,1,0:T(8,128)(2,1)S(1)} %shard_map.94), channel_id=1, source_target_pairs={{1,0},{0,1},{3,2},{2,3},{5,4},{4,5},{7,6},{6,7},{9,8},{8,9},{11,10... | collective-permute-start | bytes 3538952 | tf_op jit(solution)/shard_map/ppermute | solution.py:17
  175.1 7.0 %collective-permute-start.12 = (bf16[2,5,16,768]{3,2,1,0:T(8,128)(2,1)S(1)}, bf16[2,5,16,768]{3,2,1,0:T(8,128)(2,1)S(1)}, u32[]{:S(2)}, u32[]{:S(2)}) collective-permute-start(bf16[2,5,16,768]{3,2,1,0:T(8,128)(2,1)S(1)} %collective-permute-done.11.refs_6_), channel_id=1, source_target_pairs={{0,2},{2,0},{4,6},{6,4},{8,10},{10,8},{12,14},{14,12},{1,3},{3,1},... | collective-permute-start | bytes 737288 | tf_op jit(solution)/shard_map/ppermute | solution.py:35
  180.4 43.1 %collective-permute-start.38 = (bf16[5,16,6144]{2,1,0:T(8,128)(2,1)S(1)}, bf16[5,16,6144]{2,1,0:T(8,128)(2,1)S(1)}, u32[]{:S(2)}, u32[]{:S(2)}) collective-permute-start(bf16[5,16,6144]{2,1,0:T(8,128)(2,1)S(1)} %shard_map.93), channel_id=1, source_target_pairs={{1,0},{0,1},{3,2},{2,3},{5,4},{4,5},{7,6},{6,7},{9,8},{8,9},{11,10... | collective-permute-start | bytes 2949128 | tf_op jit(solution)/shard_map/ppermute | solution.py:17
  181.0 9.1 %collective-permute-start.28 = (bf16[12,16,768]{2,1,0:T(8,128)(2,1)S(1)}, bf16[12,16,768]{2,1,0:T(8,128)(2,1)S(1)}, u32[]{:S(2)}, u32[]{:S(2)}) collective-permute-start(bf16[12,16,768]{2,1,0:T(8,128)(2,1)S(1)} %copy-done.4), channel_id=1, source_target_pairs={{0,8},{2,10},{8,12},{10,14},{12,4},{14,6},{4,0},{6,2},{1,9},{3,11}... | collective-permute-start | bytes 884744 | tf_op jit(solution)/shard_map/ppermute | solution.py:30
  182.1 9.5 %collective-permute-start.27 = (bf16[12,16,768]{2,1,0:T(8,128)(2,1)S(1)}, bf16[12,16,768]{2,1,0:T(8,128)(2,1)S(1)}, u32[]{:S(2)}, u32[]{:S(2)}) collective-permute-start(bf16[12,16,768]{2,1,0:T(8,128)(2,1)S(1)} %copy-done.4), channel_id=1, source_target_pairs={{0,2},{2,0},{4,6},{6,4},{8,10},{10,8},{12,14},{14,12},{1,3},{3,1},... | collective-permute-start | bytes 884744 | tf_op jit(solution)/shard_map/ppermute | solution.py:35
  190.1 53.6 %collective-permute-start.13 = (bf16[5,16,6144]{2,1,0:T(8,128)(2,1)S(1)}, bf16[5,16,6144]{2,1,0:T(8,128)(2,1)S(1)}, u32[]{:S(2)}, u32[]{:S(2)}) collective-permute-start(bf16[5,16,6144]{2,1,0:T(8,128)(2,1)S(1)} %shard_map.91), channel_id=1, source_target_pairs={{1,0},{0,1},{3,2},{2,3},{5,4},{4,5},{7,6},{6,7},{9,8},{8,9},{11,10... | collective-permute-start | bytes 2949128 | tf_op jit(solution)/shard_map/ppermute | solution.py:17
  191.6 8.0 %collective-permute-start.30 = (bf16[12,16,768]{2,1,0:T(8,128)(2,1)S(1)}, bf16[12,16,768]{2,1,0:T(8,128)(2,1)S(1)}, u32[]{:S(2)}, u32[]{:S(2)}) collective-permute-start(bf16[12,16,768]{2,1,0:T(8,128)(2,1)S(1)} %collective-permute-done.28.refs_2_), channel_id=1, source_target_pairs={{0,8},{2,10},{8,12},{10,14},{12,4},{14,6},{4,0},{6,2},{1,9},{3,11}... | collective-permute-start | bytes 884744 | tf_op jit(solution)/shard_map/ppermute | solution.py:30
  199.7 7.1 %collective-permute-start.32 = (bf16[12,16,768]{2,1,0:T(8,128)(2,1)S(1)}, bf16[12,16,768]{2,1,0:T(8,128)(2,1)S(1)}, u32[]{:S(2)}, u32[]{:S(2)}) collective-permute-start(bf16[12,16,768]{2,1,0:T(8,128)(2,1)S(1)} %collective-permute-done.30.refs_4_), channel_id=1, source_target_pairs={{0,8},{2,10},{8,12},{10,14},{12,4},{14,6},{4,0},{6,2},{1,9},{3,11}... | collective-permute-start | bytes 884744 | tf_op jit(solution)/shard_map/ppermute | solution.py:30
  206.8 22.9 %collective-permute-start.29 = (bf16[12,16,768]{2,1,0:T(8,128)(2,1)S(1)}, bf16[12,16,768]{2,1,0:T(8,128)(2,1)S(1)}, u32[]{:S(2)}, u32[]{:S(2)}) collective-permute-start(bf16[12,16,768]{2,1,0:T(8,128)(2,1)S(1)} %collective-permute-done.28.refs_2_), channel_id=1, source_target_pairs={{0,2},{2,0},{4,6},{6,4},{8,10},{10,8},{12,14},{14,12},{1,3},{3,1},... | collective-permute-start | bytes 884744 | tf_op jit(solution)/shard_map/ppermute | solution.py:35
  223.5 6.2 %collective-permute-start.31 = (bf16[12,16,768]{2,1,0:T(8,128)(2,1)S(1)}, bf16[12,16,768]{2,1,0:T(8,128)(2,1)S(1)}, u32[]{:S(2)}, u32[]{:S(2)}) collective-permute-start(bf16[12,16,768]{2,1,0:T(8,128)(2,1)S(1)} %collective-permute-done.30.refs_4_), channel_id=1, source_target_pairs={{0,2},{2,0},{4,6},{6,4},{8,10},{10,8},{12,14},{14,12},{1,3},{3,1},... | collective-permute-start | bytes 884744 | tf_op jit(solution)/shard_map/ppermute | solution.py:35
  223.5 6.2 %collective-permute-start.33 = (bf16[12,16,768]{2,1,0:T(8,128)(2,1)S(1)}, bf16[12,16,768]{2,1,0:T(8,128)(2,1)S(1)}, u32[]{:S(2)}, u32[]{:S(2)}) collective-permute-start(bf16[12,16,768]{2,1,0:T(8,128)(2,1)S(1)} %collective-permute-done.32.refs_6_), channel_id=1, source_target_pairs={{0,2},{2,0},{4,6},{6,4},{8,10},{10,8},{12,14},{14,12},{1,3},{3,1},... | collective-permute-start | bytes 884744 | tf_op jit(solution)/shard_map/ppermute | solution.py:35
  (6 other events, 4.6 us)

commit v2 on v0

--- a/solution.py
+++ b/solution.py
@@ -1,13 +1,382 @@
+import functools
+import math
+
 import jax
 import jax.numpy as jnp
 from jax import lax
+from jax.experimental import pallas as pl
+from jax.experimental.pallas import tpu as pltpu
 from jax.sharding import PartitionSpec as P
+
+CORES = 2
+LANES = 128
+MIB = 1024 * 1024
 
 
 def passed_along(block, axis, distance):
     devices = range(lax.axis_size(axis))
     route = [((i - distance) % len(devices), i) for i in devices]
     return lax.ppermute(block, axis, route)
+
+
+def chip_ring(n_chips):
+    return list(range(0, n_chips, 2)) + list(range(1, n_chips, 2))[::-1]
+
+
+def ring_step(block):
+    order = chip_ring(lax.axis_size("expert") // CORES)
+    route = []
+    for at, chip in enumerate(order):
+        after = order[(at + 1) % len(order)]
+        route += [(chip * CORES + core, after * CORES + core) for core in range(CORES)]
+    return lax.ppermute(block, "expert", route)
+
+
+def core_swap(block):
+    route = [(i, i ^ 1) for i in range(lax.axis_size("expert"))]
+    return lax.ppermute(block, "expert", route)
+
+
+def piece_owner(me, piece, n_chips):
+    chip, core = me // CORES, me % CORES
+    at = jnp.where(chip % 2 == 0, chip // 2, n_chips - 1 - chip // 2)
+    at = (at - piece // CORES + n_chips) % n_chips
+    source = jnp.where(at < (n_chips + 1) // 2, 2 * at, 2 * (n_chips - 1 - at) + 1)
+    return source * CORES + (core + piece) % CORES
+
+
+def tied(value, *after):
+    return lax.optimization_barrier((value, *after))[0]
+
+
+def rows_and_columns(shape):
+    return (lax.broadcasted_iota(jnp.int32, shape, axis) for axis in (0, 1))
+
+
+def zero_one(condition):
+    return jnp.where(condition, 1.0, 0.0).astype(jnp.bfloat16)
+
+
+def dot(a, b, contract_b=0):
+    return lax.dot_general(
+        a, b, (((1,), (contract_b,)), ((), ())), preferred_element_type=jnp.float32
+    )
+
+
+def generator_kernel(
+    chunks, rank, expert_ref, task_ref, task_embed_ref, expert_embed_ref, down_ref, up_ref, rows_ref, *refs
+):
+    whole_ref, raw_down_ref, carrier_ref = refs[:3]
+    chunk_refs = refs[3 : 3 + len(chunks)]
+    code_ref, tasks_ref, experts_ref, spread_ref, down_sum, up_sum, copied = refs[3 + len(chunks) :]
+    step = pl.program_id(0)
+    n_blocks, per_step = code_ref.shape[0], spread_ref.shape[2]
+    per_seq = n_blocks // task_ref.shape[0]
+    n_rows = n_blocks * rank
+    width = down_ref.shape[3]
+    raw = raw_down_ref.shape[0]
+    pieces = carrier_ref.shape[2] // width
+    carried = carrier_ref.shape[0] - raw // pieces
+    copy = pltpu.make_async_copy(
+        rows_ref.at[pl.ds(0, carried)], carrier_ref.at[pl.ds(0, carried)], copied
+    )
+
+    @pl.when(step == 0)
+    def _():
+        copy.start()
+        tasks_ref[...] = task_embed_ref[...].astype(jnp.float32)
+        experts_ref[...] = expert_embed_ref[0].astype(jnp.float32)
+        for block in range(n_blocks):
+            task = tasks_ref[pl.ds(task_ref[block // per_seq], 1), :]
+            expert = experts_ref[pl.ds(expert_ref[block], 1), :]
+            code_ref[pl.ds(block, 1), :] = task + expert
+        code = jax.nn.silu(code_ref[...]).astype(jnp.bfloat16)
+        row, block = rows_and_columns((n_rows, n_blocks))
+        repeat = zero_one(row // rank == block)
+        for part in range(spread_ref.shape[0]):
+            columns = code[:, part * per_step : (part + 1) * per_step]
+            spread_ref[part] = dot(repeat, columns).astype(jnp.bfloat16)
+        down_sum[...] = jnp.zeros_like(down_sum)
+        up_sum[...] = jnp.zeros_like(up_sum)
+
+    entry, column = rows_and_columns((per_step, per_step * rank))
+    wide = dot(spread_ref[step], zero_one(column // rank == entry)).astype(jnp.bfloat16)
+    row, column = rows_and_columns(wide.shape)
+    wide = jnp.where(row % rank == column % rank, wide, jnp.zeros_like(wide))
+    down_sum[...] += dot(wide, down_ref[0].reshape(per_step * rank, width))
+    up_sum[...] += dot(wide, up_ref[0].reshape(per_step * rank, width))
+
+    @pl.when(step == pl.num_programs(0) - 1)
+    def _():
+        shape = (n_blocks, rank, width)
+        down = down_sum[...].astype(jnp.bfloat16).reshape(shape)
+        up = up_sum[...].astype(jnp.bfloat16).reshape(shape)
+        whole_ref[0], whole_ref[1] = down, up
+        raw_down_ref[...] = down[:raw]
+        for (first, last), ref in zip(chunks, chunk_refs):
+            ref[0], ref[1] = down[first:last], up[first:last]
+        for block in range(raw):
+            at = pl.ds(block % pieces * width, width)
+            carrier_ref[carried + block // pieces, :, at] = up[block]
+        copy.wait()
+
+
+def generated(expert_ids, task_ids, task_embed, expert_embed, gen_down, gen_up, rows, raw, carried, chunks):
+    _, hyp, rank, width = gen_down.shape
+    n_blocks, held, dim = rows.shape
+    per_step = math.gcd(hyp, 64)
+    n_rows = n_blocks * rank
+    shapes = [(2, n_blocks, rank, width), (raw, rank, width), (carried + raw * width // dim, held, dim)]
+    shapes += [(2, last - first, rank, width) for first, last in chunks]
+
+    def whole(shape):
+        return pl.BlockSpec(shape, lambda h, *_: (0,) * len(shape))
+
+    generator = pl.BlockSpec((1, per_step, rank, width), lambda h, *_: (0, h, 0, 0))
+    return pl.pallas_call(
+        functools.partial(generator_kernel, chunks, rank),
+        out_shape=[jax.ShapeDtypeStruct(shape, jnp.bfloat16) for shape in shapes],
+        grid_spec=pltpu.PrefetchScalarGridSpec(
+            num_scalar_prefetch=2,
+            grid=(hyp // per_step,),
+            in_specs=[
+                whole(task_embed.shape),
+                whole(expert_embed.shape),
+                generator,
+                generator,
+                pl.BlockSpec(memory_space=pl.ANY),
+            ],
+            out_specs=[whole(shape) for shape in shapes],
+            scratch_shapes=[
+                pltpu.VMEM((n_blocks, hyp), jnp.float32),
+                pltpu.VMEM(task_embed.shape, jnp.float32),
+                pltpu.VMEM(expert_embed.shape[1:], jnp.float32),
+                pltpu.VMEM((hyp // per_step, n_rows, per_step), jnp.bfloat16),
+                pltpu.VMEM((n_rows, width), jnp.float32),
+                pltpu.VMEM((n_rows, width), jnp.float32),
+                pltpu.SemaphoreType.DMA,
+            ],
+        ),
+        compiler_params=params(),
+        cost_estimate=tiny_cost(),
+    )(expert_ids, task_ids, task_embed, expert_embed, gen_down, gen_up, rows)
+
+
+def columns(me_ref, piece, n_pieces, width):
+    owner = piece_owner(me_ref[0], piece, n_pieces // CORES)
+    return pl.ds(pl.multiple_of(owner * width, 128), width)
+
+
+def flat(block):
+    return block.reshape(-1, block.shape[-1])
+
+
+def own_blocks(matrix, rank):
+    row, column = rows_and_columns(matrix.shape)
+    n_rows = matrix.shape[0] // (matrix.shape[1] // rank)
+    return jnp.where(row // n_rows == column // rank, matrix, jnp.zeros_like(matrix))
+
+
+def low_of(me_ref, rows_ref, gain_ref, normed_ref, maps, width, rank):
+    values = flat(rows_ref[...]).astype(jnp.float32)
+    scale = lax.rsqrt(jnp.mean(values * values, axis=-1, keepdims=True) + 1e-05)
+    normed_ref[...] = (values * scale * gain_ref[...].astype(jnp.float32)).astype(jnp.bfloat16)
+    total = None
+    for piece, down in enumerate(maps):
+        part = dot(normed_ref[:, columns(me_ref, piece, len(maps), width)], flat(down), 1)
+        total = part if total is None else total + part
+    return own_blocks(total.astype(jnp.bfloat16), rank)
+
+
+def add_update(me_ref, out_ref, rows_ref, low, maps, width):
+    for piece, up in enumerate(maps):
+        at = columns(me_ref, piece, len(maps), width)
+        block = rows_ref[:, :, at]
+        update = dot(low, flat(up)).reshape(block.shape)
+        out_ref[:, :, at] = (block.astype(jnp.float32) + update).astype(jnp.bfloat16)
+
+
+def layer_kernel(n, rank, width, me_ref, rows_ref, gain_ref, *refs):
+    pieces, wide_refs, (out_ref, normed_ref) = refs[:n], refs[n:-2], refs[-2:]
+    downs = [p[0] for p in pieces]
+    low = low_of(me_ref, rows_ref, gain_ref, normed_ref, downs, width, rank)
+    add_update(me_ref, out_ref, rows_ref, low, [p[1] for p in pieces], width)
+    dim = rows_ref.shape[2]
+    for wide_ref in wide_refs:
+        for block in range(out_ref.shape[0]):
+            part = pl.ds(block * LANES, LANES)
+            kept = (block + 1) * LANES <= wide_ref.shape[2]
+            values = wide_ref[0, :, part] if kept else jnp.zeros_like(wide_ref[0, :, :LANES])
+            out_ref[block, :, dim:] = values
+
+
+def block_columns(step, n_columns, width):
+    row, column = rows_and_columns((n_columns, width))
+    return zero_one(column == row + step * n_columns)
+
+
+def low_kernel(n, rank, width, me_ref, rows_ref, gain_ref, *refs):
+    pieces, out_ref, normed_ref, wide_ref = refs[:n], refs[n], refs[n + 1], refs[n + 2]
+    downs = [p[...].reshape(-1, rank, width) for p in pieces]
+    low = low_of(me_ref, rows_ref, gain_ref, normed_ref, downs, width, rank)
+    held = rows_ref.shape[1]
+    row, column = rows_and_columns((held, low.shape[0]))
+    folded = dot(zero_one(column % held == row), low).astype(jnp.bfloat16)
+    step = pl.program_id(0)
+    mine = dot(folded, block_columns(step, folded.shape[1], wide_ref.shape[1]))
+
+    @pl.when(step == 0)
+    def _():
+        wide_ref[...] = mine
+
+    @pl.when(step > 0)
+    def _():
+        wide_ref[...] += mine
+
+    @pl.when(step == pl.num_programs(0) - 1)
+    def _():
+        out_ref[0] = wide_ref[...].astype(out_ref.dtype)
+
+
+def update_kernel(n, rank, width, first_step, me_ref, rows_ref, wide_ref, *refs):
+    pieces, out_ref = refs[:n], refs[-1]
+    count, held, _ = rows_ref.shape
+    wide = jnp.concatenate([wide_ref[i] for i in range(wide_ref.shape[0])], axis=1)
+    places = block_columns(pl.program_id(0) + first_step, count * rank, wide.shape[1])
+    folded = dot(wide, places, 1).astype(jnp.bfloat16)
+    row, column = rows_and_columns((count * held, held))
+    low = own_blocks(dot(zero_one(row % held == column), folded).astype(jnp.bfloat16), rank)
+    add_update(me_ref, out_ref, rows_ref, low, [p[...] for p in pieces], width)
+
+
+def place_kernel(first, count, block_ref, *refs):
+    out_ref, arrived = refs[-2], refs[-1]
+    dim = out_ref.shape[2]
+    copy = pltpu.make_async_copy(
+        block_ref.at[:, :, pl.ds(0, dim)], out_ref.at[pl.ds(first, count)], arrived
+    )
+    copy.start()
+    copy.wait()
+
+
+def tiny_cost():
+    return pl.CostEstimate(flops=1, bytes_accessed=1, transcendentals=0)
+
+
+def params(mib=56):
+    return pltpu.CompilerParams(vmem_limit_bytes=mib * MIB)
+
+
+def per_step(first, count):
+    blocks = math.gcd(first, count)
+    return blocks // 2 if blocks > 4 and blocks % 2 == 0 else blocks
+
+
+def blocks_of(*shape, first=0):
+    zeros = (0,) * (len(shape) - 1)
+    return pl.BlockSpec(shape, lambda b, s: (b + first // shape[0], *zeros))
+
+
+def pair_blocks(size, rank, width, first=0):
+    return pl.BlockSpec((2, size, rank, width), lambda b, s: (0, b + first // size, 0, 0))
+
+
+def all_gain(dim):
+    return pl.BlockSpec((1, dim), lambda b, s: (0, 0))
+
+
+def layer_blocks(me, rows, first, count, gain, other, pieces, skipped, *wide):
+    rank, width = pieces[0].shape[2:]
+    held, dim = rows.shape[1:]
+    size = per_step(first, count)
+    pieces = [pieces[0], other] + pieces[1:]
+    specs = [pair_blocks(size, rank, width, skipped)] * len(pieces)
+    specs[1] = pair_blocks(size, rank, width, first)
+    specs += [pl.BlockSpec(low.shape, lambda b, s: (0, 0, 0)) for low in wide]
+    out_dim = dim + LANES * len(wide)
+    return pl.pallas_call(
+        functools.partial(layer_kernel, len(pieces), rank, width),
+        out_shape=jax.ShapeDtypeStruct((count, held, out_dim), jnp.bfloat16),
+        grid_spec=pltpu.PrefetchScalarGridSpec(
+            num_scalar_prefetch=1,
+            grid=(count // size,),
+            in_specs=[blocks_of(size, held, dim, first=first), all_gain(dim)] + specs,
+            out_specs=blocks_of(size, held, out_dim),
+            scratch_shapes=[pltpu.VMEM((size * held, dim), jnp.bfloat16)],
+        ),
+        compiler_params=params(),
+        cost_estimate=tiny_cost(),
+    )(me, rows, gain, *pieces, *wide)
+
+
+def low_lanes(raw, rank):
+    return -(-raw * rank // LANES) * LANES
+
+
+def low_blocks(me, rows, gain, other, pieces):
+    count, rank, width = pieces[0].shape
+    held, dim = rows.shape[1:]
+    size = per_step(count, count // 2)
+    lanes = low_lanes(count, rank)
+    pieces = [pieces[0], other] + pieces[1:]
+    specs = [blocks_of(size, rank, width)] * len(pieces)
+    specs[1] = pl.BlockSpec((1, size, rank, width), lambda b, s: (0, b, 0, 0))
+    return pl.pallas_call(
+        functools.partial(low_kernel, len(pieces), rank, width),
+        out_shape=jax.ShapeDtypeStruct((1, held, lanes), jnp.bfloat16),
+        grid_spec=pltpu.PrefetchScalarGridSpec(
+            num_scalar_prefetch=1,
+            grid=(count // size,),
+            in_specs=[blocks_of(size, held, dim), all_gain(dim)] + specs,
+            out_specs=pl.BlockSpec((1, held, lanes), lambda b, s: (0, 0, 0)),
+            scratch_shapes=[
+                pltpu.VMEM((size * held, dim), jnp.bfloat16),
+                pltpu.VMEM((held, lanes), jnp.float32),
+            ],
+        ),
+        compiler_params=params(),
+        cost_estimate=tiny_cost(),
+    )(me, rows, gain, *pieces)
+
+
+def update_blocks(me, rows, count, with_low, pieces, first, result):
+    n, (raw, rank, width) = len(pieces), pieces[0].shape
+    held, dim = rows.shape[1:]
+    size = per_step(first, count) if first else per_step(count, count // 2)
+    low_spec = pl.BlockSpec(
+        (low_lanes(raw, rank) // LANES, held, LANES), lambda b, s: (0, 0, dim // LANES)
+    )
+    return pl.pallas_call(
+        functools.partial(update_kernel, n, rank, width, first // size),
+        out_shape=jax.ShapeDtypeStruct(result.shape, result.dtype),
+        grid_spec=pltpu.PrefetchScalarGridSpec(
+            num_scalar_prefetch=1,
+            grid=(count // size,),
+            in_specs=[blocks_of(size, held, dim), low_spec]
+            + [blocks_of(size, rank, width, first=first)] * n
+            + [pl.BlockSpec(memory_space=pl.ANY)],
+            out_specs=blocks_of(size, held, dim, first=first),
+        ),
+        input_output_aliases={3 + n: 0},
+        compiler_params=params(),
+        cost_estimate=tiny_cost(),
+    )(me, rows, with_low, *pieces, result)
+
+
+def place_blocks(block, first, result, shape):
+    count, held = block.shape[:2]
+    into = [] if result is None else [result]
+    return pl.pallas_call(
+        functools.partial(place_kernel, first, count),
+        out_shape=jax.ShapeDtypeStruct(shape, jnp.bfloat16),
+        in_specs=[pl.BlockSpec(memory_space=pltpu.VMEM)]
+        + [pl.BlockSpec(memory_space=pl.ANY)] * len(into),
+        out_specs=pl.BlockSpec(memory_space=pl.ANY),
+        scratch_shapes=[pltpu.SemaphoreType.DMA],
+        input_output_aliases={1: 0} if into else {},
+        compiler_params=params(4),
+        cost_estimate=tiny_cost(),
+    )(block, *into)
 
 
 def norm_rows(block_rows, gain):
@@ -26,15 +395,14 @@
     return (values + update).astype(jnp.bfloat16)
 
 
-def on_device(
+def gathered_whole(
     activations, block_expert, seq_task, norm_gain, task_embed, expert_embed, gen_down, gen_up
 ):
-    tokens_in = activations[0]
+    rows = activations[0]
     expert_ids = block_expert[0, :, 0]
     n_blocks = expert_ids.shape[0]
     per_seq = n_blocks // seq_task.shape[1]
     task_ids = seq_task[0][jnp.arange(n_blocks, dtype=jnp.int32) // per_seq]
-    gain = norm_gain[0]
     code_all = jax.nn.silu(
         task_embed.astype(jnp.float32)[:, None, :] + expert_embed[0].astype(jnp.float32)[None]
     ).astype(jnp.bfloat16)
@@ -49,8 +417,80 @@
         lax.all_gather(down_part, "expert", axis=2, tiled=True),
         lax.all_gather(up_part, "expert", axis=2, tiled=True),
     )
-    result = apply_adapter(tokens_in, gain, down_full, up_full)
+    result = apply_adapter(rows, norm_gain[0], down_full, up_full)
     return passed_along(result[None], "section", 1)
+
+
+def on_device(
+    activations, block_expert, seq_task, norm_gain, task_embed, expert_embed, gen_down, gen_up
+):
+    n_blocks, held, dim = activations.shape[1:]
+    rank, width = gen_down.shape[2:]
+    n_devices = lax.axis_size("expert")
+    raw, early = n_blocks // 2, n_blocks // 8
+    chunks = [(raw, raw + n_blocks // 4), (raw + n_blocks // 4, n_blocks)]
+    aligned = held % 16 == 0 and rank % 16 == 0 and width % LANES == 0
+    if not aligned or n_blocks % 32 or raw % n_devices or n_devices % CORES or n_devices // CORES != 4:
+        return gathered_whole(
+            activations, block_expert, seq_task, norm_gain, task_embed, expert_embed, gen_down, gen_up
+        )
+
+    rows = activations[0]
+    carried = raw - early
+    early_sent = passed_along(rows[carried:raw], "section", 1)
+    whole, raw_down, carrier, *chunk_maps = generated(
+        block_expert[0, :, 0], seq_task[0], task_embed, expert_embed, gen_down, gen_up,
+        rows, raw, carried, chunks,
+    )
+    carrier_sent = passed_along(carrier, "section", 1)
+    ups = carrier_sent[carried:].reshape(-1, held, n_devices, width).swapaxes(1, 2)
+    me = jnp.reshape(lax.axis_index("expert"), (1,)).astype(jnp.int32)
+    other = core_swap(whole)
+
+    ends, swaps = [], []
+
+    class Gather:
+        def __init__(self, block):
+            self.held, self.pieces = block, [block]
+
+        def step(self, *after, before_swap=()):
+            k = len(ends)
+            after = [*after, *ends[max(k - 2, 0) : max(k - 1, 0)], *swaps[max(k - 3, 0) : max(k - 2, 0)]]
+            ends.append(ring_step(tied(self.held, *after) if after else self.held))
+            swaps.append(core_swap(tied(ends[-1], *before_swap) if before_swap else ends[-1]))
+            self.held = ends[-1]
+            self.pieces += [ends[-1], swaps[-1]]
+
+    first, second = (Gather(block) for block in chunk_maps)
+    downs, ups = Gather(raw_down), Gather(ups.reshape(raw, rank, width))
+    first.step()
+    first.step(early_sent)
+    downs.step()
+    first.step()
+    (at, end), (middle, last) = chunks[0], (chunks[1][0] + n_blocks // 8, n_blocks)
+    first_out = layer_blocks(me, rows, at, end - at, norm_gain, other, first.pieces, 0)
+    first_sent = passed_along(tied(first_out, early_sent), "section", 1)
+    downs.step()
+    second.step()
+    downs.step(first_out)
+    low = low_blocks(me, rows, norm_gain, other, downs.pieces)
+    second.step(before_swap=[low])
+    second.step()
+    second_out = layer_blocks(me, rows, end, middle - end, norm_gain, other, second.pieces, 0, low)
+    second_sent = passed_along(tied(second_out, carrier_sent), "section", 1)
+    third_out = layer_blocks(me, rows, middle, last - middle, norm_gain, other, second.pieces, middle - end)
+    third_sent = passed_along(tied(third_out, first_sent), "section", 1)
+    ups.step()
+    result = place_blocks(first_sent, at, None, rows.shape)
+    ups.held, result = lax.optimization_barrier((ups.held, result))
+    ups.step(second_out)
+    ups.step(third_out)
+
+    maps = [ups.pieces[0], core_swap(ups.pieces[0])] + ups.pieces[1:]
+    result = place_blocks(second_sent, end, result, rows.shape)
+    result = update_blocks(me, early_sent, early, second_sent, maps, carried, result)
+    result = update_blocks(me, carrier_sent, carried, second_sent, maps, 0, result)
+    return place_blocks(third_sent, middle, result, rows.shape)[None]
 
 
 def solution(mesh):

time: 314 us -> 155 us (0.49)
  waiting for transfers between devices: 256 us -> 59.9 us
  Pallas kernels: 0 us -> 45 us
  starting transfers between devices: 1.7 us -> 42.4 us
  matrix products: 28.5 us -> 0 us
  between operations: 13.5 us -> 0.28 us
  other arithmetic: 6.7 us -> 0 us
    ppermute x1 -> x5, waiting for transfers between devices: 136 us -> 0.01 us  [passed_along(): return lax.ppermute(block, axis, route)]
    all_gather x2 -> x0, waiting for transfers between devices: 120 us -> none  [the longest x1 65 us: on_device(): lax.all_gather(down_part, 'expert', axis=2, tiled=True)]
    ppermute x0 -> x26, waiting for transfers between devices: none -> 59.9 us  [the longest x12 59.1 us: ring_step(): return lax.ppermute(block, 'expert', route)]
    pallas_call x0 -> x10, Pallas kernels: none -> 45 us  [the longest x1 14 us: generated(): pl.pallas_call(functools.partial(generator_kernel, chunks, rank), out_sha...]
    ppermute x0 -> x26, starting transfers between devices: none -> 35.3 us  [the longest x12 34.3 us: ring_step(): return lax.ppermute(block, 'expert', route)]
    dot_general x3 -> x0, matrix products: 28.5 us -> none  [the longest x1 15.6 us: apply_adapter(): jnp.einsum('bnr,brd->bnd', low, up_maps, preferred_element_type=jnp.float32)]
    ppermute x1 -> x5, starting transfers between devices: 1.48 us -> 7.06 us  [passed_along(): return lax.ppermute(block, axis, route)]
    reduce_sum x1 -> x0, other arithmetic: 4.54 us -> none  [norm_rows(): scale = lax.rsqrt(jnp.mean(values * values, axis=-1, keepdims=True) + 1e-05)]
  transfers between devices with their start and end apart: 3 -> 31, of which waited for: 3 -> 13; matrix products, arithmetic and copies ran while one was open for 4% -> 1% of each run, Pallas kernels for 0% -> 29%
where the time goes in v2:
time: 155 us; the launch traced here: 154 us
  waiting for transfers between devices  59.9 us (39%)
  Pallas kernels  45 us (29%)
  starting transfers between devices  42.4 us (27%)
  local copies, waits for them, and re-layouts  6.79 us (4%)
    ppermute x12, waiting for transfers between devices, ring_step(): return lax.ppermute(block, 'expert', route)  59.1 us
    ppermute x12, starting transfers between devices, ring_step(): return lax.ppermute(block, 'expert', route)  34.3 us
    pallas_call x1, Pallas kernels, generated(): pl.pallas_call(functools.partial(generator_kernel, chunks, rank), out_sha...  14 us
    pallas_call x3, Pallas kernels, layer_blocks(): pl.pallas_call(functools.partial(layer_kernel, len(pieces), rank, width),...  13.3 us
    pallas_call x2, Pallas kernels, update_blocks(): pl.pallas_call(functools.partial(update_kernel, n, rank, width, first //...  8.22 us
    ppermute x5, starting transfers between devices, passed_along(): return lax.ppermute(block, axis, route)  7.06 us
    pallas_call x1, Pallas kernels, low_blocks(): pl.pallas_call(functools.partial(low_kernel, len(pieces), rank, width), o...  6.48 us
    unnamed x50, local copies, waits for them, and re-layouts  4.42 us
  transfers between devices with their start and end apart: 31, of which 13 were waited for; matrix products, arithmetic and copies ran while one was open for 1% of the time, Pallas kernels for 29%

profile of v2, /device:TPU:0, one launch (start us, length us, event | category | flops | bytes accessed | tf_op | source)
XLA Modules:
  0.0 154.4 jit_solution(11356474736631264497)
XLA Ops:
  0.0 1.2 slice_bitcast_fusion
  1.2 3.0 %collective-permute-start.2 = (bf16[4,16,6144]{2,1,0:T(8,128)(2,1)S(1)}, bf16[4,16,6144]{2,1,0:T(8,128)(2,1)S(1)}, u32[]{:S(2)}, u32[]{:S(2)}) collective-permute-start(bf16[4,16,6144]{2,1,0:T(8,128)(2,1)S(1)} %slice_bitcast_fusion), channel_id=1, source_target_pairs={{1,0},{0,1},{3,2},{2,3},{5,4},{4,5},{7,6},{6,7},{9,8},{8,9},{11,10... | collective-permute-start | bytes 2359304 | tf_op jit(solution)/shard_map/ppermute | solution.py:19
  4.2 14.0 %shard_map.82 = (bf16[2,32,16,768]{3,2,1,0:T(8,128)(2,1)}, bf16[16,16,768]{2,1,0:T(8,128)(2,1)}, bf16[14,16,6144]{2,1,0:T(8,128)(2,1)}, bf16[2,8,16,768]{3,2,1,0:T(8,128)(2,1)}, bf16[2,8,16,768]{3,2,1,0:T(8,128)(2,1)}) custom-call(s32[32]{0:T(128)} %bitcast.24, s32[8]{0:T(128)} %bitcast.25, bf16[8,256]{1,0:T(8,128)(2,1)} %task_embed_ref.1, ...), custom_call_target="tpu_custom_call" | custom-call | flops 1 | bytes 1 | tf_op jit(solution)/shard_map/pallas_call | solution.py:136
  18.2 2.6 %collective-permute-start.1 = (bf16[2,8,16,768]{3,2,1,0:T(8,128)(2,1)}, bf16[2,8,16,768]{3,2,1,0:T(8,128)(2,1)S(1)}, u32[]{:S(2)}, u32[]{:S(2)}) collective-permute-start(bf16[2,8,16,768]{3,2,1,0:T(8,128)(2,1)} %get-tuple-element.29.refs_0_), channel_id=1, source_target_pairs={{0,8},{2,10},{8,12},{10,14},{12,4},{14,6},{4,0},{6,2},{1,9},{3,11}... | collective-permute-start | bytes 1179656 | tf_op jit(solution)/shard_map/ppermute | solution.py:32
  20.9 0.5 collective-permute-start.22
  21.4 7.9 %collective-permute-done.1.refs_2_ = bf16[2,8,16,768]{3,2,1,0:T(8,128)(2,1)S(1)} collective-permute-done((bf16[2,8,16,768]{3,2,1,0:T(8,128)(2,1)}, bf16[2,8,16,768]{3,2,1,0:T(8,128)(2,1)S(1)}, u32[]{:S(2)}, u32[]{:S(2)}) %collective-permute-start.1) | collective-permute-done | bytes 393248 | tf_op jit(solution)/shard_map/ppermute | solution.py:32
  29.3 3.3 %collective-permute-start.3 = (bf16[2,8,16,768]{3,2,1,0:T(8,128)(2,1)S(1)}, bf16[2,8,16,768]{3,2,1,0:T(8,128)(2,1)S(1)}, u32[]{:S(2)}, u32[]{:S(2)}) collective-permute-start(bf16[2,8,16,768]{3,2,1,0:T(8,128)(2,1)S(1)} %collective-permute-done.1.refs_2_), channel_id=1, source_target_pairs={{0,8},{2,10},{8,12},{10,14},{12,4},{14,6},{4,0},{6,2},{1,9},{3,11}... | collective-permute-start | bytes 1179656 | tf_op jit(solution)/shard_map/ppermute | solution.py:32
  32.6 0.7 collective-permute-start.6
  33.3 8.9 %collective-permute-done.3.refs_4_ = bf16[2,8,16,768]{3,2,1,0:T(8,128)(2,1)S(1)} collective-permute-done((bf16[2,8,16,768]{3,2,1,0:T(8,128)(2,1)S(1)}, bf16[2,8,16,768]{3,2,1,0:T(8,128)(2,1)S(1)}, u32[]{:S(2)}, u32[]{:S(2)}) %collective-permute-start.3) | collective-permute-done | bytes 393248 | tf_op jit(solution)/shard_map/ppermute | solution.py:32
  42.2 0.0 collective-permute-start.10
  42.2 0.0 collective-permute-done.4.refs_3_
  42.2 3.4 %collective-permute-start.5 = (bf16[2,8,16,768]{3,2,1,0:T(8,128)(2,1)S(1)}, bf16[2,8,16,768]{3,2,1,0:T(8,128)(2,1)}, u32[]{:S(2)}, u32[]{:S(2)}) collective-permute-start(bf16[2,8,16,768]{3,2,1,0:T(8,128)(2,1)S(1)} %collective-permute-done.3.refs_4_), channel_id=1, source_target_pairs={{0,8},{2,10},{8,12},{10,14},{12,4},{14,6},{4,0},{6,2},{1,9},{3,11}... | collective-permute-start | bytes 1179656 | tf_op jit(solution)/shard_map/ppermute | solution.py:32
  45.6 4.6 %collective-permute-done.6.refs_2_ = bf16[16,16,768]{2,1,0:T(8,128)(2,1)S(1)} collective-permute-done((bf16[16,16,768]{2,1,0:T(8,128)(2,1)}, bf16[16,16,768]{2,1,0:T(8,128)(2,1)S(1)}, u32[]{:S(2)}, u32[]{:S(2)}) %collective-permute-start.6) | collective-permute-done | bytes 393248 | tf_op jit(solution)/shard_map/ppermute | solution.py:32
  50.3 3.3 %collective-permute-start.11 = (bf16[16,16,768]{2,1,0:T(8,128)(2,1)S(1)}, bf16[16,16,768]{2,1,0:T(8,128)(2,1)}, u32[]{:S(2)}, u32[]{:S(2)}) collective-permute-start(bf16[16,16,768]{2,1,0:T(8,128)(2,1)S(1)} %collective-permute-done.6.refs_2_), channel_id=1, source_target_pairs={{0,8},{2,10},{8,12},{10,14},{12,4},{14,6},{4,0},{6,2},{1,9},{3,11}... | collective-permute-start | bytes 1179656 | tf_op jit(solution)/shard_map/ppermute | solution.py:32
  53.6 5.0 %collective-permute-done.5.refs_6_ = bf16[2,8,16,768]{3,2,1,0:T(8,128)(2,1)} collective-permute-done((bf16[2,8,16,768]{3,2,1,0:T(8,128)(2,1)S(1)}, bf16[2,8,16,768]{3,2,1,0:T(8,128)(2,1)}, u32[]{:S(2)}, u32[]{:S(2)}) %collective-permute-start.5) | collective-permute-done | bytes 393248 | tf_op jit(solution)/shard_map/ppermute | solution.py:32
  58.6 0.0 collective-permute-start.14
  58.6 3.5 %collective-permute-start.8 = (bf16[2,8,16,768]{3,2,1,0:T(8,128)(2,1)}, bf16[2,8,16,768]{3,2,1,0:T(8,128)(2,1)S(1)}, u32[]{:S(2)}, u32[]{:S(2)}) collective-permute-start(bf16[2,8,16,768]{3,2,1,0:T(8,128)(2,1)} %get-tuple-element.34.refs_0_), channel_id=1, source_target_pairs={{0,8},{2,10},{8,12},{10,14},{12,4},{14,6},{4,0},{6,2},{1,9},{3,11}... | collective-permute-start | bytes 1179656 | tf_op jit(solution)/shard_map/ppermute | solution.py:32
  62.2 4.9 %collective-permute-done.11.refs_4_ = bf16[16,16,768]{2,1,0:T(8,128)(2,1)} collective-permute-done((bf16[16,16,768]{2,1,0:T(8,128)(2,1)S(1)}, bf16[16,16,768]{2,1,0:T(8,128)(2,1)}, u32[]{:S(2)}, u32[]{:S(2)}) %collective-permute-start.11) | collective-permute-done | bytes 393248 | tf_op jit(solution)/shard_map/ppermute | solution.py:32
  67.0 0.0 collective-permute-start.12
  67.0 0.0 collective-permute-done.refs_1_
  67.1 1.1 copy-done.1
  68.2 5.4 %shard_map.83 = bf16[8,16,6144]{2,1,0:T(8,128)(2,1)} custom-call(s32[1]{0:T(128)} %bitcast.me_ref, bf16[32,16,6144]{2,1,0:T(8,128)(2,1)} %bitcast.15, bf16[1,6144]{1,0:T(2,128)(2,1)} %gain_ref.7, bf16[2,8,16,768]{3,2,1,0:T(8,128)(2,1)} %get-tuple-element.29.refs_0_, bf16[2,32,16,768]{3,2,1,0:T(8,128)(2,1)} %copy-done.1, bf16[2,8,16,768]{3,2,1,0:T(8,128)(2,1)} %copy-done.17, ...), custom_call_target="tpu_custom_call" | custom-call | flops 1 | bytes 1 | tf_op jit(solution)/shard_map/pallas_call | solution.py:297
  73.6 0.5 collective-permute-start.20
  74.2 3.5 %collective-permute-start.15 = (bf16[16,16,768]{2,1,0:T(8,128)(2,1)}, bf16[16,16,768]{2,1,0:T(8,128)(2,1)S(1)}, u32[]{:S(2)}, u32[]{:S(2)}) collective-permute-start(bf16[16,16,768]{2,1,0:T(8,128)(2,1)} %collective-permute-done.11.refs_4_), channel_id=1, source_target_pairs={{0,8},{2,10},{8,12},{10,14},{12,4},{14,6},{4,0},{6,2},{1,9},{3,11}... | collective-permute-start | bytes 1179656 | tf_op jit(solution)/shard_map/ppermute | solution.py:32
  77.7 0.0 collective-permute-done.8.refs_2_
  77.7 0.0 collective-permute-start.9
  77.7 0.3 collective-permute-start.13
  78.0 9.5 %collective-permute-done.15.refs_6_ = bf16[16,16,768]{2,1,0:T(8,128)(2,1)S(1)} collective-permute-done((bf16[16,16,768]{2,1,0:T(8,128)(2,1)}, bf16[16,16,768]{2,1,0:T(8,128)(2,1)S(1)}, u32[]{:S(2)}, u32[]{:S(2)}) %collective-permute-start.15) | collective-permute-done | bytes 393248 | tf_op jit(solution)/shard_map/ppermute | solution.py:32
  87.4 0.0 collective-permute-start.16
  87.4 0.0 collective-permute-done.9.refs_3_
  87.5 7.6 %collective-permute-done.13.refs_4_ = bf16[2,8,16,768]{3,2,1,0:T(8,128)(2,1)S(1)} collective-permute-done((bf16[2,8,16,768]{3,2,1,0:T(8,128)(2,1)S(1)}, bf16[2,8,16,768]{3,2,1,0:T(8,128)(2,1)S(1)}, u32[]{:S(2)}, u32[]{:S(2)}) %collective-permute-start.13) | collective-permute-done | bytes 393248 | tf_op jit(solution)/shard_map/ppermute | solution.py:32
  95.1 3.4 %collective-permute-start.18 = (bf16[2,8,16,768]{3,2,1,0:T(8,128)(2,1)S(1)}, bf16[2,8,16,768]{3,2,1,0:T(8,128)(2,1)S(1)}, u32[]{:S(2)}, u32[]{:S(2)}) collective-permute-start(bf16[2,8,16,768]{3,2,1,0:T(8,128)(2,1)S(1)} %collective-permute-done.13.refs_4_), channel_id=1, source_target_pairs={{0,8},{2,10},{8,12},{10,14},{12,4},{14,6},{4,0},{6,2},{1,9},{3,11}... | collective-permute-start | bytes 1179656 | tf_op jit(solution)/shard_map/ppermute | solution.py:32
  98.4 0.7 copy-done.24
  99.2 6.5 %shard_map.84.refs_8_ = bf16[1,16,256]{2,1,0:T(8,128)(2,1)} custom-call(s32[1]{0:T(128)} %bitcast.me_ref, bf16[32,16,6144]{2,1,0:T(8,128)(2,1)} %bitcast.16, bf16[1,6144]{1,0:T(2,128)(2,1)} %gain_ref.7, bf16[16,16,768]{2,1,0:T(8,128)(2,1)} %get-tuple-element.33.refs_0_, bf16[2,32,16,768]{3,2,1,0:T(8,128)(2,1)} %copy-done.1, bf16[16,16,768]{2,1,0:T(8,128)(2,1)} %copy-done.21, ...), custom_call_target="tpu_custom_call" | custom-call | flops 1 | bytes 1 | tf_op jit(solution)/shard_map/pallas_call | solution.py:324
  105.7 0.0 collective-permute-start.17
  105.7 0.7 collective-permute-done.18.refs_6_
  106.4 0.0 collective-permute-done.22.rows_ref
  106.4 1.2 slice.12
  107.6 3.5 %collective-permute-start.25 = (bf16[16,16,768]{2,1,0:T(8,128)(2,1)S(1)}, bf16[16,16,768]{2,1,0:T(8,128)(2,1)S(1)}, u32[]{:S(2)}, u32[]{:S(2)}) collective-permute-start(bf16[16,16,768]{2,1,0:T(8,128)(2,1)S(1)} %bitcast.19), channel_id=1, source_target_pairs={{0,8},{2,10},{8,12},{10,14},{12,4},{14,6},{4,0},{6,2},{1,9},{3,11}... | collective-permute-start | bytes 1179656 | tf_op jit(solution)/shard_map/ppermute | solution.py:32
  111.0 0.0 collective-permute-done.17.refs_5_
  111.1 0.0 collective-permute-done.19.refs_7_
  111.1 0.7 copy-done.7
  111.8 0.8 copy-done.8
  112.6 4.0 %shard_map.86 = bf16[4,16,6272]{2,1,0:T(8,128)(2,1)} custom-call(s32[1]{0:T(128)} %bitcast.me_ref, bf16[32,16,6144]{2,1,0:T(8,128)(2,1)} %bitcast.17, bf16[1,6144]{1,0:T(2,128)(2,1)} %gain_ref.7, bf16[2,8,16,768]{3,2,1,0:T(8,128)(2,1)} %get-tuple-element.34.refs_0_, bf16[2,32,16,768]{3,2,1,0:T(8,128)(2,1)} %copy-done.1, bf16[2,8,16,768]{3,2,1,0:T(8,128)(2,1)} %copy-done.3, ...), custom_call_target="tpu_custom_call" | custom-call | flops 1 | bytes 1 | tf_op jit(solution)/shard_map/pallas_call | solution.py:297
  116.5 1.5 collective-permute-start.23
  118.0 1.2 shard_map.87.refs_0_
  119.2 0.7 collective-permute-done.25.refs_2_
  119.9 3.4 %collective-permute-start.27 = (bf16[16,16,768]{2,1,0:T(8,128)(2,1)S(1)}, bf16[16,16,768]{2,1,0:T(8,128)(2,1)S(1)}, u32[]{:S(2)}, u32[]{:S(2)}) collective-permute-start(bf16[16,16,768]{2,1,0:T(8,128)(2,1)S(1)} %collective-permute-done.25.refs_2_), channel_id=1, source_target_pairs={{0,8},{2,10},{8,12},{10,14},{12,4},{14,6},{4,0},{6,2},{1,9},{3,11}... | collective-permute-start | bytes 1179656 | tf_op jit(solution)/shard_map/ppermute | solution.py:32
  123.3 3.9 %shard_map.85 = bf16[4,16,6144]{2,1,0:T(8,128)(2,1)} custom-call(s32[1]{0:T(128)} %bitcast.me_ref, bf16[32,16,6144]{2,1,0:T(8,128)(2,1)} %bitcast.18, bf16[1,6144]{1,0:T(2,128)(2,1)} %gain_ref.7, bf16[2,8,16,768]{3,2,1,0:T(8,128)(2,1)} %get-tuple-element.34.refs_0_, bf16[2,32,16,768]{3,2,1,0:T(8,128)(2,1)} %copy-done.1, bf16[2,8,16,768]{3,2,1,0:T(8,128)(2,1)} %copy-done.3, ...), custom_call_target="tpu_custom_call" | custom-call | flops 1 | bytes 1 | tf_op jit(solution)/shard_map/pallas_call | solution.py:297
  127.3 4.1 %collective-permute-done.27.refs_4_ = bf16[16,16,768]{2,1,0:T(8,128)(2,1)S(1)} collective-permute-done((bf16[16,16,768]{2,1,0:T(8,128)(2,1)S(1)}, bf16[16,16,768]{2,1,0:T(8,128)(2,1)S(1)}, u32[]{:S(2)}, u32[]{:S(2)}) %collective-permute-start.27) | collective-permute-done | bytes 393248 | tf_op jit(solution)/shard_map/ppermute | solution.py:32
  131.4 3.4 %collective-permute-start.29 = (bf16[16,16,768]{2,1,0:T(8,128)(2,1)S(1)}, bf16[16,16,768]{2,1,0:T(8,128)(2,1)S(1)}, u32[]{:S(2)}, u32[]{:S(2)}) collective-permute-start(bf16[16,16,768]{2,1,0:T(8,128)(2,1)S(1)} %collective-permute-done.27.refs_4_), channel_id=1, source_target_pairs={{0,8},{2,10},{8,12},{10,14},{12,4},{14,6},{4,0},{6,2},{1,9},{3,11}... | collective-permute-start | bytes 1179656 | tf_op jit(solution)/shard_map/ppermute | solution.py:32
  134.8 1.5 collective-permute-start.21
  136.3 0.5 collective-permute-start.26
  136.8 5.2 %collective-permute-done.29.refs_6_ = bf16[16,16,768]{2,1,0:T(8,128)(2,1)S(1)} collective-permute-done((bf16[16,16,768]{2,1,0:T(8,128)(2,1)S(1)}, bf16[16,16,768]{2,1,0:T(8,128)(2,1)S(1)}, u32[]{:S(2)}, u32[]{:S(2)}) %collective-permute-start.29) | collective-permute-done | bytes 393248 | tf_op jit(solution)/shard_map/ppermute | solution.py:32
  142.0 0.5 collective-permute-start.30
  142.5 0.9 shard_map.88.refs_8_
  143.5 0.2 collective-permute-done.28.refs_5_
  143.7 0.6 collective-permute-done.30.refs_7_
  144.2 0.1 copy-done.13
  144.3 0.1 copy-done.14
  144.5 0.8 copy-done.15
  145.3 2.9 %shard_map.89.refs_8_ = bf16[32,16,6144]{2,1,0:T(8,128)(2,1)} custom-call(s32[1]{0:T(128)} %bitcast.me_ref, bf16[4,16,6144]{2,1,0:T(8,128)(2,1)} %copy-done.16, bf16[4,16,6272]{2,1,0:T(8,128)(2,1)} %copy-done, bf16[16,16,768]{2,1,0:T(8,128)(2,1)} %bitcast.21, bf16[16,16,768]{2,1,0:T(8,128)(2,1)} %copy-done.12, ...), custom_call_target="tpu_custom_call", output_to_operand_aliasing={{}: (11, {})} | custom-call | flops 1 | bytes 1 | tf_op jit(solution)/shard_map/pallas_call | solution.py:349
  148.1 5.3 %shard_map.90.refs_0_ = bf16[32,16,6144]{2,1,0:T(8,128)(2,1)} custom-call(s32[1]{0:T(128)} %bitcast.me_ref, bf16[14,16,6144]{2,1,0:T(8,128)(2,1)} %collective-permute-done.22.rows_ref, bf16[4,16,6272]{2,1,0:T(8,128)(2,1)} %copy-done, bf16[16,16,768]{2,1,0:T(8,128)(2,1)} %bitcast.22, ...), custom_call_target="tpu_custom_call", output_to_operand_aliasing={{}: (11, {})} | custom-call | flops 1 | bytes 1 | tf_op jit(solution)/shard_map/pallas_call | solution.py:349
  153.5 0.9 shard_map.91
  (61 shorter events, 0.2 us)
Async XLA Ops:
  1.2 28.1 %collective-permute-start.2 = (bf16[4,16,6144]{2,1,0:T(8,128)(2,1)S(1)}, bf16[4,16,6144]{2,1,0:T(8,128)(2,1)S(1)}, u32[]{:S(2)}, u32[]{:S(2)}) collective-permute-start(bf16[4,16,6144]{2,1,0:T(8,128)(2,1)S(1)} %slice_bitcast_fusion), channel_id=1, source_target_pairs={{1,0},{0,1},{3,2},{2,3},{5,4},{4,5},{7,6},{6,7},{9,8},{8,9},{11,10... | collective-permute-start | bytes 2359304 | tf_op jit(solution)/shard_map/ppermute | solution.py:19
  18.2 11.0 %collective-permute-start.1 = (bf16[2,8,16,768]{3,2,1,0:T(8,128)(2,1)}, bf16[2,8,16,768]{3,2,1,0:T(8,128)(2,1)S(1)}, u32[]{:S(2)}, u32[]{:S(2)}) collective-permute-start(bf16[2,8,16,768]{3,2,1,0:T(8,128)(2,1)} %get-tuple-element.29.refs_0_), channel_id=1, source_target_pairs={{0,8},{2,10},{8,12},{10,14},{12,4},{14,6},{4,0},{6,2},{1,9},{3,11}... | collective-permute-start | bytes 1179656 | tf_op jit(solution)/shard_map/ppermute | solution.py:32
  20.9 46.2 %collective-permute-start = (bf16[2,32,16,768]{3,2,1,0:T(8,128)(2,1)}, bf16[2,32,16,768]{3,2,1,0:T(8,128)(2,1)S(1)}, u32[]{:S(2)}, u32[]{:S(2)}) collective-permute-start(bf16[2,32,16,768]{3,2,1,0:T(8,128)(2,1)} %get-tuple-element.28), channel_id=1, source_target_pairs={{0,2},{2,0},{4,6},{6,4},{8,10},{10,8},{12,14},{14,12},{1,3},{3,1},... | collective-permute-start | bytes 4718600 | tf_op jit(solution)/shard_map/ppermute | solution.py:37
  20.9 85.5 %collective-permute-start.22 = (bf16[14,16,6144]{2,1,0:T(8,128)(2,1)}, bf16[14,16,6144]{2,1,0:T(8,128)(2,1)}, u32[]{:S(2)}, u32[]{:S(2)}) collective-permute-start(bf16[14,16,6144]{2,1,0:T(8,128)(2,1)} %get-tuple-element.42), channel_id=1, source_target_pairs={{1,0},{0,1},{3,2},{2,3},{5,4},{4,5},{7,6},{6,7},{9,8},{8,9},{11,10... | collective-permute-start | bytes 8257544 | tf_op jit(solution)/shard_map/ppermute | solution.py:19
  29.3 37.8 %copy-start.17 = (bf16[2,8,16,768]{3,2,1,0:T(8,128)(2,1)}, bf16[2,8,16,768]{3,2,1,0:T(8,128)(2,1)S(1)}, u32[]{:S(2)}) copy-start(bf16[2,8,16,768]{3,2,1,0:T(8,128)(2,1)S(1)} %collective-permute-done.1.refs_2_) | copy-start | bytes 1179652
  29.3 89.9 %copy-start.16 = (bf16[4,16,6144]{2,1,0:T(8,128)(2,1)}, bf16[4,16,6144]{2,1,0:T(8,128)(2,1)S(1)}, u32[]{:S(2)}) copy-start(bf16[4,16,6144]{2,1,0:T(8,128)(2,1)S(1)} %collective-permute-done.2.rows_ref) | copy-start | bytes 2359300
  29.3 12.9 %collective-permute-start.3 = (bf16[2,8,16,768]{3,2,1,0:T(8,128)(2,1)S(1)}, bf16[2,8,16,768]{3,2,1,0:T(8,128)(2,1)S(1)}, u32[]{:S(2)}, u32[]{:S(2)}) collective-permute-start(bf16[2,8,16,768]{3,2,1,0:T(8,128)(2,1)S(1)} %collective-permute-done.1.refs_2_), channel_id=1, source_target_pairs={{0,8},{2,10},{8,12},{10,14},{12,4},{14,6},{4,0},{6,2},{1,9},{3,11}... | collective-permute-start | bytes 1179656 | tf_op jit(solution)/shard_map/ppermute | solution.py:32
  32.6 9.6 %collective-permute-start.4 = (bf16[2,8,16,768]{3,2,1,0:T(8,128)(2,1)S(1)}, bf16[2,8,16,768]{3,2,1,0:T(8,128)(2,1)S(1)}, u32[]{:S(2)}, u32[]{:S(2)}) collective-permute-start(bf16[2,8,16,768]{3,2,1,0:T(8,128)(2,1)S(1)} %collective-permute-done.1.refs_2_), channel_id=1, source_target_pairs={{0,2},{2,0},{4,6},{6,4},{8,10},{10,8},{12,14},{14,12},{1,3},{3,1},... | collective-permute-start | bytes 1179656 | tf_op jit(solution)/shard_map/ppermute | solution.py:37
  32.6 17.7 %collective-permute-start.6 = (bf16[16,16,768]{2,1,0:T(8,128)(2,1)}, bf16[16,16,768]{2,1,0:T(8,128)(2,1)S(1)}, u32[]{:S(2)}, u32[]{:S(2)}) collective-permute-start(bf16[16,16,768]{2,1,0:T(8,128)(2,1)} %get-tuple-element.33.refs_0_), channel_id=1, source_target_pairs={{0,8},{2,10},{8,12},{10,14},{12,4},{14,6},{4,0},{6,2},{1,9},{3,11}... | collective-permute-start | bytes 1179656 | tf_op jit(solution)/shard_map/ppermute | solution.py:32
  42.2 24.9 %copy-start.18 = (bf16[2,8,16,768]{3,2,1,0:T(8,128)(2,1)}, bf16[2,8,16,768]{3,2,1,0:T(8,128)(2,1)S(1)}, u32[]{:S(2)}) copy-start(bf16[2,8,16,768]{3,2,1,0:T(8,128)(2,1)S(1)} %collective-permute-done.3.refs_4_) | copy-start | bytes 1179652
  42.2 8.1 %collective-permute-start.10 = (bf16[2,8,16,768]{3,2,1,0:T(8,128)(2,1)S(1)}, bf16[2,8,16,768]{3,2,1,0:T(8,128)(2,1)S(1)}, u32[]{:S(2)}, u32[]{:S(2)}) collective-permute-start(bf16[2,8,16,768]{3,2,1,0:T(8,128)(2,1)S(1)} %collective-permute-done.3.refs_4_), channel_id=1, source_target_pairs={{0,2},{2,0},{4,6},{6,4},{8,10},{10,8},{12,14},{14,12},{1,3},{3,1},... | collective-permute-start | bytes 1179656 | tf_op jit(solution)/shard_map/ppermute | solution.py:37
  42.2 16.4 %copy-start.19 = (bf16[2,8,16,768]{3,2,1,0:T(8,128)(2,1)}, bf16[2,8,16,768]{3,2,1,0:T(8,128)(2,1)S(1)}, u32[]{:S(2)}) copy-start(bf16[2,8,16,768]{3,2,1,0:T(8,128)(2,1)S(1)} %collective-permute-done.4.refs_3_) | copy-start | bytes 1179652
  42.2 16.4 %collective-permute-start.5 = (bf16[2,8,16,768]{3,2,1,0:T(8,128)(2,1)S(1)}, bf16[2,8,16,768]{3,2,1,0:T(8,128)(2,1)}, u32[]{:S(2)}, u32[]{:S(2)}) collective-permute-start(bf16[2,8,16,768]{3,2,1,0:T(8,128)(2,1)S(1)} %collective-permute-done.3.refs_4_), channel_id=1, source_target_pairs={{0,8},{2,10},{8,12},{10,14},{12,4},{14,6},{4,0},{6,2},{1,9},{3,11}... | collective-permute-start | bytes 1179656 | tf_op jit(solution)/shard_map/ppermute | solution.py:32
  50.3 11.9 %copy-start.21 = (bf16[16,16,768]{2,1,0:T(8,128)(2,1)}, bf16[16,16,768]{2,1,0:T(8,128)(2,1)S(1)}, u32[]{:S(2)}) copy-start(bf16[16,16,768]{2,1,0:T(8,128)(2,1)S(1)} %collective-permute-done.6.refs_2_) | copy-start | bytes 1179652
  50.3 8.3 %collective-permute-start.7 = (bf16[16,16,768]{2,1,0:T(8,128)(2,1)S(1)}, bf16[16,16,768]{2,1,0:T(8,128)(2,1)S(1)}, u32[]{:S(2)}, u32[]{:S(2)}) collective-permute-start(bf16[16,16,768]{2,1,0:T(8,128)(2,1)S(1)} %collective-permute-done.6.refs_2_), channel_id=1, source_target_pairs={{0,2},{2,0},{4,6},{6,4},{8,10},{10,8},{12,14},{14,12},{1,3},{3,1},... | collective-permute-start | bytes 1179656 | tf_op jit(solution)/shard_map/ppermute | solution.py:37
  50.3 8.3 %copy-start.20 = (bf16[2,8,16,768]{3,2,1,0:T(8,128)(2,1)}, bf16[2,8,16,768]{3,2,1,0:T(8,128)(2,1)S(1)}, u32[]{:S(2)}) copy-start(bf16[2,8,16,768]{3,2,1,0:T(8,128)(2,1)S(1)} %collective-permute-done.10.refs_5_) | copy-start | bytes 1179652
  50.3 16.7 %collective-permute-start.11 = (bf16[16,16,768]{2,1,0:T(8,128)(2,1)S(1)}, bf16[16,16,768]{2,1,0:T(8,128)(2,1)}, u32[]{:S(2)}, u32[]{:S(2)}) collective-permute-start(bf16[16,16,768]{2,1,0:T(8,128)(2,1)S(1)} %collective-permute-done.6.refs_2_), channel_id=1, source_target_pairs={{0,8},{2,10},{8,12},{10,14},{12,4},{14,6},{4,0},{6,2},{1,9},{3,11}... | collective-permute-start | bytes 1179656 | tf_op jit(solution)/shard_map/ppermute | solution.py:32
  58.6 8.5 %collective-permute-start.14 = (bf16[2,8,16,768]{3,2,1,0:T(8,128)(2,1)}, bf16[2,8,16,768]{3,2,1,0:T(8,128)(2,1)}, u32[]{:S(2)}, u32[]{:S(2)}) collective-permute-start(bf16[2,8,16,768]{3,2,1,0:T(8,128)(2,1)} %collective-permute-done.5.refs_6_), channel_id=1, source_target_pairs={{0,2},{2,0},{4,6},{6,4},{8,10},{10,8},{12,14},{14,12},{1,3},{3,1},... | collective-permute-start | bytes 1179656 | tf_op jit(solution)/shard_map/ppermute | solution.py:37
  58.6 8.4 %copy-start.22 = (bf16[16,16,768]{2,1,0:T(8,128)(2,1)}, bf16[16,16,768]{2,1,0:T(8,128)(2,1)S(1)}, u32[]{:S(2)}) copy-start(bf16[16,16,768]{2,1,0:T(8,128)(2,1)S(1)} %collective-permute-done.7.refs_3_) | copy-start | bytes 1179652
  58.6 19.0 %collective-permute-start.8 = (bf16[2,8,16,768]{3,2,1,0:T(8,128)(2,1)}, bf16[2,8,16,768]{3,2,1,0:T(8,128)(2,1)S(1)}, u32[]{:S(2)}, u32[]{:S(2)}) collective-permute-start(bf16[2,8,16,768]{3,2,1,0:T(8,128)(2,1)} %get-tuple-element.34.refs_0_), channel_id=1, source_target_pairs={{0,8},{2,10},{8,12},{10,14},{12,4},{14,6},{4,0},{6,2},{1,9},{3,11}... | collective-permute-start | bytes 1179656 | tf_op jit(solution)/shard_map/ppermute | solution.py:32
  67.0 10.6 %collective-permute-start.12 = (bf16[16,16,768]{2,1,0:T(8,128)(2,1)}, bf16[16,16,768]{2,1,0:T(8,128)(2,1)}, u32[]{:S(2)}, u32[]{:S(2)}) collective-permute-start(bf16[16,16,768]{2,1,0:T(8,128)(2,1)} %collective-permute-done.11.refs_4_), channel_id=1, source_target_pairs={{0,2},{2,0},{4,6},{6,4},{8,10},{10,8},{12,14},{14,12},{1,3},{3,1},... | collective-permute-start | bytes 1179656 | tf_op jit(solution)/shard_map/ppermute | solution.py:37
  67.0 1.2 copy-start.1
  73.6 44.4 %collective-permute-start.20 = (bf16[8,16,6144]{2,1,0:T(8,128)(2,1)}, bf16[8,16,6144]{2,1,0:T(8,128)(2,1)S(1)}, u32[]{:S(2)}, u32[]{:S(2)}) collective-permute-start(bf16[8,16,6144]{2,1,0:T(8,128)(2,1)} %shard_map.83), channel_id=1, source_target_pairs={{1,0},{0,1},{3,2},{2,3},{5,4},{4,5},{7,6},{6,7},{9,8},{8,9},{11,10... | collective-permute-start | bytes 4718600 | tf_op jit(solution)/shard_map/ppermute | solution.py:19
  74.2 13.3 %collective-permute-start.15 = (bf16[16,16,768]{2,1,0:T(8,128)(2,1)}, bf16[16,16,768]{2,1,0:T(8,128)(2,1)S(1)}, u32[]{:S(2)}, u32[]{:S(2)}) collective-permute-start(bf16[16,16,768]{2,1,0:T(8,128)(2,1)} %collective-permute-done.11.refs_4_), channel_id=1, source_target_pairs={{0,8},{2,10},{8,12},{10,14},{12,4},{14,6},{4,0},{6,2},{1,9},{3,11}... | collective-permute-start | bytes 1179656 | tf_op jit(solution)/shard_map/ppermute | solution.py:32
  77.7 33.4 %copy-start.3 = (bf16[2,8,16,768]{3,2,1,0:T(8,128)(2,1)}, bf16[2,8,16,768]{3,2,1,0:T(8,128)(2,1)S(1)}, u32[]{:S(2)}) copy-start(bf16[2,8,16,768]{3,2,1,0:T(8,128)(2,1)S(1)} %collective-permute-done.8.refs_2_) | copy-start | bytes 1179652
  77.7 9.8 %collective-permute-start.9 = (bf16[2,8,16,768]{3,2,1,0:T(8,128)(2,1)S(1)}, bf16[2,8,16,768]{3,2,1,0:T(8,128)(2,1)S(1)}, u32[]{:S(2)}, u32[]{:S(2)}) collective-permute-start(bf16[2,8,16,768]{3,2,1,0:T(8,128)(2,1)S(1)} %collective-permute-done.8.refs_2_), channel_id=1, source_target_pairs={{0,2},{2,0},{4,6},{6,4},{8,10},{10,8},{12,14},{14,12},{1,3},{3,1},... | collective-permute-start | bytes 1179656 | tf_op jit(solution)/shard_map/ppermute | solution.py:37
  77.7 17.4 %collective-permute-start.13 = (bf16[2,8,16,768]{3,2,1,0:T(8,128)(2,1)S(1)}, bf16[2,8,16,768]{3,2,1,0:T(8,128)(2,1)S(1)}, u32[]{:S(2)}, u32[]{:S(2)}) collective-permute-start(bf16[2,8,16,768]{3,2,1,0:T(8,128)(2,1)S(1)} %collective-permute-done.8.refs_2_), channel_id=1, source_target_pairs={{0,8},{2,10},{8,12},{10,14},{12,4},{14,6},{4,0},{6,2},{1,9},{3,11}... | collective-permute-start | bytes 1179656 | tf_op jit(solution)/shard_map/ppermute | solution.py:32
  87.4 11.0 %copy-start.23 = (bf16[16,16,768]{2,1,0:T(8,128)(2,1)}, bf16[16,16,768]{2,1,0:T(8,128)(2,1)S(1)}, u32[]{:S(2)}) copy-start(bf16[16,16,768]{2,1,0:T(8,128)(2,1)S(1)} %collective-permute-done.15.refs_6_) | copy-start | bytes 1179652
  87.4 11.0 %collective-permute-start.16 = (bf16[16,16,768]{2,1,0:T(8,128)(2,1)S(1)}, bf16[16,16,768]{2,1,0:T(8,128)(2,1)S(1)}, u32[]{:S(2)}, u32[]{:S(2)}) collective-permute-start(bf16[16,16,768]{2,1,0:T(8,128)(2,1)S(1)} %collective-permute-done.15.refs_6_), channel_id=1, source_target_pairs={{0,2},{2,0},{4,6},{6,4},{8,10},{10,8},{12,14},{14,12},{1,3},{3,1},... | collective-permute-start | bytes 1179656 | tf_op jit(solution)/shard_map/ppermute | solution.py:37
  87.4 23.6 %copy-start.4 = (bf16[2,8,16,768]{3,2,1,0:T(8,128)(2,1)}, bf16[2,8,16,768]{3,2,1,0:T(8,128)(2,1)S(1)}, u32[]{:S(2)}) copy-start(bf16[2,8,16,768]{3,2,1,0:T(8,128)(2,1)S(1)} %collective-permute-done.9.refs_3_) | copy-start | bytes 1179652
  95.1 16.0 %copy-start.5 = (bf16[2,8,16,768]{3,2,1,0:T(8,128)(2,1)}, bf16[2,8,16,768]{3,2,1,0:T(8,128)(2,1)S(1)}, u32[]{:S(2)}) copy-start(bf16[2,8,16,768]{3,2,1,0:T(8,128)(2,1)S(1)} %collective-permute-done.13.refs_4_) | copy-start | bytes 1179652
  95.1 11.3 %collective-permute-start.18 = (bf16[2,8,16,768]{3,2,1,0:T(8,128)(2,1)S(1)}, bf16[2,8,16,768]{3,2,1,0:T(8,128)(2,1)S(1)}, u32[]{:S(2)}, u32[]{:S(2)}) collective-permute-start(bf16[2,8,16,768]{3,2,1,0:T(8,128)(2,1)S(1)} %collective-permute-done.13.refs_4_), channel_id=1, source_target_pairs={{0,8},{2,10},{8,12},{10,14},{12,4},{14,6},{4,0},{6,2},{1,9},{3,11}... | collective-permute-start | bytes 1179656 | tf_op jit(solution)/shard_map/ppermute | solution.py:32
  98.4 0.7 copy-start.24
  105.7 5.4 %collective-permute-start.17 = (bf16[2,8,16,768]{3,2,1,0:T(8,128)(2,1)S(1)}, bf16[2,8,16,768]{3,2,1,0:T(8,128)(2,1)S(1)}, u32[]{:S(2)}, u32[]{:S(2)}) collective-permute-start(bf16[2,8,16,768]{3,2,1,0:T(8,128)(2,1)S(1)} %collective-permute-done.13.refs_4_), channel_id=1, source_target_pairs={{0,2},{2,0},{4,6},{6,4},{8,10},{10,8},{12,14},{14,12},{1,3},{3,1},... | collective-permute-start | bytes 1179656 | tf_op jit(solution)/shard_map/ppermute | solution.py:37
  106.4 4.7 %copy-start.6 = (bf16[2,8,16,768]{3,2,1,0:T(8,128)(2,1)}, bf16[2,8,16,768]{3,2,1,0:T(8,128)(2,1)S(1)}, u32[]{:S(2)}) copy-start(bf16[2,8,16,768]{3,2,1,0:T(8,128)(2,1)S(1)} %collective-permute-done.18.refs_6_) | copy-start | bytes 1179652
  106.4 4.7 %collective-permute-start.19 = (bf16[2,8,16,768]{3,2,1,0:T(8,128)(2,1)S(1)}, bf16[2,8,16,768]{3,2,1,0:T(8,128)(2,1)S(1)}, u32[]{:S(2)}, u32[]{:S(2)}) collective-permute-start(bf16[2,8,16,768]{3,2,1,0:T(8,128)(2,1)S(1)} %collective-permute-done.18.refs_6_), channel_id=1, source_target_pairs={{0,2},{2,0},{4,6},{6,4},{8,10},{10,8},{12,14},{14,12},{1,3},{3,1},... | collective-permute-start | bytes 1179656 | tf_op jit(solution)/shard_map/ppermute | solution.py:37
  107.6 28.7 %copy-start.2 = (bf16[2,2,8,8,768]{4,3,1,2,0:T(8,128)(2,1)}, bf16[2,2,8,8,768]{4,3,1,2,0:T(8,128)(2,1)S(1)}, u32[]{:S(2)}) copy-start(bf16[2,2,8,8,768]{4,3,1,2,0:T(8,128)(2,1)S(1)} %copy.16) | copy-start | bytes 1179652
  107.6 12.3 %collective-permute-start.25 = (bf16[16,16,768]{2,1,0:T(8,128)(2,1)S(1)}, bf16[16,16,768]{2,1,0:T(8,128)(2,1)S(1)}, u32[]{:S(2)}, u32[]{:S(2)}) collective-permute-start(bf16[16,16,768]{2,1,0:T(8,128)(2,1)S(1)} %bitcast.19), channel_id=1, source_target_pairs={{0,8},{2,10},{8,12},{10,14},{12,4},{14,6},{4,0},{6,2},{1,9},{3,11}... | collective-permute-start | bytes 1179656 | tf_op jit(solution)/shard_map/ppermute | solution.py:32
  111.1 0.8 copy-start.7
  111.8 0.8 copy-start.8
  116.5 25.4 %collective-permute-start.23 = (bf16[4,16,6272]{2,1,0:T(8,128)(2,1)}, bf16[4,16,6272]{2,1,0:T(8,128)(2,1)S(1)}, u32[]{:S(2)}, u32[]{:S(2)}) collective-permute-start(bf16[4,16,6272]{2,1,0:T(8,128)(2,1)} %shard_map.86), channel_id=1, source_target_pairs={{1,0},{0,1},{3,2},{2,3},{5,4},{4,5},{7,6},{6,7},{9,8},{8,9},{11,10... | collective-permute-start | bytes 2408456 | tf_op jit(solution)/shard_map/ppermute | solution.py:19
  119.9 23.4 %copy-start.9 = (bf16[16,16,768]{2,1,0:T(8,128)(2,1)}, bf16[16,16,768]{2,1,0:T(8,128)(2,1)S(1)}, u32[]{:S(2)}) copy-start(bf16[16,16,768]{2,1,0:T(8,128)(2,1)S(1)} %collective-permute-done.25.refs_2_) | copy-start | bytes 1179652
  119.9 11.5 %collective-permute-start.27 = (bf16[16,16,768]{2,1,0:T(8,128)(2,1)S(1)}, bf16[16,16,768]{2,1,0:T(8,128)(2,1)S(1)}, u32[]{:S(2)}, u32[]{:S(2)}) collective-permute-start(bf16[16,16,768]{2,1,0:T(8,128)(2,1)S(1)} %collective-permute-done.25.refs_2_), channel_id=1, source_target_pairs={{0,8},{2,10},{8,12},{10,14},{12,4},{14,6},{4,0},{6,2},{1,9},{3,11}... | collective-permute-start | bytes 1179656 | tf_op jit(solution)/shard_map/ppermute | solution.py:32
  131.4 12.0 %copy-start.10 = (bf16[16,16,768]{2,1,0:T(8,128)(2,1)}, bf16[16,16,768]{2,1,0:T(8,128)(2,1)S(1)}, u32[]{:S(2)}) copy-start(bf16[16,16,768]{2,1,0:T(8,128)(2,1)S(1)} %collective-permute-done.27.refs_4_) | copy-start | bytes 1179652
  131.4 10.6 %collective-permute-start.29 = (bf16[16,16,768]{2,1,0:T(8,128)(2,1)S(1)}, bf16[16,16,768]{2,1,0:T(8,128)(2,1)S(1)}, u32[]{:S(2)}, u32[]{:S(2)}) collective-permute-start(bf16[16,16,768]{2,1,0:T(8,128)(2,1)S(1)} %collective-permute-done.27.refs_4_), channel_id=1, source_target_pairs={{0,8},{2,10},{8,12},{10,14},{12,4},{14,6},{4,0},{6,2},{1,9},{3,11}... | collective-permute-start | bytes 1179656 | tf_op jit(solution)/shard_map/ppermute | solution.py:32
  134.8 18.7 %collective-permute-start.21 = (bf16[4,16,6144]{2,1,0:T(8,128)(2,1)}, bf16[4,16,6144]{2,1,0:T(8,128)(2,1)S(1)}, u32[]{:S(2)}, u32[]{:S(2)}) collective-permute-start(bf16[4,16,6144]{2,1,0:T(8,128)(2,1)} %shard_map.85), channel_id=1, source_target_pairs={{1,0},{0,1},{3,2},{2,3},{5,4},{4,5},{7,6},{6,7},{9,8},{8,9},{11,10... | collective-permute-start | bytes 2359304 | tf_op jit(solution)/shard_map/ppermute | solution.py:19
  136.3 7.1 %collective-permute-start.24 = (bf16[16,16,768]{2,1,0:T(8,128)(2,1)S(1)}, bf16[16,16,768]{2,1,0:T(8,128)(2,1)S(1)}, u32[]{:S(2)}, u32[]{:S(2)}) collective-permute-start(bf16[16,16,768]{2,1,0:T(8,128)(2,1)S(1)} %bitcast.20), channel_id=1, source_target_pairs={{0,2},{2,0},{4,6},{6,4},{8,10},{10,8},{12,14},{14,12},{1,3},{3,1},... | collective-permute-start | bytes 1179656 | tf_op jit(solution)/shard_map/ppermute | solution.py:37
  136.3 7.2 %collective-permute-start.26 = (bf16[16,16,768]{2,1,0:T(8,128)(2,1)S(1)}, bf16[16,16,768]{2,1,0:T(8,128)(2,1)S(1)}, u32[]{:S(2)}, u32[]{:S(2)}) collective-permute-start(bf16[16,16,768]{2,1,0:T(8,128)(2,1)S(1)} %collective-permute-done.25.refs_2_), channel_id=1, source_target_pairs={{0,2},{2,0},{4,6},{6,4},{8,10},{10,8},{12,14},{14,12},{1,3},{3,1},... | collective-permute-start | bytes 1179656 | tf_op jit(solution)/shard_map/ppermute | solution.py:37
  142.0 1.4 copy-start.11
  142.0 1.7 %collective-permute-start.28 = (bf16[16,16,768]{2,1,0:T(8,128)(2,1)S(1)}, bf16[16,16,768]{2,1,0:T(8,128)(2,1)S(1)}, u32[]{:S(2)}, u32[]{:S(2)}) collective-permute-start(bf16[16,16,768]{2,1,0:T(8,128)(2,1)S(1)} %collective-permute-done.27.refs_4_), channel_id=1, source_target_pairs={{0,2},{2,0},{4,6},{6,4},{8,10},{10,8},{12,14},{14,12},{1,3},{3,1},... | collective-permute-start | bytes 1179656 | tf_op jit(solution)/shard_map/ppermute | solution.py:37
  142.0 1.4 copy-start
  142.0 2.3 %collective-permute-start.30 = (bf16[16,16,768]{2,1,0:T(8,128)(2,1)S(1)}, bf16[16,16,768]{2,1,0:T(8,128)(2,1)S(1)}, u32[]{:S(2)}, u32[]{:S(2)}) collective-permute-start(bf16[16,16,768]{2,1,0:T(8,128)(2,1)S(1)} %collective-permute-done.29.refs_6_), channel_id=1, source_target_pairs={{0,2},{2,0},{4,6},{6,4},{8,10},{10,8},{12,14},{14,12},{1,3},{3,1},... | collective-permute-start | bytes 1179656 | tf_op jit(solution)/shard_map/ppermute | solution.py:37
  143.4 0.8 copy-start.12
  143.4 0.9 copy-start.13
  143.7 0.8 copy-start.14
  144.5 0.8 copy-start.15

commit v3 on v2

--- a/solution.py
+++ b/solution.py
@@ -197,10 +197,10 @@
 
 
 def layer_kernel(n, rank, width, me_ref, rows_ref, gain_ref, *refs):
-    pieces, wide_refs, (out_ref, normed_ref) = refs[:n], refs[n:-2], refs[-2:]
-    downs = [p[0] for p in pieces]
-    low = low_of(me_ref, rows_ref, gain_ref, normed_ref, downs, width, rank)
-    add_update(me_ref, out_ref, rows_ref, low, [p[1] for p in pieces], width)
+    downs, ups, wide_refs = refs[:n], refs[n : 2 * n], refs[2 * n : -2]
+    out_ref, normed_ref = refs[-2:]
+    low = low_of(me_ref, rows_ref, gain_ref, normed_ref, [p[...] for p in downs], width, rank)
+    add_update(me_ref, out_ref, rows_ref, low, [p[...] for p in ups], width)
     dim = rows_ref.shape[2]
     for wide_ref in wide_refs:
         for block in range(out_ref.shape[0]):
@@ -277,25 +277,31 @@
     return pl.BlockSpec(shape, lambda b, s: (b + first // shape[0], *zeros))
 
 
-def pair_blocks(size, rank, width, first=0):
-    return pl.BlockSpec((2, size, rank, width), lambda b, s: (0, b + first // size, 0, 0))
+def half_blocks(half, size, rank, width, first=0):
+    return pl.BlockSpec((None, size, rank, width), lambda b, s: (half, b + first // size, 0, 0))
 
 
 def all_gain(dim):
     return pl.BlockSpec((1, dim), lambda b, s: (0, 0))
 
 
-def layer_blocks(me, rows, first, count, gain, other, pieces, skipped, *wide):
-    rank, width = pieces[0].shape[2:]
+def layer_blocks(me, rows, first, count, gain, other, downs, ups, skipped, *wide):
+    rank, width = downs[0].shape[-2:]
     held, dim = rows.shape[1:]
     size = per_step(first, count)
-    pieces = [pieces[0], other] + pieces[1:]
-    specs = [pair_blocks(size, rank, width, skipped)] * len(pieces)
-    specs[1] = pair_blocks(size, rank, width, first)
+    specs, pieces = [], []
+    for half, maps in enumerate((downs, ups)):
+        for at, block in enumerate([maps[0], other] + maps[1:]):
+            offset = first if at == 1 else skipped
+            if block.ndim == 4:
+                specs.append(half_blocks(half, size, rank, width, offset))
+            else:
+                specs.append(blocks_of(size, rank, width, first=offset))
+            pieces.append(block)
     specs += [pl.BlockSpec(low.shape, lambda b, s: (0, 0, 0)) for low in wide]
     out_dim = dim + LANES * len(wide)
     return pl.pallas_call(
-        functools.partial(layer_kernel, len(pieces), rank, width),
+        functools.partial(layer_kernel, len(pieces) // 2, rank, width),
         out_shape=jax.ShapeDtypeStruct((count, held, out_dim), jnp.bfloat16),
         grid_spec=pltpu.PrefetchScalarGridSpec(
             num_scalar_prefetch=1,
@@ -453,37 +459,43 @@
         def __init__(self, block):
             self.held, self.pieces = block, [block]
 
-        def step(self, *after, before_swap=()):
+        def step(self, *after, before_swap=(), split=False):
             k = len(ends)
             after = [*after, *ends[max(k - 2, 0) : max(k - 1, 0)], *swaps[max(k - 3, 0) : max(k - 2, 0)]]
             ends.append(ring_step(tied(self.held, *after) if after else self.held))
+            if split:
+                self.pieces += [ends[-1], [core_swap(half) for half in ends[-1]]]
+                swaps.append(self.pieces[-1][0])
+                return
             swaps.append(core_swap(tied(ends[-1], *before_swap) if before_swap else ends[-1]))
             self.held = ends[-1]
             self.pieces += [ends[-1], swaps[-1]]
 
     first, second = (Gather(block) for block in chunk_maps)
     downs, ups = Gather(raw_down), Gather(ups.reshape(raw, rank, width))
+    (at, end), (middle, last) = chunks[0], (chunks[1][0] + n_blocks // 8, n_blocks)
+    result = None
     first.step()
     first.step(early_sent)
     downs.step()
     first.step()
-    (at, end), (middle, last) = chunks[0], (chunks[1][0] + n_blocks // 8, n_blocks)
-    first_out = layer_blocks(me, rows, at, end - at, norm_gain, other, first.pieces, 0)
+    first_out = layer_blocks(me, rows, at, end - at, norm_gain, other, first.pieces, first.pieces, 0)
     first_sent = passed_along(tied(first_out, early_sent), "section", 1)
+    second.step()
     downs.step()
-    second.step()
     downs.step(first_out)
     low = low_blocks(me, rows, norm_gain, other, downs.pieces)
     second.step(before_swap=[low])
-    second.step()
-    second_out = layer_blocks(me, rows, end, middle - end, norm_gain, other, second.pieces, 0, low)
+    second.step(split=True)
+    maps = second.pieces[:-1] + second.pieces[-1][:1], second.pieces[:-1] + second.pieces[-1][1:]
+    second_out = layer_blocks(me, rows, end, middle - end, norm_gain, other, *maps, 0, low)
     second_sent = passed_along(tied(second_out, carrier_sent), "section", 1)
-    third_out = layer_blocks(me, rows, middle, last - middle, norm_gain, other, second.pieces, middle - end)
+    third_out = layer_blocks(me, rows, middle, last - middle, norm_gain, other, *maps, middle - end)
     third_sent = passed_along(tied(third_out, first_sent), "section", 1)
     ups.step()
+    ups.step(second_out)
     result = place_blocks(first_sent, at, None, rows.shape)
     ups.held, result = lax.optimization_barrier((ups.held, result))
-    ups.step(second_out)
     ups.step(third_out)
 
     maps = [ups.pieces[0], core_swap(ups.pieces[0])] + ups.pieces[1:]

time: 155 us -> 152 us (0.981)
  starting transfers between devices: 42.4 us -> 34.3 us
  waiting for transfers between devices: 59.9 us -> 64.4 us
    ppermute x12, starting transfers between devices: 34.3 us -> 27.5 us  [ring_step(): return lax.ppermute(block, 'expert', route)]
    ppermute x12, waiting for transfers between devices: 59.1 us -> 61.5 us  [ring_step(): return lax.ppermute(block, 'expert', route)]
    ppermute x5, starting transfers between devices: 7.06 us -> 5.16 us  [passed_along(): return lax.ppermute(block, axis, route)]
    unnamed x50 -> x54, local copies, waits for them, and re-layouts: 4.42 us -> 4.67 us
  transfers between devices with their start and end apart: 31 -> 32, of which waited for: 13 -> 16; matrix products, arithmetic and copies ran while one was open for 1% -> 1% of each run, Pallas kernels for 29% -> 29%
where the time goes in v3:
time: 152 us; the launch traced here: 151 us
  waiting for transfers between devices  64.4 us (42%)
  Pallas kernels  45.3 us (30%)
  starting transfers between devices  34.3 us (23%)
  local copies, waits for them, and re-layouts  6.93 us (5%)
    ppermute x12, waiting for transfers between devices, ring_step(): return lax.ppermute(block, 'expert', route)  61.5 us
    ppermute x12, starting transfers between devices, ring_step(): return lax.ppermute(block, 'expert', route)  27.5 us
    pallas_call x1, Pallas kernels, generated(): pl.pallas_call(functools.partial(generator_kernel, chunks, rank), out_sha...  14 us
    pallas_call x3, Pallas kernels, layer_blocks(): pl.pallas_call(functools.partial(layer_kernel, len(pieces) // 2, rank, wi...  13.7 us
    pallas_call x2, Pallas kernels, update_blocks(): pl.pallas_call(functools.partial(update_kernel, n, rank, width, first //...  8.21 us
    pallas_call x1, Pallas kernels, low_blocks(): pl.pallas_call(functools.partial(low_kernel, len(pieces), rank, width), o...  6.49 us
    ppermute x5, starting transfers between devices, passed_along(): return lax.ppermute(block, axis, route)  5.16 us
    unnamed x54, local copies, waits for them, and re-layouts  4.67 us
  transfers between devices with their start and end apart: 32, of which 16 were waited for; matrix products, arithmetic and copies ran while one was open for 1% of the time, Pallas kernels for 29%

profile of v3, /device:TPU:0, one launch (start us, length us, event | category | flops | bytes accessed | tf_op | source)
XLA Modules:
  0.0 151.3 jit_solution(3621910800146587685)
XLA Ops:
  0.0 1.2 slice_bitcast_fusion
  1.2 3.0 %collective-permute-start.3 = (bf16[4,16,6144]{2,1,0:T(8,128)(2,1)S(1)}, bf16[4,16,6144]{2,1,0:T(8,128)(2,1)S(1)}, u32[]{:S(2)}, u32[]{:S(2)}) collective-permute-start(bf16[4,16,6144]{2,1,0:T(8,128)(2,1)S(1)} %slice_bitcast_fusion), channel_id=1, source_target_pairs={{1,0},{0,1},{3,2},{2,3},{5,4},{4,5},{7,6},{6,7},{9,8},{8,9},{11,10... | collective-permute-start | bytes 2359304 | tf_op jit(solution)/shard_map/ppermute | solution.py:19
  4.2 14.0 %shard_map.82 = (bf16[2,32,16,768]{3,2,1,0:T(8,128)(2,1)}, bf16[16,16,768]{2,1,0:T(8,128)(2,1)}, bf16[14,16,6144]{2,1,0:T(8,128)(2,1)}, bf16[2,8,16,768]{3,2,1,0:T(8,128)(2,1)}, bf16[2,8,16,768]{3,2,1,0:T(8,128)(2,1)}) custom-call(s32[32]{0:T(128)} %bitcast.28, s32[8]{0:T(128)} %bitcast.29, bf16[8,256]{1,0:T(8,128)(2,1)} %task_embed_ref.1, ...), custom_call_target="tpu_custom_call" | custom-call | flops 1 | bytes 1 | tf_op jit(solution)/shard_map/pallas_call | solution.py:136
  18.2 2.6 %collective-permute-start.1 = (bf16[2,8,16,768]{3,2,1,0:T(8,128)(2,1)}, bf16[2,8,16,768]{3,2,1,0:T(8,128)(2,1)S(1)}, u32[]{:S(2)}, u32[]{:S(2)}) collective-permute-start(bf16[2,8,16,768]{3,2,1,0:T(8,128)(2,1)} %get-tuple-element.30.refs_0_.refs_8_), channel_id=1, source_target_pairs={{0,8},{2,10},{8,12},{10,14},{12,4},{14,6},{4,0},{6,2},{1,9},{3,11}... | collective-permute-start | bytes 1179656 | tf_op jit(solution)/shard_map/ppermute | solution.py:32
  20.8 0.5 collective-permute-start.23
  21.4 0.0 collective-permute-start
  21.4 7.9 %collective-permute-done.1.refs_2_.refs_10_ = bf16[2,8,16,768]{3,2,1,0:T(8,128)(2,1)S(1)} collective-permute-done((bf16[2,8,16,768]{3,2,1,0:T(8,128)(2,1)}, bf16[2,8,16,768]{3,2,1,0:T(8,128)(2,1)S(1)}, u32[]{:S(2)}, u32[]{:S(2)}) %collective-permute-start.1) | collective-permute-done | bytes 393248 | tf_op jit(solution)/shard_map/ppermute | solution.py:32
  29.3 0.0 collective-permute-done.3.rows_ref
  29.3 3.3 %collective-permute-start.4 = (bf16[2,8,16,768]{3,2,1,0:T(8,128)(2,1)S(1)}, bf16[2,8,16,768]{3,2,1,0:T(8,128)(2,1)S(1)}, u32[]{:S(2)}, u32[]{:S(2)}) collective-permute-start(bf16[2,8,16,768]{3,2,1,0:T(8,128)(2,1)S(1)} %collective-permute-done.1.refs_2_.refs_10_), channel_id=1, source_target_pairs={{0,8},{2,10},{8,12},{10,14},{12,4},{14,6},{4,0},{6,2},{1,9},{3,11}... | collective-permute-start | bytes 1179656 | tf_op jit(solution)/shard_map/ppermute | solution.py:32
  32.6 0.0 collective-permute-start.8
  32.6 0.7 collective-permute-start.2
  33.3 8.9 %collective-permute-done.4.refs_4_.refs_12_ = bf16[2,8,16,768]{3,2,1,0:T(8,128)(2,1)S(1)} collective-permute-done((bf16[2,8,16,768]{3,2,1,0:T(8,128)(2,1)S(1)}, bf16[2,8,16,768]{3,2,1,0:T(8,128)(2,1)S(1)}, u32[]{:S(2)}, u32[]{:S(2)}) %collective-permute-start.4) | collective-permute-done | bytes 393248 | tf_op jit(solution)/shard_map/ppermute | solution.py:32
  42.2 0.0 collective-permute-done.8.refs_3_.refs_11_
  42.2 3.4 %collective-permute-start.9 = (bf16[2,8,16,768]{3,2,1,0:T(8,128)(2,1)S(1)}, bf16[2,8,16,768]{3,2,1,0:T(8,128)(2,1)}, u32[]{:S(2)}, u32[]{:S(2)}) collective-permute-start(bf16[2,8,16,768]{3,2,1,0:T(8,128)(2,1)S(1)} %collective-permute-done.4.refs_4_.refs_12_), channel_id=1, source_target_pairs={{0,8},{2,10},{8,12},{10,14},{12,4},{14,6},{4,0},{6,2},{1,9},{3,11}... | collective-permute-start | bytes 1179656 | tf_op jit(solution)/shard_map/ppermute | solution.py:32
  45.6 4.6 %collective-permute-done.2.refs_2_ = bf16[16,16,768]{2,1,0:T(8,128)(2,1)} collective-permute-done((bf16[16,16,768]{2,1,0:T(8,128)(2,1)}, bf16[16,16,768]{2,1,0:T(8,128)(2,1)}, u32[]{:S(2)}, u32[]{:S(2)}) %collective-permute-start.2) | collective-permute-done | bytes 393248 | tf_op jit(solution)/shard_map/ppermute | solution.py:32
  50.3 0.7 copy-done.18
  51.0 3.4 %collective-permute-start.6 = (bf16[2,8,16,768]{3,2,1,0:T(8,128)(2,1)}, bf16[2,8,16,768]{3,2,1,0:T(8,128)(2,1)S(1)}, u32[]{:S(2)}, u32[]{:S(2)}) collective-permute-start(bf16[2,8,16,768]{3,2,1,0:T(8,128)(2,1)} %get-tuple-element.33.refs_0_.refs_8_), channel_id=1, source_target_pairs={{0,8},{2,10},{8,12},{10,14},{12,4},{14,6},{4,0},{6,2},{1,9},{3,11}... | collective-permute-start | bytes 1179656 | tf_op jit(solution)/shard_map/ppermute | solution.py:32
  54.4 3.6 %collective-permute-done.9.refs_6_.refs_14_ = bf16[2,8,16,768]{3,2,1,0:T(8,128)(2,1)} collective-permute-done((bf16[2,8,16,768]{3,2,1,0:T(8,128)(2,1)S(1)}, bf16[2,8,16,768]{3,2,1,0:T(8,128)(2,1)}, u32[]{:S(2)}, u32[]{:S(2)}) %collective-permute-start.9) | collective-permute-done | bytes 393248 | tf_op jit(solution)/shard_map/ppermute | solution.py:32
  58.0 3.5 %collective-permute-start.11 = (bf16[16,16,768]{2,1,0:T(8,128)(2,1)}, bf16[16,16,768]{2,1,0:T(8,128)(2,1)}, u32[]{:S(2)}, u32[]{:S(2)}) collective-permute-start(bf16[16,16,768]{2,1,0:T(8,128)(2,1)} %collective-permute-done.2.refs_2_), channel_id=1, source_target_pairs={{0,8},{2,10},{8,12},{10,14},{12,4},{14,6},{4,0},{6,2},{1,9},{3,11}... | collective-permute-start | bytes 1179656 | tf_op jit(solution)/shard_map/ppermute | solution.py:32
  61.5 5.0 %collective-permute-done.6.refs_2_.refs_10_ = bf16[2,8,16,768]{3,2,1,0:T(8,128)(2,1)S(1)} collective-permute-done((bf16[2,8,16,768]{3,2,1,0:T(8,128)(2,1)}, bf16[2,8,16,768]{3,2,1,0:T(8,128)(2,1)S(1)}, u32[]{:S(2)}, u32[]{:S(2)}) %collective-permute-start.6) | collective-permute-done | bytes 393248 | tf_op jit(solution)/shard_map/ppermute | solution.py:32
  66.5 0.0 collective-permute-start.7
  66.5 0.0 collective-permute-done.14.refs_7_.refs_15_
  66.6 1.1 copy-done.1
  67.7 5.6 %shard_map.83 = bf16[8,16,6144]{2,1,0:T(8,128)(2,1)} custom-call(s32[1]{0:T(128)} %bitcast.me_ref, bf16[32,16,6144]{2,1,0:T(8,128)(2,1)} %bitcast.19, bf16[1,6144]{1,0:T(2,128)(2,1)} %gain_ref.7, bf16[2,8,16,768]{3,2,1,0:T(8,128)(2,1)} %get-tuple-element.30.refs_0_.refs_8_, bf16[2,32,16,768]{3,2,1,0:T(8,128)(2,1)} %copy-done.1, ...), custom_call_target="tpu_custom_call" | custom-call | flops 1 | bytes 1 | tf_op jit(solution)/shard_map/pallas_call | solution.py:303
  73.3 0.3 collective-permute-done.11.refs_4_
  73.6 3.4 %collective-permute-start.15 = (bf16[16,16,768]{2,1,0:T(8,128)(2,1)}, bf16[16,16,768]{2,1,0:T(8,128)(2,1)S(1)}, u32[]{:S(2)}, u32[]{:S(2)}) collective-permute-start(bf16[16,16,768]{2,1,0:T(8,128)(2,1)} %collective-permute-done.11.refs_4_), channel_id=1, source_target_pairs={{0,8},{2,10},{8,12},{10,14},{12,4},{14,6},{4,0},{6,2},{1,9},{3,11}... | collective-permute-start | bytes 1179656 | tf_op jit(solution)/shard_map/ppermute | solution.py:32
  77.0 0.2 collective-permute-start.12
  77.2 0.5 collective-permute-start.21
  77.7 9.0 %collective-permute-done.15.refs_6_ = bf16[16,16,768]{2,1,0:T(8,128)(2,1)S(1)} collective-permute-done((bf16[16,16,768]{2,1,0:T(8,128)(2,1)}, bf16[16,16,768]{2,1,0:T(8,128)(2,1)S(1)}, u32[]{:S(2)}, u32[]{:S(2)}) %collective-permute-start.15) | collective-permute-done | bytes 393248 | tf_op jit(solution)/shard_map/ppermute | solution.py:32
  86.8 0.0 collective-permute-start.16
  86.8 7.5 %collective-permute-done.12.refs_4_.refs_12_ = bf16[2,8,16,768]{3,2,1,0:T(8,128)(2,1)S(1)} collective-permute-done((bf16[2,8,16,768]{3,2,1,0:T(8,128)(2,1)S(1)}, bf16[2,8,16,768]{3,2,1,0:T(8,128)(2,1)S(1)}, u32[]{:S(2)}, u32[]{:S(2)}) %collective-permute-start.12) | collective-permute-done | bytes 393248 | tf_op jit(solution)/shard_map/ppermute | solution.py:32
  94.2 3.4 %collective-permute-start.18 = (bf16[2,8,16,768]{3,2,1,0:T(8,128)(2,1)S(1)}, bf16[2,8,16,768]{3,2,1,0:T(8,128)(2,1)S(1)}, u32[]{:S(2)}, u32[]{:S(2)}) collective-permute-start(bf16[2,8,16,768]{3,2,1,0:T(8,128)(2,1)S(1)} %collective-permute-done.12.refs_4_.refs_12_), channel_id=1, source_target_pairs={{0,8},{2,10},{8,12},{10,14},{12,4},{14,6},{4,0},{6,2},{1,9},{3,11}... | collective-permute-start | bytes 1179656 | tf_op jit(solution)/shard_map/ppermute | solution.py:32
  97.6 0.7 copy-done.26
  98.4 6.5 %shard_map.84.refs_16_ = bf16[1,16,256]{2,1,0:T(8,128)(2,1)} custom-call(s32[1]{0:T(128)} %bitcast.me_ref, bf16[32,16,6144]{2,1,0:T(8,128)(2,1)} %bitcast.20, bf16[1,6144]{1,0:T(2,128)(2,1)} %gain_ref.7, bf16[16,16,768]{2,1,0:T(8,128)(2,1)} %get-tuple-element.31.refs_0_, bf16[2,32,16,768]{3,2,1,0:T(8,128)(2,1)} %copy-done.1, ...), custom_call_target="tpu_custom_call" | custom-call | flops 1 | bytes 1 | tf_op jit(solution)/shard_map/pallas_call | solution.py:330
  104.9 1.0 slice.12
  106.0 0.1 collective-permute-start.26
  106.1 0.5 collective-permute-start.20
  106.7 0.1 collective-permute-start.19
  106.7 1.0 collective-permute-done.20.refs_15_
  107.7 0.4 collective-permute-done.19.refs_7_
  108.1 0.3 copy-done.19
  108.4 0.7 copy-done.20
  109.1 4.1 %shard_map.86 = bf16[4,16,6272]{2,1,0:T(8,128)(2,1)} custom-call(s32[1]{0:T(128)} %bitcast.me_ref, bf16[32,16,6144]{2,1,0:T(8,128)(2,1)} %bitcast.21, bf16[1,6144]{1,0:T(2,128)(2,1)} %gain_ref.7, bf16[2,8,16,768]{3,2,1,0:T(8,128)(2,1)} %get-tuple-element.33.refs_0_.refs_8_, bf16[2,32,16,768]{3,2,1,0:T(8,128)(2,1)} %copy-done.1, ...), custom_call_target="tpu_custom_call" | custom-call | flops 1 | bytes 1 | tf_op jit(solution)/shard_map/pallas_call | solution.py:303
  113.2 0.6 collective-permute-start.24
  113.7 3.8 %collective-permute-done.26.refs_2_ = bf16[16,16,768]{2,1,0:T(8,128)(2,1)S(1)} collective-permute-done((bf16[16,16,768]{2,1,0:T(8,128)(2,1)S(1)}, bf16[16,16,768]{2,1,0:T(8,128)(2,1)S(1)}, u32[]{:S(2)}, u32[]{:S(2)}) %collective-permute-start.26) | collective-permute-done | bytes 393248 | tf_op jit(solution)/shard_map/ppermute | solution.py:32
  117.5 1.2 collective-permute-start.28
  118.7 4.0 %shard_map.85 = bf16[4,16,6144]{2,1,0:T(8,128)(2,1)} custom-call(s32[1]{0:T(128)} %bitcast.me_ref, bf16[32,16,6144]{2,1,0:T(8,128)(2,1)} %bitcast.22, bf16[1,6144]{1,0:T(2,128)(2,1)} %gain_ref.7, bf16[2,8,16,768]{3,2,1,0:T(8,128)(2,1)} %get-tuple-element.33.refs_0_.refs_8_, bf16[2,32,16,768]{3,2,1,0:T(8,128)(2,1)} %copy-done.1, ...), custom_call_target="tpu_custom_call" | custom-call | flops 1 | bytes 1 | tf_op jit(solution)/shard_map/pallas_call | solution.py:303
  122.8 1.2 shard_map.87.refs_0_
  123.9 4.3 %collective-permute-done.28.refs_4_ = bf16[16,16,768]{2,1,0:T(8,128)(2,1)S(1)} collective-permute-done((bf16[16,16,768]{2,1,0:T(8,128)(2,1)S(1)}, bf16[16,16,768]{2,1,0:T(8,128)(2,1)S(1)}, u32[]{:S(2)}, u32[]{:S(2)}) %collective-permute-start.28) | collective-permute-done | bytes 393248 | tf_op jit(solution)/shard_map/ppermute | solution.py:32
  128.3 2.2 %collective-permute-start.30 = (bf16[16,16,768]{2,1,0:T(8,128)(2,1)S(1)}, bf16[16,16,768]{2,1,0:T(8,128)(2,1)S(1)}, u32[]{:S(2)}, u32[]{:S(2)}) collective-permute-start(bf16[16,16,768]{2,1,0:T(8,128)(2,1)S(1)} %collective-permute-done.28.refs_4_), channel_id=1, source_target_pairs={{0,8},{2,10},{8,12},{10,14},{12,4},{14,6},{4,0},{6,2},{1,9},{3,11}... | collective-permute-start | bytes 1179656 | tf_op jit(solution)/shard_map/ppermute | solution.py:32
  130.5 0.5 collective-permute-start.22
  131.1 0.5 collective-permute-start.27
  131.6 6.5 %collective-permute-done.30.refs_6_ = bf16[16,16,768]{2,1,0:T(8,128)(2,1)S(1)} collective-permute-done((bf16[16,16,768]{2,1,0:T(8,128)(2,1)S(1)}, bf16[16,16,768]{2,1,0:T(8,128)(2,1)S(1)}, u32[]{:S(2)}, u32[]{:S(2)}) %collective-permute-start.30) | collective-permute-done | bytes 393248 | tf_op jit(solution)/shard_map/ppermute | solution.py:32
  138.1 0.5 collective-permute-start.31
  138.6 0.9 shard_map.88.refs_8_
  139.6 0.2 collective-permute-done.29.refs_5_
  139.8 0.6 collective-permute-done.31.refs_7_
  140.4 0.1 copy-done.12
  140.5 0.1 copy-done.13
  140.6 0.8 copy-done.14
  141.4 2.9 %shard_map.89.refs_8_ = bf16[32,16,6144]{2,1,0:T(8,128)(2,1)} custom-call(s32[1]{0:T(128)} %bitcast.me_ref, bf16[4,16,6144]{2,1,0:T(8,128)(2,1)} %copy-done.21, bf16[4,16,6272]{2,1,0:T(8,128)(2,1)} %copy-done, bf16[16,16,768]{2,1,0:T(8,128)(2,1)} %bitcast.25, bf16[16,16,768]{2,1,0:T(8,128)(2,1)} %copy-done.11, ...), custom_call_target="tpu_custom_call", output_to_operand_aliasing={{}: (11, {})} | custom-call | flops 1 | bytes 1 | tf_op jit(solution)/shard_map/pallas_call | solution.py:355
  144.3 5.3 %shard_map.90.refs_0_ = bf16[32,16,6144]{2,1,0:T(8,128)(2,1)} custom-call(s32[1]{0:T(128)} %bitcast.me_ref, bf16[14,16,6144]{2,1,0:T(8,128)(2,1)} %collective-permute-done.23.rows_ref, bf16[4,16,6272]{2,1,0:T(8,128)(2,1)} %copy-done, bf16[16,16,768]{2,1,0:T(8,128)(2,1)} %bitcast.26, ...), custom_call_target="tpu_custom_call", output_to_operand_aliasing={{}: (11, {})} | custom-call | flops 1 | bytes 1 | tf_op jit(solution)/shard_map/pallas_call | solution.py:355
  149.6 0.8 collective-permute-done.22.block_ref
  150.4 0.9 shard_map.91
  (68 shorter events, 0.2 us)
Async XLA Ops:
  1.2 28.1 %collective-permute-start.3 = (bf16[4,16,6144]{2,1,0:T(8,128)(2,1)S(1)}, bf16[4,16,6144]{2,1,0:T(8,128)(2,1)S(1)}, u32[]{:S(2)}, u32[]{:S(2)}) collective-permute-start(bf16[4,16,6144]{2,1,0:T(8,128)(2,1)S(1)} %slice_bitcast_fusion), channel_id=1, source_target_pairs={{1,0},{0,1},{3,2},{2,3},{5,4},{4,5},{7,6},{6,7},{9,8},{8,9},{11,10... | collective-permute-start | bytes 2359304 | tf_op jit(solution)/shard_map/ppermute | solution.py:19
  18.2 11.0 %collective-permute-start.1 = (bf16[2,8,16,768]{3,2,1,0:T(8,128)(2,1)}, bf16[2,8,16,768]{3,2,1,0:T(8,128)(2,1)S(1)}, u32[]{:S(2)}, u32[]{:S(2)}) collective-permute-start(bf16[2,8,16,768]{3,2,1,0:T(8,128)(2,1)} %get-tuple-element.30.refs_0_.refs_8_), channel_id=1, source_target_pairs={{0,8},{2,10},{8,12},{10,14},{12,4},{14,6},{4,0},{6,2},{1,9},{3,11}... | collective-permute-start | bytes 1179656 | tf_op jit(solution)/shard_map/ppermute | solution.py:32
  20.8 84.0 %collective-permute-start.23 = (bf16[14,16,6144]{2,1,0:T(8,128)(2,1)}, bf16[14,16,6144]{2,1,0:T(8,128)(2,1)}, u32[]{:S(2)}, u32[]{:S(2)}) collective-permute-start(bf16[14,16,6144]{2,1,0:T(8,128)(2,1)} %get-tuple-element.42), channel_id=1, source_target_pairs={{1,0},{0,1},{3,2},{2,3},{5,4},{4,5},{7,6},{6,7},{9,8},{8,9},{11,10... | collective-permute-start | bytes 8257544 | tf_op jit(solution)/shard_map/ppermute | solution.py:19
  21.4 45.1 %collective-permute-start = (bf16[2,32,16,768]{3,2,1,0:T(8,128)(2,1)}, bf16[2,32,16,768]{3,2,1,0:T(8,128)(2,1)S(1)}, u32[]{:S(2)}, u32[]{:S(2)}) collective-permute-start(bf16[2,32,16,768]{3,2,1,0:T(8,128)(2,1)} %get-tuple-element.28), channel_id=1, source_target_pairs={{0,2},{2,0},{4,6},{6,4},{8,10},{10,8},{12,14},{14,12},{1,3},{3,1},... | collective-permute-start | bytes 4718600 | tf_op jit(solution)/shard_map/ppermute | solution.py:37
  29.2 37.3 %copy-start.15 = (bf16[2,8,16,768]{3,2,1,0:T(8,128)(2,1)}, bf16[2,8,16,768]{3,2,1,0:T(8,128)(2,1)S(1)}, u32[]{:S(2)}) copy-start(bf16[2,8,16,768]{3,2,1,0:T(8,128)(2,1)S(1)} %collective-permute-done.1.refs_2_.refs_10_) | copy-start | bytes 1179652
  29.3 37.2 %copy-start.21 = (bf16[4,16,6144]{2,1,0:T(8,128)(2,1)}, bf16[4,16,6144]{2,1,0:T(8,128)(2,1)S(1)}, u32[]{:S(2)}) copy-start(bf16[4,16,6144]{2,1,0:T(8,128)(2,1)S(1)} %collective-permute-done.3.rows_ref) | copy-start | bytes 2359300
  29.3 12.9 %collective-permute-start.4 = (bf16[2,8,16,768]{3,2,1,0:T(8,128)(2,1)S(1)}, bf16[2,8,16,768]{3,2,1,0:T(8,128)(2,1)S(1)}, u32[]{:S(2)}, u32[]{:S(2)}) collective-permute-start(bf16[2,8,16,768]{3,2,1,0:T(8,128)(2,1)S(1)} %collective-permute-done.1.refs_2_.refs_10_), channel_id=1, source_target_pairs={{0,8},{2,10},{8,12},{10,14},{12,4},{14,6},{4,0},{6,2},{1,9},{3,11}... | collective-permute-start | bytes 1179656 | tf_op jit(solution)/shard_map/ppermute | solution.py:32
  32.6 9.6 %collective-permute-start.8 = (bf16[2,8,16,768]{3,2,1,0:T(8,128)(2,1)S(1)}, bf16[2,8,16,768]{3,2,1,0:T(8,128)(2,1)S(1)}, u32[]{:S(2)}, u32[]{:S(2)}) collective-permute-start(bf16[2,8,16,768]{3,2,1,0:T(8,128)(2,1)S(1)} %collective-permute-done.1.refs_2_.refs_10_), channel_id=1, source_target_pairs={{0,2},{2,0},{4,6},{6,4},{8,10},{10,8},{12,14},{14,12},{1,3},{3,1},... | collective-permute-start | bytes 1179656 | tf_op jit(solution)/shard_map/ppermute | solution.py:37
  32.6 17.7 %collective-permute-start.2 = (bf16[16,16,768]{2,1,0:T(8,128)(2,1)}, bf16[16,16,768]{2,1,0:T(8,128)(2,1)}, u32[]{:S(2)}, u32[]{:S(2)}) collective-permute-start(bf16[16,16,768]{2,1,0:T(8,128)(2,1)} %get-tuple-element.31.refs_0_), channel_id=1, source_target_pairs={{0,8},{2,10},{8,12},{10,14},{12,4},{14,6},{4,0},{6,2},{1,9},{3,11}... | collective-permute-start | bytes 1179656 | tf_op jit(solution)/shard_map/ppermute | solution.py:32
  42.1 24.4 %copy-start.16 = (bf16[2,8,16,768]{3,2,1,0:T(8,128)(2,1)}, bf16[2,8,16,768]{3,2,1,0:T(8,128)(2,1)S(1)}, u32[]{:S(2)}) copy-start(bf16[2,8,16,768]{3,2,1,0:T(8,128)(2,1)S(1)} %collective-permute-done.4.refs_4_.refs_12_) | copy-start | bytes 1179652
  42.2 8.1 %collective-permute-start.5 = (bf16[2,8,16,768]{3,2,1,0:T(8,128)(2,1)S(1)}, bf16[2,8,16,768]{3,2,1,0:T(8,128)(2,1)S(1)}, u32[]{:S(2)}, u32[]{:S(2)}) collective-permute-start(bf16[2,8,16,768]{3,2,1,0:T(8,128)(2,1)S(1)} %collective-permute-done.4.refs_4_.refs_12_), channel_id=1, source_target_pairs={{0,2},{2,0},{4,6},{6,4},{8,10},{10,8},{12,14},{14,12},{1,3},{3,1},... | collective-permute-start | bytes 1179656 | tf_op jit(solution)/shard_map/ppermute | solution.py:37
  42.2 24.4 %copy-start.17 = (bf16[2,8,16,768]{3,2,1,0:T(8,128)(2,1)}, bf16[2,8,16,768]{3,2,1,0:T(8,128)(2,1)S(1)}, u32[]{:S(2)}) copy-start(bf16[2,8,16,768]{3,2,1,0:T(8,128)(2,1)S(1)} %collective-permute-done.8.refs_3_.refs_11_) | copy-start | bytes 1179652
  42.2 15.8 %collective-permute-start.9 = (bf16[2,8,16,768]{3,2,1,0:T(8,128)(2,1)S(1)}, bf16[2,8,16,768]{3,2,1,0:T(8,128)(2,1)}, u32[]{:S(2)}, u32[]{:S(2)}) collective-permute-start(bf16[2,8,16,768]{3,2,1,0:T(8,128)(2,1)S(1)} %collective-permute-done.4.refs_4_.refs_12_), channel_id=1, source_target_pairs={{0,8},{2,10},{8,12},{10,14},{12,4},{14,6},{4,0},{6,2},{1,9},{3,11}... | collective-permute-start | bytes 1179656 | tf_op jit(solution)/shard_map/ppermute | solution.py:32
  50.3 7.7 %collective-permute-start.10 = (bf16[16,16,768]{2,1,0:T(8,128)(2,1)}, bf16[16,16,768]{2,1,0:T(8,128)(2,1)S(1)}, u32[]{:S(2)}, u32[]{:S(2)}) collective-permute-start(bf16[16,16,768]{2,1,0:T(8,128)(2,1)} %collective-permute-done.2.refs_2_), channel_id=1, source_target_pairs={{0,2},{2,0},{4,6},{6,4},{8,10},{10,8},{12,14},{14,12},{1,3},{3,1},... | collective-permute-start | bytes 1179656 | tf_op jit(solution)/shard_map/ppermute | solution.py:37
  50.3 0.8 copy-start.18
  51.0 15.5 %collective-permute-start.6 = (bf16[2,8,16,768]{3,2,1,0:T(8,128)(2,1)}, bf16[2,8,16,768]{3,2,1,0:T(8,128)(2,1)S(1)}, u32[]{:S(2)}, u32[]{:S(2)}) collective-permute-start(bf16[2,8,16,768]{3,2,1,0:T(8,128)(2,1)} %get-tuple-element.33.refs_0_.refs_8_), channel_id=1, source_target_pairs={{0,8},{2,10},{8,12},{10,14},{12,4},{14,6},{4,0},{6,2},{1,9},{3,11}... | collective-permute-start | bytes 1179656 | tf_op jit(solution)/shard_map/ppermute | solution.py:32
  57.9 8.6 %collective-permute-start.14 = (bf16[2,8,16,768]{3,2,1,0:T(8,128)(2,1)}, bf16[2,8,16,768]{3,2,1,0:T(8,128)(2,1)}, u32[]{:S(2)}, u32[]{:S(2)}) collective-permute-start(bf16[2,8,16,768]{3,2,1,0:T(8,128)(2,1)} %collective-permute-done.9.refs_6_.refs_14_), channel_id=1, source_target_pairs={{0,2},{2,0},{4,6},{6,4},{8,10},{10,8},{12,14},{14,12},{1,3},{3,1},... | collective-permute-start | bytes 1179656 | tf_op jit(solution)/shard_map/ppermute | solution.py:37
  58.0 8.5 %copy-start.23 = (bf16[16,16,768]{2,1,0:T(8,128)(2,1)}, bf16[16,16,768]{2,1,0:T(8,128)(2,1)S(1)}, u32[]{:S(2)}) copy-start(bf16[16,16,768]{2,1,0:T(8,128)(2,1)S(1)} %collective-permute-done.10.refs_3_) | copy-start | bytes 1179652
  58.0 15.6 %collective-permute-start.11 = (bf16[16,16,768]{2,1,0:T(8,128)(2,1)}, bf16[16,16,768]{2,1,0:T(8,128)(2,1)}, u32[]{:S(2)}, u32[]{:S(2)}) collective-permute-start(bf16[16,16,768]{2,1,0:T(8,128)(2,1)} %collective-permute-done.2.refs_2_), channel_id=1, source_target_pairs={{0,8},{2,10},{8,12},{10,14},{12,4},{14,6},{4,0},{6,2},{1,9},{3,11}... | collective-permute-start | bytes 1179656 | tf_op jit(solution)/shard_map/ppermute | solution.py:32
  66.5 41.6 %copy-start.3 = (bf16[2,8,16,768]{3,2,1,0:T(8,128)(2,1)}, bf16[2,8,16,768]{3,2,1,0:T(8,128)(2,1)S(1)}, u32[]{:S(2)}) copy-start(bf16[2,8,16,768]{3,2,1,0:T(8,128)(2,1)S(1)} %collective-permute-done.6.refs_2_.refs_10_) | copy-start | bytes 1179652
  66.5 10.5 %collective-permute-start.7 = (bf16[2,8,16,768]{3,2,1,0:T(8,128)(2,1)S(1)}, bf16[2,8,16,768]{3,2,1,0:T(8,128)(2,1)S(1)}, u32[]{:S(2)}, u32[]{:S(2)}) collective-permute-start(bf16[2,8,16,768]{3,2,1,0:T(8,128)(2,1)S(1)} %collective-permute-done.6.refs_2_.refs_10_), channel_id=1, source_target_pairs={{0,2},{2,0},{4,6},{6,4},{8,10},{10,8},{12,14},{14,12},{1,3},{3,1},... | collective-permute-start | bytes 1179656 | tf_op jit(solution)/shard_map/ppermute | solution.py:37
  66.5 1.2 copy-start.1
  73.6 13.2 %collective-permute-start.15 = (bf16[16,16,768]{2,1,0:T(8,128)(2,1)}, bf16[16,16,768]{2,1,0:T(8,128)(2,1)S(1)}, u32[]{:S(2)}, u32[]{:S(2)}) collective-permute-start(bf16[16,16,768]{2,1,0:T(8,128)(2,1)} %collective-permute-done.11.refs_4_), channel_id=1, source_target_pairs={{0,8},{2,10},{8,12},{10,14},{12,4},{14,6},{4,0},{6,2},{1,9},{3,11}... | collective-permute-start | bytes 1179656 | tf_op jit(solution)/shard_map/ppermute | solution.py:32
  77.0 9.8 %collective-permute-start.13 = (bf16[16,16,768]{2,1,0:T(8,128)(2,1)}, bf16[16,16,768]{2,1,0:T(8,128)(2,1)S(1)}, u32[]{:S(2)}, u32[]{:S(2)}) collective-permute-start(bf16[16,16,768]{2,1,0:T(8,128)(2,1)} %collective-permute-done.11.refs_4_), channel_id=1, source_target_pairs={{0,2},{2,0},{4,6},{6,4},{8,10},{10,8},{12,14},{14,12},{1,3},{3,1},... | collective-permute-start | bytes 1179656 | tf_op jit(solution)/shard_map/ppermute | solution.py:37
  77.0 29.1 %copy-start.4 = (bf16[2,8,16,768]{3,2,1,0:T(8,128)(2,1)}, bf16[2,8,16,768]{3,2,1,0:T(8,128)(2,1)S(1)}, u32[]{:S(2)}) copy-start(bf16[2,8,16,768]{3,2,1,0:T(8,128)(2,1)S(1)} %collective-permute-done.7.refs_3_.refs_11_) | copy-start | bytes 1179652
  77.0 17.3 %collective-permute-start.12 = (bf16[2,8,16,768]{3,2,1,0:T(8,128)(2,1)S(1)}, bf16[2,8,16,768]{3,2,1,0:T(8,128)(2,1)S(1)}, u32[]{:S(2)}, u32[]{:S(2)}) collective-permute-start(bf16[2,8,16,768]{3,2,1,0:T(8,128)(2,1)S(1)} %collective-permute-done.6.refs_2_.refs_10_), channel_id=1, source_target_pairs={{0,8},{2,10},{8,12},{10,14},{12,4},{14,6},{4,0},{6,2},{1,9},{3,11}... | collective-permute-start | bytes 1179656 | tf_op jit(solution)/shard_map/ppermute | solution.py:32
  77.2 45.6 %collective-permute-start.21 = (bf16[8,16,6144]{2,1,0:T(8,128)(2,1)}, bf16[8,16,6144]{2,1,0:T(8,128)(2,1)S(1)}, u32[]{:S(2)}, u32[]{:S(2)}) collective-permute-start(bf16[8,16,6144]{2,1,0:T(8,128)(2,1)} %shard_map.83), channel_id=1, source_target_pairs={{1,0},{0,1},{3,2},{2,3},{5,4},{4,5},{7,6},{6,7},{9,8},{8,9},{11,10... | collective-permute-start | bytes 4718600 | tf_op jit(solution)/shard_map/ppermute | solution.py:19
  86.8 10.9 %copy-start.24 = (bf16[16,16,768]{2,1,0:T(8,128)(2,1)}, bf16[16,16,768]{2,1,0:T(8,128)(2,1)S(1)}, u32[]{:S(2)}) copy-start(bf16[16,16,768]{2,1,0:T(8,128)(2,1)S(1)} %collective-permute-done.15.refs_6_) | copy-start | bytes 1179652
  86.8 10.9 %collective-permute-start.16 = (bf16[16,16,768]{2,1,0:T(8,128)(2,1)S(1)}, bf16[16,16,768]{2,1,0:T(8,128)(2,1)S(1)}, u32[]{:S(2)}, u32[]{:S(2)}) collective-permute-start(bf16[16,16,768]{2,1,0:T(8,128)(2,1)S(1)} %collective-permute-done.15.refs_6_), channel_id=1, source_target_pairs={{0,2},{2,0},{4,6},{6,4},{8,10},{10,8},{12,14},{14,12},{1,3},{3,1},... | collective-permute-start | bytes 1179656 | tf_op jit(solution)/shard_map/ppermute | solution.py:37
  86.8 10.9 %copy-start.25 = (bf16[16,16,768]{2,1,0:T(8,128)(2,1)}, bf16[16,16,768]{2,1,0:T(8,128)(2,1)S(1)}, u32[]{:S(2)}) copy-start(bf16[16,16,768]{2,1,0:T(8,128)(2,1)S(1)} %collective-permute-done.13.refs_5_) | copy-start | bytes 1179652
  94.2 11.9 %copy-start.5 = (bf16[2,8,16,768]{3,2,1,0:T(8,128)(2,1)}, bf16[2,8,16,768]{3,2,1,0:T(8,128)(2,1)S(1)}, u32[]{:S(2)}) copy-start(bf16[2,8,16,768]{3,2,1,0:T(8,128)(2,1)S(1)} %collective-permute-done.12.refs_4_.refs_12_) | copy-start | bytes 1179652
  94.2 11.8 %collective-permute-start.18 = (bf16[2,8,16,768]{3,2,1,0:T(8,128)(2,1)S(1)}, bf16[2,8,16,768]{3,2,1,0:T(8,128)(2,1)S(1)}, u32[]{:S(2)}, u32[]{:S(2)}) collective-permute-start(bf16[2,8,16,768]{3,2,1,0:T(8,128)(2,1)S(1)} %collective-permute-done.12.refs_4_.refs_12_), channel_id=1, source_target_pairs={{0,8},{2,10},{8,12},{10,14},{12,4},{14,6},{4,0},{6,2},{1,9},{3,11}... | collective-permute-start | bytes 1179656 | tf_op jit(solution)/shard_map/ppermute | solution.py:32
  97.6 0.7 copy-start.26
  104.9 1.9 %collective-permute-start.17 = (bf16[2,8,16,768]{3,2,1,0:T(8,128)(2,1)S(1)}, bf16[2,8,16,768]{3,2,1,0:T(8,128)(2,1)S(1)}, u32[]{:S(2)}, u32[]{:S(2)}) collective-permute-start(bf16[2,8,16,768]{3,2,1,0:T(8,128)(2,1)S(1)} %collective-permute-done.12.refs_4_.refs_12_), channel_id=1, source_target_pairs={{0,2},{2,0},{4,6},{6,4},{8,10},{10,8},{12,14},{14,12},{1,3},{3,1},... | collective-permute-start | bytes 1179656 | tf_op jit(solution)/shard_map/ppermute | solution.py:37
  105.9 25.1 %copy-start.7 = (bf16[2,2,8,8,768]{4,3,1,2,0:T(8,128)(2,1)}, bf16[2,2,8,8,768]{4,3,1,2,0:T(8,128)(2,1)S(1)}, u32[]{:S(2)}) copy-start(bf16[2,2,8,8,768]{4,3,1,2,0:T(8,128)(2,1)S(1)} %copy.16) | copy-start | bytes 1179652
  106.0 11.6 %collective-permute-start.26 = (bf16[16,16,768]{2,1,0:T(8,128)(2,1)S(1)}, bf16[16,16,768]{2,1,0:T(8,128)(2,1)S(1)}, u32[]{:S(2)}, u32[]{:S(2)}) collective-permute-start(bf16[16,16,768]{2,1,0:T(8,128)(2,1)S(1)} %bitcast.23), channel_id=1, source_target_pairs={{0,8},{2,10},{8,12},{10,14},{12,4},{14,6},{4,0},{6,2},{1,9},{3,11}... | collective-permute-start | bytes 1179656 | tf_op jit(solution)/shard_map/ppermute | solution.py:32
  106.1 2.0 %copy-start.2 = (bf16[2,8,16,768]{3,2,1,0:T(8,128)(2,1)}, bf16[2,8,16,768]{3,2,1,0:T(8,128)(2,1)S(1)}, u32[]{:S(2)}) copy-start(bf16[2,8,16,768]{3,2,1,0:T(8,128)(2,1)S(1)} %collective-permute-done.18.refs_6_.refs_14_) | copy-start | bytes 1179652
  106.1 1.6 %collective-permute-start.20 = (bf16[8,16,768]{2,1,0:T(8,128)(2,1)S(1)}, bf16[8,16,768]{2,1,0:T(8,128)(2,1)S(1)}, u32[]{:S(2)}, u32[]{:S(2)}) collective-permute-start(bf16[8,16,768]{2,1,0:T(8,128)(2,1)S(1)} %get-tuple-element.49), channel_id=1, source_target_pairs={{0,2},{2,0},{4,6},{6,4},{8,10},{10,8},{12,14},{14,12},{1,3},{3,1},... | collective-permute-start | bytes 589832 | tf_op jit(solution)/shard_map/ppermute | solution.py:37
  106.7 1.4 collective-permute-start.19
  106.7 1.4 copy-start.6
  107.7 0.7 copy-start.19
  108.4 0.7 copy-start.20
  113.2 25.0 %collective-permute-start.24 = (bf16[4,16,6272]{2,1,0:T(8,128)(2,1)}, bf16[4,16,6272]{2,1,0:T(8,128)(2,1)S(1)}, u32[]{:S(2)}, u32[]{:S(2)}) collective-permute-start(bf16[4,16,6272]{2,1,0:T(8,128)(2,1)} %shard_map.86), channel_id=1, source_target_pairs={{1,0},{0,1},{3,2},{2,3},{5,4},{4,5},{7,6},{6,7},{9,8},{8,9},{11,10... | collective-permute-start | bytes 2408456 | tf_op jit(solution)/shard_map/ppermute | solution.py:19
  117.5 13.5 %copy-start.8 = (bf16[16,16,768]{2,1,0:T(8,128)(2,1)}, bf16[16,16,768]{2,1,0:T(8,128)(2,1)S(1)}, u32[]{:S(2)}) copy-start(bf16[16,16,768]{2,1,0:T(8,128)(2,1)S(1)} %collective-permute-done.26.refs_2_) | copy-start | bytes 1179652
  117.5 10.7 %collective-permute-start.28 = (bf16[16,16,768]{2,1,0:T(8,128)(2,1)S(1)}, bf16[16,16,768]{2,1,0:T(8,128)(2,1)S(1)}, u32[]{:S(2)}, u32[]{:S(2)}) collective-permute-start(bf16[16,16,768]{2,1,0:T(8,128)(2,1)S(1)} %collective-permute-done.26.refs_2_), channel_id=1, source_target_pairs={{0,8},{2,10},{8,12},{10,14},{12,4},{14,6},{4,0},{6,2},{1,9},{3,11}... | collective-permute-start | bytes 1179656 | tf_op jit(solution)/shard_map/ppermute | solution.py:32
  122.8 7.8 %copy-start.22 = (bf16[4,16,6144]{2,1,0:T(8,128)(2,1)S(1)}, bf16[4,16,6144]{2,1,0:T(8,128)(2,1)}, u32[]{:S(2)}) copy-start(bf16[4,16,6144]{2,1,0:T(8,128)(2,1)} %shard_map.85) | copy-start | bytes 2359300
  128.3 11.3 %copy-start.9 = (bf16[16,16,768]{2,1,0:T(8,128)(2,1)}, bf16[16,16,768]{2,1,0:T(8,128)(2,1)S(1)}, u32[]{:S(2)}) copy-start(bf16[16,16,768]{2,1,0:T(8,128)(2,1)S(1)} %collective-permute-done.28.refs_4_) | copy-start | bytes 1179652
  128.3 9.8 %collective-permute-start.30 = (bf16[16,16,768]{2,1,0:T(8,128)(2,1)S(1)}, bf16[16,16,768]{2,1,0:T(8,128)(2,1)S(1)}, u32[]{:S(2)}, u32[]{:S(2)}) collective-permute-start(bf16[16,16,768]{2,1,0:T(8,128)(2,1)S(1)} %collective-permute-done.28.refs_4_), channel_id=1, source_target_pairs={{0,8},{2,10},{8,12},{10,14},{12,4},{14,6},{4,0},{6,2},{1,9},{3,11}... | collective-permute-start | bytes 1179656 | tf_op jit(solution)/shard_map/ppermute | solution.py:32
  130.5 19.9 %collective-permute-start.22 = (bf16[4,16,6144]{2,1,0:T(8,128)(2,1)S(1)}, bf16[4,16,6144]{2,1,0:T(8,128)(2,1)S(1)}, u32[]{:S(2)}, u32[]{:S(2)}) collective-permute-start(bf16[4,16,6144]{2,1,0:T(8,128)(2,1)S(1)} %copy-done.22), channel_id=1, source_target_pairs={{1,0},{0,1},{3,2},{2,3},{5,4},{4,5},{7,6},{6,7},{9,8},{8,9},{11,10... | collective-permute-start | bytes 2359304 | tf_op jit(solution)/shard_map/ppermute | solution.py:19
  131.1 8.5 %collective-permute-start.25 = (bf16[16,16,768]{2,1,0:T(8,128)(2,1)S(1)}, bf16[16,16,768]{2,1,0:T(8,128)(2,1)S(1)}, u32[]{:S(2)}, u32[]{:S(2)}) collective-permute-start(bf16[16,16,768]{2,1,0:T(8,128)(2,1)S(1)} %bitcast.24), channel_id=1, source_target_pairs={{0,2},{2,0},{4,6},{6,4},{8,10},{10,8},{12,14},{14,12},{1,3},{3,1},... | collective-permute-start | bytes 1179656 | tf_op jit(solution)/shard_map/ppermute | solution.py:37
  131.1 8.5 %collective-permute-start.27 = (bf16[16,16,768]{2,1,0:T(8,128)(2,1)S(1)}, bf16[16,16,768]{2,1,0:T(8,128)(2,1)S(1)}, u32[]{:S(2)}, u32[]{:S(2)}) collective-permute-start(bf16[16,16,768]{2,1,0:T(8,128)(2,1)S(1)} %collective-permute-done.26.refs_2_), channel_id=1, source_target_pairs={{0,2},{2,0},{4,6},{6,4},{8,10},{10,8},{12,14},{14,12},{1,3},{3,1},... | collective-permute-start | bytes 1179656 | tf_op jit(solution)/shard_map/ppermute | solution.py:37
  138.1 1.4 copy-start.10
  138.1 1.7 %collective-permute-start.29 = (bf16[16,16,768]{2,1,0:T(8,128)(2,1)S(1)}, bf16[16,16,768]{2,1,0:T(8,128)(2,1)S(1)}, u32[]{:S(2)}, u32[]{:S(2)}) collective-permute-start(bf16[16,16,768]{2,1,0:T(8,128)(2,1)S(1)} %collective-permute-done.28.refs_4_), channel_id=1, source_target_pairs={{0,2},{2,0},{4,6},{6,4},{8,10},{10,8},{12,14},{14,12},{1,3},{3,1},... | collective-permute-start | bytes 1179656 | tf_op jit(solution)/shard_map/ppermute | solution.py:37
  138.1 1.4 copy-start
  138.1 2.3 %collective-permute-start.31 = (bf16[16,16,768]{2,1,0:T(8,128)(2,1)S(1)}, bf16[16,16,768]{2,1,0:T(8,128)(2,1)S(1)}, u32[]{:S(2)}, u32[]{:S(2)}) collective-permute-start(bf16[16,16,768]{2,1,0:T(8,128)(2,1)S(1)} %collective-permute-done.30.refs_6_), channel_id=1, source_target_pairs={{0,2},{2,0},{4,6},{6,4},{8,10},{10,8},{12,14},{14,12},{1,3},{3,1},... | collective-permute-start | bytes 1179656 | tf_op jit(solution)/shard_map/ppermute | solution.py:37
  139.6 0.8 copy-start.11
  139.6 0.9 copy-start.12
  139.8 0.8 copy-start.13
  140.6 0.8 copy-start.14

commit v4 on v3

--- a/solution.py
+++ b/solution.py
@@ -238,15 +238,25 @@
         out_ref[0] = wide_ref[...].astype(out_ref.dtype)
 
 
-def update_kernel(n, rank, width, first_step, me_ref, rows_ref, wide_ref, *refs):
+def update_kernel(n, rank, me_ref, carrier_ref, early_ref, wide_ref, *refs):
     pieces, out_ref = refs[:n], refs[-1]
-    count, held, _ = rows_ref.shape
+    count, held, _ = early_ref.shape
+    step, last = pl.program_id(0), pl.num_programs(0) - 1
+    width = pieces[0].shape[2]
     wide = jnp.concatenate([wide_ref[i] for i in range(wide_ref.shape[0])], axis=1)
-    places = block_columns(pl.program_id(0) + first_step, count * rank, wide.shape[1])
+    places = block_columns(step, count * rank, wide.shape[1])
     folded = dot(wide, places, 1).astype(jnp.bfloat16)
     row, column = rows_and_columns((count * held, held))
     low = own_blocks(dot(zero_one(row % held == column), folded).astype(jnp.bfloat16), rank)
-    add_update(me_ref, out_ref, rows_ref, low, [p[...] for p in pieces], width)
+    maps = [p[...] for p in pieces]
+
+    @pl.when(step < last)
+    def _():
+        add_update(me_ref, out_ref, carrier_ref, low, maps, width)
+
+    @pl.when(step == last)
+    def _():
+        add_update(me_ref, out_ref, early_ref, low, maps, width)
 
 
 def place_kernel(first, count, block_ref, *refs):
@@ -345,28 +355,32 @@
     )(me, rows, gain, *pieces)
 
 
-def update_blocks(me, rows, count, with_low, pieces, first, result):
+def update_blocks(me, carrier, early, with_low, pieces, result):
     n, (raw, rank, width) = len(pieces), pieces[0].shape
-    held, dim = rows.shape[1:]
-    size = per_step(first, count) if first else per_step(count, count // 2)
+    size, held, dim = early.shape
+    steps = raw // size
     low_spec = pl.BlockSpec(
         (low_lanes(raw, rank) // LANES, held, LANES), lambda b, s: (0, 0, dim // LANES)
     )
     return pl.pallas_call(
-        functools.partial(update_kernel, n, rank, width, first // size),
+        functools.partial(update_kernel, n, rank),
         out_shape=jax.ShapeDtypeStruct(result.shape, result.dtype),
         grid_spec=pltpu.PrefetchScalarGridSpec(
             num_scalar_prefetch=1,
-            grid=(count // size,),
-            in_specs=[blocks_of(size, held, dim), low_spec]
-            + [blocks_of(size, rank, width, first=first)] * n
+            grid=(steps,),
+            in_specs=[
+                pl.BlockSpec((size, held, dim), lambda b, s: (jnp.minimum(b, steps - 2), 0, 0)),
+                pl.BlockSpec((size, held, dim), lambda b, s: (0, 0, 0)),
+                low_spec,
+            ]
+            + [blocks_of(size, rank, width)] * n
             + [pl.BlockSpec(memory_space=pl.ANY)],
-            out_specs=blocks_of(size, held, dim, first=first),
+            out_specs=blocks_of(size, held, dim),
         ),
-        input_output_aliases={3 + n: 0},
+        input_output_aliases={4 + n: 0},
         compiler_params=params(),
         cost_estimate=tiny_cost(),
-    )(me, rows, with_low, *pieces, result)
+    )(me, carrier, early, with_low, *pieces, result)
 
 
 def place_blocks(block, first, result, shape):
@@ -500,8 +514,7 @@
 
     maps = [ups.pieces[0], core_swap(ups.pieces[0])] + ups.pieces[1:]
     result = place_blocks(second_sent, end, result, rows.shape)
-    result = update_blocks(me, early_sent, early, second_sent, maps, carried, result)
-    result = update_blocks(me, carrier_sent, carried, second_sent, maps, 0, result)
+    result = update_blocks(me, carrier_sent, early_sent, second_sent, maps, result)
     return place_blocks(third_sent, middle, result, rows.shape)[None]
 
 

time: 152 us -> 152 us (level)
  Pallas kernels: 45.3 us -> 43.3 us
  waiting for transfers between devices: 64.4 us -> 66.4 us
    ppermute x5, waiting for transfers between devices: 0.8 us -> 2.77 us  [passed_along(): return lax.ppermute(block, axis, route)]
    pallas_call x2 -> x1, Pallas kernels: 8.21 us -> 6.24 us  [update_blocks(): pl.pallas_call(functools.partial(update_kernel, n, rank), out_shape=jax.S...]
  transfers between devices with their start and end apart: 32 -> 32, of which waited for: 16 -> 16; matrix products, arithmetic and copies ran while one was open for 1% -> 1% of each run, Pallas kernels for 29% -> 28%
where the time goes in v4:
time: 152 us; the launch traced here: 151 us
  waiting for transfers between devices  66.4 us (44%)
  Pallas kernels  43.3 us (28%)
  starting transfers between devices  34.3 us (23%)
  local copies, waits for them, and re-layouts  6.93 us (5%)
    ppermute x12, waiting for transfers between devices, ring_step(): return lax.ppermute(block, 'expert', route)  61.5 us
    ppermute x12, starting transfers between devices, ring_step(): return lax.ppermute(block, 'expert', route)  27.5 us
    pallas_call x1, Pallas kernels, generated(): pl.pallas_call(functools.partial(generator_kernel, chunks, rank), out_sha...  14 us
    pallas_call x3, Pallas kernels, layer_blocks(): pl.pallas_call(functools.partial(layer_kernel, len(pieces) // 2, rank, wi...  13.7 us
    pallas_call x1, Pallas kernels, low_blocks(): pl.pallas_call(functools.partial(low_kernel, len(pieces), rank, width), o...  6.49 us
    pallas_call x1, Pallas kernels, update_blocks(): pl.pallas_call(functools.partial(update_kernel, n, rank), out_shape=jax.S...  6.24 us
    ppermute x5, starting transfers between devices, passed_along(): return lax.ppermute(block, axis, route)  5.16 us
    unnamed x54, local copies, waits for them, and re-layouts  4.67 us
  transfers between devices with their start and end apart: 32, of which 16 were waited for; matrix products, arithmetic and copies ran while one was open for 1% of the time, Pallas kernels for 28%

profile of v4, /device:TPU:0, one launch (start us, length us, event | category | flops | bytes accessed | tf_op | source)
XLA Modules:
  0.0 151.3 jit_solution(16380956854632946188)
XLA Ops:
  0.0 1.2 slice_bitcast_fusion
  1.2 3.0 %collective-permute-start.3 = (bf16[4,16,6144]{2,1,0:T(8,128)(2,1)S(1)}, bf16[4,16,6144]{2,1,0:T(8,128)(2,1)S(1)}, u32[]{:S(2)}, u32[]{:S(2)}) collective-permute-start(bf16[4,16,6144]{2,1,0:T(8,128)(2,1)S(1)} %slice_bitcast_fusion), channel_id=1, source_target_pairs={{1,0},{0,1},{3,2},{2,3},{5,4},{4,5},{7,6},{6,7},{9,8},{8,9},{11,10... | collective-permute-start | bytes 2359304 | tf_op jit(solution)/shard_map/ppermute | solution.py:19
  4.2 14.0 %shard_map.82 = (bf16[2,32,16,768]{3,2,1,0:T(8,128)(2,1)}, bf16[16,16,768]{2,1,0:T(8,128)(2,1)}, bf16[14,16,6144]{2,1,0:T(8,128)(2,1)}, bf16[2,8,16,768]{3,2,1,0:T(8,128)(2,1)}, bf16[2,8,16,768]{3,2,1,0:T(8,128)(2,1)}) custom-call(s32[32]{0:T(128)} %bitcast.27, s32[8]{0:T(128)} %bitcast.28, bf16[8,256]{1,0:T(8,128)(2,1)} %task_embed_ref.1, ...), custom_call_target="tpu_custom_call" | custom-call | flops 1 | bytes 1 | tf_op jit(solution)/shard_map/pallas_call | solution.py:136
  18.2 2.6 %collective-permute-start.1 = (bf16[2,8,16,768]{3,2,1,0:T(8,128)(2,1)}, bf16[2,8,16,768]{3,2,1,0:T(8,128)(2,1)S(1)}, u32[]{:S(2)}, u32[]{:S(2)}) collective-permute-start(bf16[2,8,16,768]{3,2,1,0:T(8,128)(2,1)} %get-tuple-element.30.refs_0_.refs_8_), channel_id=1, source_target_pairs={{0,8},{2,10},{8,12},{10,14},{12,4},{14,6},{4,0},{6,2},{1,9},{3,11}... | collective-permute-start | bytes 1179656 | tf_op jit(solution)/shard_map/ppermute | solution.py:32
  20.8 0.5 collective-permute-start.23
  21.4 0.0 collective-permute-start
  21.4 7.9 %collective-permute-done.1.refs_2_.refs_10_ = bf16[2,8,16,768]{3,2,1,0:T(8,128)(2,1)S(1)} collective-permute-done((bf16[2,8,16,768]{3,2,1,0:T(8,128)(2,1)}, bf16[2,8,16,768]{3,2,1,0:T(8,128)(2,1)S(1)}, u32[]{:S(2)}, u32[]{:S(2)}) %collective-permute-start.1) | collective-permute-done | bytes 393248 | tf_op jit(solution)/shard_map/ppermute | solution.py:32
  29.3 0.0 collective-permute-done.3.early_ref
  29.3 3.3 %collective-permute-start.4 = (bf16[2,8,16,768]{3,2,1,0:T(8,128)(2,1)S(1)}, bf16[2,8,16,768]{3,2,1,0:T(8,128)(2,1)S(1)}, u32[]{:S(2)}, u32[]{:S(2)}) collective-permute-start(bf16[2,8,16,768]{3,2,1,0:T(8,128)(2,1)S(1)} %collective-permute-done.1.refs_2_.refs_10_), channel_id=1, source_target_pairs={{0,8},{2,10},{8,12},{10,14},{12,4},{14,6},{4,0},{6,2},{1,9},{3,11}... | collective-permute-start | bytes 1179656 | tf_op jit(solution)/shard_map/ppermute | solution.py:32
  32.6 0.0 collective-permute-start.8
  32.6 0.7 collective-permute-start.2
  33.3 8.9 %collective-permute-done.4.refs_4_.refs_12_ = bf16[2,8,16,768]{3,2,1,0:T(8,128)(2,1)S(1)} collective-permute-done((bf16[2,8,16,768]{3,2,1,0:T(8,128)(2,1)S(1)}, bf16[2,8,16,768]{3,2,1,0:T(8,128)(2,1)S(1)}, u32[]{:S(2)}, u32[]{:S(2)}) %collective-permute-start.4) | collective-permute-done | bytes 393248 | tf_op jit(solution)/shard_map/ppermute | solution.py:32
  42.2 0.0 collective-permute-done.8.refs_3_.refs_11_
  42.2 3.4 %collective-permute-start.9 = (bf16[2,8,16,768]{3,2,1,0:T(8,128)(2,1)S(1)}, bf16[2,8,16,768]{3,2,1,0:T(8,128)(2,1)}, u32[]{:S(2)}, u32[]{:S(2)}) collective-permute-start(bf16[2,8,16,768]{3,2,1,0:T(8,128)(2,1)S(1)} %collective-permute-done.4.refs_4_.refs_12_), channel_id=1, source_target_pairs={{0,8},{2,10},{8,12},{10,14},{12,4},{14,6},{4,0},{6,2},{1,9},{3,11}... | collective-permute-start | bytes 1179656 | tf_op jit(solution)/shard_map/ppermute | solution.py:32
  45.6 4.6 %collective-permute-done.2.refs_2_ = bf16[16,16,768]{2,1,0:T(8,128)(2,1)} collective-permute-done((bf16[16,16,768]{2,1,0:T(8,128)(2,1)}, bf16[16,16,768]{2,1,0:T(8,128)(2,1)}, u32[]{:S(2)}, u32[]{:S(2)}) %collective-permute-start.2) | collective-permute-done | bytes 393248 | tf_op jit(solution)/shard_map/ppermute | solution.py:32
  50.3 0.7 copy-done.11
  51.0 3.4 %collective-permute-start.6 = (bf16[2,8,16,768]{3,2,1,0:T(8,128)(2,1)}, bf16[2,8,16,768]{3,2,1,0:T(8,128)(2,1)S(1)}, u32[]{:S(2)}, u32[]{:S(2)}) collective-permute-start(bf16[2,8,16,768]{3,2,1,0:T(8,128)(2,1)} %get-tuple-element.33.refs_0_.refs_8_), channel_id=1, source_target_pairs={{0,8},{2,10},{8,12},{10,14},{12,4},{14,6},{4,0},{6,2},{1,9},{3,11}... | collective-permute-start | bytes 1179656 | tf_op jit(solution)/shard_map/ppermute | solution.py:32
  54.4 3.6 %collective-permute-done.9.refs_6_.refs_14_ = bf16[2,8,16,768]{3,2,1,0:T(8,128)(2,1)} collective-permute-done((bf16[2,8,16,768]{3,2,1,0:T(8,128)(2,1)S(1)}, bf16[2,8,16,768]{3,2,1,0:T(8,128)(2,1)}, u32[]{:S(2)}, u32[]{:S(2)}) %collective-permute-start.9) | collective-permute-done | bytes 393248 | tf_op jit(solution)/shard_map/ppermute | solution.py:32
  58.0 3.5 %collective-permute-start.11 = (bf16[16,16,768]{2,1,0:T(8,128)(2,1)}, bf16[16,16,768]{2,1,0:T(8,128)(2,1)}, u32[]{:S(2)}, u32[]{:S(2)}) collective-permute-start(bf16[16,16,768]{2,1,0:T(8,128)(2,1)} %collective-permute-done.2.refs_2_), channel_id=1, source_target_pairs={{0,8},{2,10},{8,12},{10,14},{12,4},{14,6},{4,0},{6,2},{1,9},{3,11}... | collective-permute-start | bytes 1179656 | tf_op jit(solution)/shard_map/ppermute | solution.py:32
  61.5 5.0 %collective-permute-done.6.refs_2_.refs_10_ = bf16[2,8,16,768]{3,2,1,0:T(8,128)(2,1)S(1)} collective-permute-done((bf16[2,8,16,768]{3,2,1,0:T(8,128)(2,1)}, bf16[2,8,16,768]{3,2,1,0:T(8,128)(2,1)S(1)}, u32[]{:S(2)}, u32[]{:S(2)}) %collective-permute-start.6) | collective-permute-done | bytes 393248 | tf_op jit(solution)/shard_map/ppermute | solution.py:32
  66.5 0.0 collective-permute-start.7
  66.5 0.0 collective-permute-done.14.refs_7_.refs_15_
  66.6 1.1 copy-done.1
  67.7 5.6 %shard_map.83 = bf16[8,16,6144]{2,1,0:T(8,128)(2,1)} custom-call(s32[1]{0:T(128)} %bitcast.me_ref, bf16[32,16,6144]{2,1,0:T(8,128)(2,1)} %bitcast.19, bf16[1,6144]{1,0:T(2,128)(2,1)} %gain_ref.7, bf16[2,8,16,768]{3,2,1,0:T(8,128)(2,1)} %get-tuple-element.30.refs_0_.refs_8_, bf16[2,32,16,768]{3,2,1,0:T(8,128)(2,1)} %copy-done.1, ...), custom_call_target="tpu_custom_call" | custom-call | flops 1 | bytes 1 | tf_op jit(solution)/shard_map/pallas_call | solution.py:313
  73.3 0.3 collective-permute-done.11.refs_4_
  73.6 3.4 %collective-permute-start.15 = (bf16[16,16,768]{2,1,0:T(8,128)(2,1)}, bf16[16,16,768]{2,1,0:T(8,128)(2,1)S(1)}, u32[]{:S(2)}, u32[]{:S(2)}) collective-permute-start(bf16[16,16,768]{2,1,0:T(8,128)(2,1)} %collective-permute-done.11.refs_4_), channel_id=1, source_target_pairs={{0,8},{2,10},{8,12},{10,14},{12,4},{14,6},{4,0},{6,2},{1,9},{3,11}... | collective-permute-start | bytes 1179656 | tf_op jit(solution)/shard_map/ppermute | solution.py:32
  77.0 0.2 collective-permute-start.12
  77.2 0.5 collective-permute-start.21
  77.7 9.0 %collective-permute-done.15.refs_6_ = bf16[16,16,768]{2,1,0:T(8,128)(2,1)S(1)} collective-permute-done((bf16[16,16,768]{2,1,0:T(8,128)(2,1)}, bf16[16,16,768]{2,1,0:T(8,128)(2,1)S(1)}, u32[]{:S(2)}, u32[]{:S(2)}) %collective-permute-start.15) | collective-permute-done | bytes 393248 | tf_op jit(solution)/shard_map/ppermute | solution.py:32
  86.8 0.0 collective-permute-start.16
  86.8 0.0 collective-permute-done.13.refs_5_
  86.8 7.5 %collective-permute-done.12.refs_4_.refs_12_ = bf16[2,8,16,768]{3,2,1,0:T(8,128)(2,1)S(1)} collective-permute-done((bf16[2,8,16,768]{3,2,1,0:T(8,128)(2,1)S(1)}, bf16[2,8,16,768]{3,2,1,0:T(8,128)(2,1)S(1)}, u32[]{:S(2)}, u32[]{:S(2)}) %collective-permute-start.12) | collective-permute-done | bytes 393248 | tf_op jit(solution)/shard_map/ppermute | solution.py:32
  94.2 3.4 %collective-permute-start.18 = (bf16[2,8,16,768]{3,2,1,0:T(8,128)(2,1)S(1)}, bf16[2,8,16,768]{3,2,1,0:T(8,128)(2,1)S(1)}, u32[]{:S(2)}, u32[]{:S(2)}) collective-permute-start(bf16[2,8,16,768]{3,2,1,0:T(8,128)(2,1)S(1)} %collective-permute-done.12.refs_4_.refs_12_), channel_id=1, source_target_pairs={{0,8},{2,10},{8,12},{10,14},{12,4},{14,6},{4,0},{6,2},{1,9},{3,11}... | collective-permute-start | bytes 1179656 | tf_op jit(solution)/shard_map/ppermute | solution.py:32
  97.6 0.7 copy-done.26
  98.4 6.5 %shard_map.84.refs_16_ = bf16[1,16,256]{2,1,0:T(8,128)(2,1)} custom-call(s32[1]{0:T(128)} %bitcast.me_ref, bf16[32,16,6144]{2,1,0:T(8,128)(2,1)} %bitcast.20, bf16[1,6144]{1,0:T(2,128)(2,1)} %gain_ref.7, bf16[16,16,768]{2,1,0:T(8,128)(2,1)} %get-tuple-element.31.refs_0_, bf16[2,32,16,768]{3,2,1,0:T(8,128)(2,1)} %copy-done.1, ...), custom_call_target="tpu_custom_call" | custom-call | flops 1 | bytes 1 | tf_op jit(solution)/shard_map/pallas_call | solution.py:340
  104.9 1.0 slice.12
  106.0 0.1 collective-permute-start.26
  106.1 0.5 collective-permute-start.20
  106.7 0.1 collective-permute-start.19
  106.7 1.0 collective-permute-done.20.refs_15_
  107.7 0.4 collective-permute-done.19.refs_7_
  108.1 0.3 copy-done.12
  108.4 0.7 copy-done.13
  109.1 4.1 %shard_map.86 = bf16[4,16,6272]{2,1,0:T(8,128)(2,1)} custom-call(s32[1]{0:T(128)} %bitcast.me_ref, bf16[32,16,6144]{2,1,0:T(8,128)(2,1)} %bitcast.21, bf16[1,6144]{1,0:T(2,128)(2,1)} %gain_ref.7, bf16[2,8,16,768]{3,2,1,0:T(8,128)(2,1)} %get-tuple-element.33.refs_0_.refs_8_, bf16[2,32,16,768]{3,2,1,0:T(8,128)(2,1)} %copy-done.1, ...), custom_call_target="tpu_custom_call" | custom-call | flops 1 | bytes 1 | tf_op jit(solution)/shard_map/pallas_call | solution.py:313
  113.2 0.6 collective-permute-start.24
  113.7 3.8 %collective-permute-done.26.refs_2_ = bf16[16,16,768]{2,1,0:T(8,128)(2,1)S(1)} collective-permute-done((bf16[16,16,768]{2,1,0:T(8,128)(2,1)S(1)}, bf16[16,16,768]{2,1,0:T(8,128)(2,1)S(1)}, u32[]{:S(2)}, u32[]{:S(2)}) %collective-permute-start.26) | collective-permute-done | bytes 393248 | tf_op jit(solution)/shard_map/ppermute | solution.py:32
  117.5 1.2 collective-permute-start.28
  118.7 4.0 %shard_map.85 = bf16[4,16,6144]{2,1,0:T(8,128)(2,1)} custom-call(s32[1]{0:T(128)} %bitcast.me_ref, bf16[32,16,6144]{2,1,0:T(8,128)(2,1)} %bitcast.22, bf16[1,6144]{1,0:T(2,128)(2,1)} %gain_ref.7, bf16[2,8,16,768]{3,2,1,0:T(8,128)(2,1)} %get-tuple-element.33.refs_0_.refs_8_, bf16[2,32,16,768]{3,2,1,0:T(8,128)(2,1)} %copy-done.1, ...), custom_call_target="tpu_custom_call" | custom-call | flops 1 | bytes 1 | tf_op jit(solution)/shard_map/pallas_call | solution.py:313
  122.8 1.2 shard_map.87.refs_0_
  123.9 4.3 %collective-permute-done.28.refs_4_ = bf16[16,16,768]{2,1,0:T(8,128)(2,1)S(1)} collective-permute-done((bf16[16,16,768]{2,1,0:T(8,128)(2,1)S(1)}, bf16[16,16,768]{2,1,0:T(8,128)(2,1)S(1)}, u32[]{:S(2)}, u32[]{:S(2)}) %collective-permute-start.28) | collective-permute-done | bytes 393248 | tf_op jit(solution)/shard_map/ppermute | solution.py:32
  128.3 2.2 %collective-permute-start.30 = (bf16[16,16,768]{2,1,0:T(8,128)(2,1)S(1)}, bf16[16,16,768]{2,1,0:T(8,128)(2,1)S(1)}, u32[]{:S(2)}, u32[]{:S(2)}) collective-permute-start(bf16[16,16,768]{2,1,0:T(8,128)(2,1)S(1)} %collective-permute-done.28.refs_4_), channel_id=1, source_target_pairs={{0,8},{2,10},{8,12},{10,14},{12,4},{14,6},{4,0},{6,2},{1,9},{3,11}... | collective-permute-start | bytes 1179656 | tf_op jit(solution)/shard_map/ppermute | solution.py:32
  130.5 0.5 collective-permute-start.22
  131.1 0.5 collective-permute-start.27
  131.6 6.5 %collective-permute-done.30.refs_6_ = bf16[16,16,768]{2,1,0:T(8,128)(2,1)S(1)} collective-permute-done((bf16[16,16,768]{2,1,0:T(8,128)(2,1)S(1)}, bf16[16,16,768]{2,1,0:T(8,128)(2,1)S(1)}, u32[]{:S(2)}, u32[]{:S(2)}) %collective-permute-start.30) | collective-permute-done | bytes 393248 | tf_op jit(solution)/shard_map/ppermute | solution.py:32
  138.1 0.5 collective-permute-start.31
  138.6 0.9 shard_map.88.refs_8_
  139.6 0.2 collective-permute-done.29.refs_5_
  139.8 0.6 collective-permute-done.31.refs_7_
  140.4 0.1 copy-done.22
  140.5 0.1 copy-done.24
  140.6 0.8 copy-done.25
  141.4 6.2 %shard_map.89.refs_0_ = bf16[32,16,6144]{2,1,0:T(8,128)(2,1)} custom-call(s32[1]{0:T(128)} %bitcast.me_ref, bf16[14,16,6144]{2,1,0:T(8,128)(2,1)} %collective-permute-done.23.carrier_ref, bf16[4,16,6144]{2,1,0:T(8,128)(2,1)} %copy-done.14, bf16[4,16,6272]{2,1,0:T(8,128)(2,1)} %copy-done, ...), custom_call_target="tpu_custom_call", output_to_operand_aliasing={{}: (12, {})} | custom-call | flops 1 | bytes 1 | tf_op jit(solution)/shard_map/pallas_call | solution.py:365
  147.6 2.8 %collective-permute-done.22.block_ref = bf16[4,16,6144]{2,1,0:T(8,128)(2,1)S(1)} collective-permute-done((bf16[4,16,6144]{2,1,0:T(8,128)(2,1)S(1)}, bf16[4,16,6144]{2,1,0:T(8,128)(2,1)S(1)}, u32[]{:S(2)}, u32[]{:S(2)}) %collective-permute-start.22) | collective-permute-done | bytes 786464 | tf_op jit(solution)/shard_map/ppermute | solution.py:19
  150.4 0.9 shard_map.90
  (67 shorter events, 0.2 us)
Async XLA Ops:
  1.2 28.1 %collective-permute-start.3 = (bf16[4,16,6144]{2,1,0:T(8,128)(2,1)S(1)}, bf16[4,16,6144]{2,1,0:T(8,128)(2,1)S(1)}, u32[]{:S(2)}, u32[]{:S(2)}) collective-permute-start(bf16[4,16,6144]{2,1,0:T(8,128)(2,1)S(1)} %slice_bitcast_fusion), channel_id=1, source_target_pairs={{1,0},{0,1},{3,2},{2,3},{5,4},{4,5},{7,6},{6,7},{9,8},{8,9},{11,10... | collective-permute-start | bytes 2359304 | tf_op jit(solution)/shard_map/ppermute | solution.py:19
  18.2 11.0 %collective-permute-start.1 = (bf16[2,8,16,768]{3,2,1,0:T(8,128)(2,1)}, bf16[2,8,16,768]{3,2,1,0:T(8,128)(2,1)S(1)}, u32[]{:S(2)}, u32[]{:S(2)}) collective-permute-start(bf16[2,8,16,768]{3,2,1,0:T(8,128)(2,1)} %get-tuple-element.30.refs_0_.refs_8_), channel_id=1, source_target_pairs={{0,8},{2,10},{8,12},{10,14},{12,4},{14,6},{4,0},{6,2},{1,9},{3,11}... | collective-permute-start | bytes 1179656 | tf_op jit(solution)/shard_map/ppermute | solution.py:32
  20.8 84.0 %collective-permute-start.23 = (bf16[14,16,6144]{2,1,0:T(8,128)(2,1)}, bf16[14,16,6144]{2,1,0:T(8,128)(2,1)}, u32[]{:S(2)}, u32[]{:S(2)}) collective-permute-start(bf16[14,16,6144]{2,1,0:T(8,128)(2,1)} %get-tuple-element.42), channel_id=1, source_target_pairs={{1,0},{0,1},{3,2},{2,3},{5,4},{4,5},{7,6},{6,7},{9,8},{8,9},{11,10... | collective-permute-start | bytes 8257544 | tf_op jit(solution)/shard_map/ppermute | solution.py:19
  21.4 45.1 %collective-permute-start = (bf16[2,32,16,768]{3,2,1,0:T(8,128)(2,1)}, bf16[2,32,16,768]{3,2,1,0:T(8,128)(2,1)S(1)}, u32[]{:S(2)}, u32[]{:S(2)}) collective-permute-start(bf16[2,32,16,768]{3,2,1,0:T(8,128)(2,1)} %get-tuple-element.28), channel_id=1, source_target_pairs={{0,2},{2,0},{4,6},{6,4},{8,10},{10,8},{12,14},{14,12},{1,3},{3,1},... | collective-permute-start | bytes 4718600 | tf_op jit(solution)/shard_map/ppermute | solution.py:37
  29.2 37.3 %copy-start.8 = (bf16[2,8,16,768]{3,2,1,0:T(8,128)(2,1)}, bf16[2,8,16,768]{3,2,1,0:T(8,128)(2,1)S(1)}, u32[]{:S(2)}) copy-start(bf16[2,8,16,768]{3,2,1,0:T(8,128)(2,1)S(1)} %collective-permute-done.1.refs_2_.refs_10_) | copy-start | bytes 1179652
  29.3 37.2 %copy-start.14 = (bf16[4,16,6144]{2,1,0:T(8,128)(2,1)}, bf16[4,16,6144]{2,1,0:T(8,128)(2,1)S(1)}, u32[]{:S(2)}) copy-start(bf16[4,16,6144]{2,1,0:T(8,128)(2,1)S(1)} %collective-permute-done.3.early_ref) | copy-start | bytes 2359300
  29.3 12.9 %collective-permute-start.4 = (bf16[2,8,16,768]{3,2,1,0:T(8,128)(2,1)S(1)}, bf16[2,8,16,768]{3,2,1,0:T(8,128)(2,1)S(1)}, u32[]{:S(2)}, u32[]{:S(2)}) collective-permute-start(bf16[2,8,16,768]{3,2,1,0:T(8,128)(2,1)S(1)} %collective-permute-done.1.refs_2_.refs_10_), channel_id=1, source_target_pairs={{0,8},{2,10},{8,12},{10,14},{12,4},{14,6},{4,0},{6,2},{1,9},{3,11}... | collective-permute-start | bytes 1179656 | tf_op jit(solution)/shard_map/ppermute | solution.py:32
  32.6 9.6 %collective-permute-start.8 = (bf16[2,8,16,768]{3,2,1,0:T(8,128)(2,1)S(1)}, bf16[2,8,16,768]{3,2,1,0:T(8,128)(2,1)S(1)}, u32[]{:S(2)}, u32[]{:S(2)}) collective-permute-start(bf16[2,8,16,768]{3,2,1,0:T(8,128)(2,1)S(1)} %collective-permute-done.1.refs_2_.refs_10_), channel_id=1, source_target_pairs={{0,2},{2,0},{4,6},{6,4},{8,10},{10,8},{12,14},{14,12},{1,3},{3,1},... | collective-permute-start | bytes 1179656 | tf_op jit(solution)/shard_map/ppermute | solution.py:37
  32.6 17.7 %collective-permute-start.2 = (bf16[16,16,768]{2,1,0:T(8,128)(2,1)}, bf16[16,16,768]{2,1,0:T(8,128)(2,1)}, u32[]{:S(2)}, u32[]{:S(2)}) collective-permute-start(bf16[16,16,768]{2,1,0:T(8,128)(2,1)} %get-tuple-element.31.refs_0_), channel_id=1, source_target_pairs={{0,8},{2,10},{8,12},{10,14},{12,4},{14,6},{4,0},{6,2},{1,9},{3,11}... | collective-permute-start | bytes 1179656 | tf_op jit(solution)/shard_map/ppermute | solution.py:32
  42.1 24.4 %copy-start.9 = (bf16[2,8,16,768]{3,2,1,0:T(8,128)(2,1)}, bf16[2,8,16,768]{3,2,1,0:T(8,128)(2,1)S(1)}, u32[]{:S(2)}) copy-start(bf16[2,8,16,768]{3,2,1,0:T(8,128)(2,1)S(1)} %collective-permute-done.4.refs_4_.refs_12_) | copy-start | bytes 1179652
  42.2 8.1 %collective-permute-start.5 = (bf16[2,8,16,768]{3,2,1,0:T(8,128)(2,1)S(1)}, bf16[2,8,16,768]{3,2,1,0:T(8,128)(2,1)S(1)}, u32[]{:S(2)}, u32[]{:S(2)}) collective-permute-start(bf16[2,8,16,768]{3,2,1,0:T(8,128)(2,1)S(1)} %collective-permute-done.4.refs_4_.refs_12_), channel_id=1, source_target_pairs={{0,2},{2,0},{4,6},{6,4},{8,10},{10,8},{12,14},{14,12},{1,3},{3,1},... | collective-permute-start | bytes 1179656 | tf_op jit(solution)/shard_map/ppermute | solution.py:37
  42.2 24.4 %copy-start.10 = (bf16[2,8,16,768]{3,2,1,0:T(8,128)(2,1)}, bf16[2,8,16,768]{3,2,1,0:T(8,128)(2,1)S(1)}, u32[]{:S(2)}) copy-start(bf16[2,8,16,768]{3,2,1,0:T(8,128)(2,1)S(1)} %collective-permute-done.8.refs_3_.refs_11_) | copy-start | bytes 1179652
  42.2 15.8 %collective-permute-start.9 = (bf16[2,8,16,768]{3,2,1,0:T(8,128)(2,1)S(1)}, bf16[2,8,16,768]{3,2,1,0:T(8,128)(2,1)}, u32[]{:S(2)}, u32[]{:S(2)}) collective-permute-start(bf16[2,8,16,768]{3,2,1,0:T(8,128)(2,1)S(1)} %collective-permute-done.4.refs_4_.refs_12_), channel_id=1, source_target_pairs={{0,8},{2,10},{8,12},{10,14},{12,4},{14,6},{4,0},{6,2},{1,9},{3,11}... | collective-permute-start | bytes 1179656 | tf_op jit(solution)/shard_map/ppermute | solution.py:32
  50.3 7.7 %collective-permute-start.10 = (bf16[16,16,768]{2,1,0:T(8,128)(2,1)}, bf16[16,16,768]{2,1,0:T(8,128)(2,1)S(1)}, u32[]{:S(2)}, u32[]{:S(2)}) collective-permute-start(bf16[16,16,768]{2,1,0:T(8,128)(2,1)} %collective-permute-done.2.refs_2_), channel_id=1, source_target_pairs={{0,2},{2,0},{4,6},{6,4},{8,10},{10,8},{12,14},{14,12},{1,3},{3,1},... | collective-permute-start | bytes 1179656 | tf_op jit(solution)/shard_map/ppermute | solution.py:37
  50.3 0.8 copy-start.11
  51.0 15.5 %collective-permute-start.6 = (bf16[2,8,16,768]{3,2,1,0:T(8,128)(2,1)}, bf16[2,8,16,768]{3,2,1,0:T(8,128)(2,1)S(1)}, u32[]{:S(2)}, u32[]{:S(2)}) collective-permute-start(bf16[2,8,16,768]{3,2,1,0:T(8,128)(2,1)} %get-tuple-element.33.refs_0_.refs_8_), channel_id=1, source_target_pairs={{0,8},{2,10},{8,12},{10,14},{12,4},{14,6},{4,0},{6,2},{1,9},{3,11}... | collective-permute-start | bytes 1179656 | tf_op jit(solution)/shard_map/ppermute | solution.py:32
  57.9 8.6 %collective-permute-start.14 = (bf16[2,8,16,768]{3,2,1,0:T(8,128)(2,1)}, bf16[2,8,16,768]{3,2,1,0:T(8,128)(2,1)}, u32[]{:S(2)}, u32[]{:S(2)}) collective-permute-start(bf16[2,8,16,768]{3,2,1,0:T(8,128)(2,1)} %collective-permute-done.9.refs_6_.refs_14_), channel_id=1, source_target_pairs={{0,2},{2,0},{4,6},{6,4},{8,10},{10,8},{12,14},{14,12},{1,3},{3,1},... | collective-permute-start | bytes 1179656 | tf_op jit(solution)/shard_map/ppermute | solution.py:37
  58.0 8.5 %copy-start.17 = (bf16[16,16,768]{2,1,0:T(8,128)(2,1)}, bf16[16,16,768]{2,1,0:T(8,128)(2,1)S(1)}, u32[]{:S(2)}) copy-start(bf16[16,16,768]{2,1,0:T(8,128)(2,1)S(1)} %collective-permute-done.10.refs_3_) | copy-start | bytes 1179652
  58.0 15.6 %collective-permute-start.11 = (bf16[16,16,768]{2,1,0:T(8,128)(2,1)}, bf16[16,16,768]{2,1,0:T(8,128)(2,1)}, u32[]{:S(2)}, u32[]{:S(2)}) collective-permute-start(bf16[16,16,768]{2,1,0:T(8,128)(2,1)} %collective-permute-done.2.refs_2_), channel_id=1, source_target_pairs={{0,8},{2,10},{8,12},{10,14},{12,4},{14,6},{4,0},{6,2},{1,9},{3,11}... | collective-permute-start | bytes 1179656 | tf_op jit(solution)/shard_map/ppermute | solution.py:32
  66.5 41.6 %copy-start.3 = (bf16[2,8,16,768]{3,2,1,0:T(8,128)(2,1)}, bf16[2,8,16,768]{3,2,1,0:T(8,128)(2,1)S(1)}, u32[]{:S(2)}) copy-start(bf16[2,8,16,768]{3,2,1,0:T(8,128)(2,1)S(1)} %collective-permute-done.6.refs_2_.refs_10_) | copy-start | bytes 1179652
  66.5 10.5 %collective-permute-start.7 = (bf16[2,8,16,768]{3,2,1,0:T(8,128)(2,1)S(1)}, bf16[2,8,16,768]{3,2,1,0:T(8,128)(2,1)S(1)}, u32[]{:S(2)}, u32[]{:S(2)}) collective-permute-start(bf16[2,8,16,768]{3,2,1,0:T(8,128)(2,1)S(1)} %collective-permute-done.6.refs_2_.refs_10_), channel_id=1, source_target_pairs={{0,2},{2,0},{4,6},{6,4},{8,10},{10,8},{12,14},{14,12},{1,3},{3,1},... | collective-permute-start | bytes 1179656 | tf_op jit(solution)/shard_map/ppermute | solution.py:37
  66.5 1.2 copy-start.1
  73.6 13.2 %collective-permute-start.15 = (bf16[16,16,768]{2,1,0:T(8,128)(2,1)}, bf16[16,16,768]{2,1,0:T(8,128)(2,1)S(1)}, u32[]{:S(2)}, u32[]{:S(2)}) collective-permute-start(bf16[16,16,768]{2,1,0:T(8,128)(2,1)} %collective-permute-done.11.refs_4_), channel_id=1, source_target_pairs={{0,8},{2,10},{8,12},{10,14},{12,4},{14,6},{4,0},{6,2},{1,9},{3,11}... | collective-permute-start | bytes 1179656 | tf_op jit(solution)/shard_map/ppermute | solution.py:32
  77.0 9.8 %collective-permute-start.13 = (bf16[16,16,768]{2,1,0:T(8,128)(2,1)}, bf16[16,16,768]{2,1,0:T(8,128)(2,1)S(1)}, u32[]{:S(2)}, u32[]{:S(2)}) collective-permute-start(bf16[16,16,768]{2,1,0:T(8,128)(2,1)} %collective-permute-done.11.refs_4_), channel_id=1, source_target_pairs={{0,2},{2,0},{4,6},{6,4},{8,10},{10,8},{12,14},{14,12},{1,3},{3,1},... | collective-permute-start | bytes 1179656 | tf_op jit(solution)/shard_map/ppermute | solution.py:37
  77.0 29.1 %copy-start.4 = (bf16[2,8,16,768]{3,2,1,0:T(8,128)(2,1)}, bf16[2,8,16,768]{3,2,1,0:T(8,128)(2,1)S(1)}, u32[]{:S(2)}) copy-start(bf16[2,8,16,768]{3,2,1,0:T(8,128)(2,1)S(1)} %collective-permute-done.7.refs_3_.refs_11_) | copy-start | bytes 1179652
  77.0 17.3 %collective-permute-start.12 = (bf16[2,8,16,768]{3,2,1,0:T(8,128)(2,1)S(1)}, bf16[2,8,16,768]{3,2,1,0:T(8,128)(2,1)S(1)}, u32[]{:S(2)}, u32[]{:S(2)}) collective-permute-start(bf16[2,8,16,768]{3,2,1,0:T(8,128)(2,1)S(1)} %collective-permute-done.6.refs_2_.refs_10_), channel_id=1, source_target_pairs={{0,8},{2,10},{8,12},{10,14},{12,4},{14,6},{4,0},{6,2},{1,9},{3,11}... | collective-permute-start | bytes 1179656 | tf_op jit(solution)/shard_map/ppermute | solution.py:32
  77.2 45.6 %collective-permute-start.21 = (bf16[8,16,6144]{2,1,0:T(8,128)(2,1)}, bf16[8,16,6144]{2,1,0:T(8,128)(2,1)S(1)}, u32[]{:S(2)}, u32[]{:S(2)}) collective-permute-start(bf16[8,16,6144]{2,1,0:T(8,128)(2,1)} %shard_map.83), channel_id=1, source_target_pairs={{1,0},{0,1},{3,2},{2,3},{5,4},{4,5},{7,6},{6,7},{9,8},{8,9},{11,10... | collective-permute-start | bytes 4718600 | tf_op jit(solution)/shard_map/ppermute | solution.py:19
  86.8 10.9 %copy-start.21 = (bf16[16,16,768]{2,1,0:T(8,128)(2,1)}, bf16[16,16,768]{2,1,0:T(8,128)(2,1)S(1)}, u32[]{:S(2)}) copy-start(bf16[16,16,768]{2,1,0:T(8,128)(2,1)S(1)} %collective-permute-done.15.refs_6_) | copy-start | bytes 1179652
  86.8 10.9 %collective-permute-start.16 = (bf16[16,16,768]{2,1,0:T(8,128)(2,1)S(1)}, bf16[16,16,768]{2,1,0:T(8,128)(2,1)S(1)}, u32[]{:S(2)}, u32[]{:S(2)}) collective-permute-start(bf16[16,16,768]{2,1,0:T(8,128)(2,1)S(1)} %collective-permute-done.15.refs_6_), channel_id=1, source_target_pairs={{0,2},{2,0},{4,6},{6,4},{8,10},{10,8},{12,14},{14,12},{1,3},{3,1},... | collective-permute-start | bytes 1179656 | tf_op jit(solution)/shard_map/ppermute | solution.py:37
  86.8 10.9 %copy-start.23 = (bf16[16,16,768]{2,1,0:T(8,128)(2,1)}, bf16[16,16,768]{2,1,0:T(8,128)(2,1)S(1)}, u32[]{:S(2)}) copy-start(bf16[16,16,768]{2,1,0:T(8,128)(2,1)S(1)} %collective-permute-done.13.refs_5_) | copy-start | bytes 1179652
  94.2 11.9 %copy-start.5 = (bf16[2,8,16,768]{3,2,1,0:T(8,128)(2,1)}, bf16[2,8,16,768]{3,2,1,0:T(8,128)(2,1)S(1)}, u32[]{:S(2)}) copy-start(bf16[2,8,16,768]{3,2,1,0:T(8,128)(2,1)S(1)} %collective-permute-done.12.refs_4_.refs_12_) | copy-start | bytes 1179652
  94.2 11.8 %collective-permute-start.18 = (bf16[2,8,16,768]{3,2,1,0:T(8,128)(2,1)S(1)}, bf16[2,8,16,768]{3,2,1,0:T(8,128)(2,1)S(1)}, u32[]{:S(2)}, u32[]{:S(2)}) collective-permute-start(bf16[2,8,16,768]{3,2,1,0:T(8,128)(2,1)S(1)} %collective-permute-done.12.refs_4_.refs_12_), channel_id=1, source_target_pairs={{0,8},{2,10},{8,12},{10,14},{12,4},{14,6},{4,0},{6,2},{1,9},{3,11}... | collective-permute-start | bytes 1179656 | tf_op jit(solution)/shard_map/ppermute | solution.py:32
  97.6 0.7 copy-start.26
  104.9 1.9 %collective-permute-start.17 = (bf16[2,8,16,768]{3,2,1,0:T(8,128)(2,1)S(1)}, bf16[2,8,16,768]{3,2,1,0:T(8,128)(2,1)S(1)}, u32[]{:S(2)}, u32[]{:S(2)}) collective-permute-start(bf16[2,8,16,768]{3,2,1,0:T(8,128)(2,1)S(1)} %collective-permute-done.12.refs_4_.refs_12_), channel_id=1, source_target_pairs={{0,2},{2,0},{4,6},{6,4},{8,10},{10,8},{12,14},{14,12},{1,3},{3,1},... | collective-permute-start | bytes 1179656 | tf_op jit(solution)/shard_map/ppermute | solution.py:37
  105.9 25.1 %copy-start.7 = (bf16[2,2,8,8,768]{4,3,1,2,0:T(8,128)(2,1)}, bf16[2,2,8,8,768]{4,3,1,2,0:T(8,128)(2,1)S(1)}, u32[]{:S(2)}) copy-start(bf16[2,2,8,8,768]{4,3,1,2,0:T(8,128)(2,1)S(1)} %copy.15) | copy-start | bytes 1179652
  106.0 11.6 %collective-permute-start.26 = (bf16[16,16,768]{2,1,0:T(8,128)(2,1)S(1)}, bf16[16,16,768]{2,1,0:T(8,128)(2,1)S(1)}, u32[]{:S(2)}, u32[]{:S(2)}) collective-permute-start(bf16[16,16,768]{2,1,0:T(8,128)(2,1)S(1)} %bitcast.24), channel_id=1, source_target_pairs={{0,8},{2,10},{8,12},{10,14},{12,4},{14,6},{4,0},{6,2},{1,9},{3,11}... | collective-permute-start | bytes 1179656 | tf_op jit(solution)/shard_map/ppermute | solution.py:32
  106.1 2.0 %copy-start.2 = (bf16[2,8,16,768]{3,2,1,0:T(8,128)(2,1)}, bf16[2,8,16,768]{3,2,1,0:T(8,128)(2,1)S(1)}, u32[]{:S(2)}) copy-start(bf16[2,8,16,768]{3,2,1,0:T(8,128)(2,1)S(1)} %collective-permute-done.18.refs_6_.refs_14_) | copy-start | bytes 1179652
  106.1 1.6 %collective-permute-start.20 = (bf16[8,16,768]{2,1,0:T(8,128)(2,1)S(1)}, bf16[8,16,768]{2,1,0:T(8,128)(2,1)S(1)}, u32[]{:S(2)}, u32[]{:S(2)}) collective-permute-start(bf16[8,16,768]{2,1,0:T(8,128)(2,1)S(1)} %get-tuple-element.49), channel_id=1, source_target_pairs={{0,2},{2,0},{4,6},{6,4},{8,10},{10,8},{12,14},{14,12},{1,3},{3,1},... | collective-permute-start | bytes 589832 | tf_op jit(solution)/shard_map/ppermute | solution.py:37
  106.7 1.4 collective-permute-start.19
  106.7 1.4 copy-start.6
  107.7 0.7 copy-start.12
  108.4 0.7 copy-start.13
  113.2 25.0 %collective-permute-start.24 = (bf16[4,16,6272]{2,1,0:T(8,128)(2,1)}, bf16[4,16,6272]{2,1,0:T(8,128)(2,1)S(1)}, u32[]{:S(2)}, u32[]{:S(2)}) collective-permute-start(bf16[4,16,6272]{2,1,0:T(8,128)(2,1)} %shard_map.86), channel_id=1, source_target_pairs={{1,0},{0,1},{3,2},{2,3},{5,4},{4,5},{7,6},{6,7},{9,8},{8,9},{11,10... | collective-permute-start | bytes 2408456 | tf_op jit(solution)/shard_map/ppermute | solution.py:19
  117.5 13.5 %copy-start.16 = (bf16[16,16,768]{2,1,0:T(8,128)(2,1)}, bf16[16,16,768]{2,1,0:T(8,128)(2,1)S(1)}, u32[]{:S(2)}) copy-start(bf16[16,16,768]{2,1,0:T(8,128)(2,1)S(1)} %collective-permute-done.26.refs_2_) | copy-start | bytes 1179652
  117.5 10.7 %collective-permute-start.28 = (bf16[16,16,768]{2,1,0:T(8,128)(2,1)S(1)}, bf16[16,16,768]{2,1,0:T(8,128)(2,1)S(1)}, u32[]{:S(2)}, u32[]{:S(2)}) collective-permute-start(bf16[16,16,768]{2,1,0:T(8,128)(2,1)S(1)} %collective-permute-done.26.refs_2_), channel_id=1, source_target_pairs={{0,8},{2,10},{8,12},{10,14},{12,4},{14,6},{4,0},{6,2},{1,9},{3,11}... | collective-permute-start | bytes 1179656 | tf_op jit(solution)/shard_map/ppermute | solution.py:32
  122.8 7.8 %copy-start.15 = (bf16[4,16,6144]{2,1,0:T(8,128)(2,1)S(1)}, bf16[4,16,6144]{2,1,0:T(8,128)(2,1)}, u32[]{:S(2)}) copy-start(bf16[4,16,6144]{2,1,0:T(8,128)(2,1)} %shard_map.85) | copy-start | bytes 2359300
  128.3 11.3 %copy-start.18 = (bf16[16,16,768]{2,1,0:T(8,128)(2,1)}, bf16[16,16,768]{2,1,0:T(8,128)(2,1)S(1)}, u32[]{:S(2)}) copy-start(bf16[16,16,768]{2,1,0:T(8,128)(2,1)S(1)} %collective-permute-done.28.refs_4_) | copy-start | bytes 1179652
  128.3 9.8 %collective-permute-start.30 = (bf16[16,16,768]{2,1,0:T(8,128)(2,1)S(1)}, bf16[16,16,768]{2,1,0:T(8,128)(2,1)S(1)}, u32[]{:S(2)}, u32[]{:S(2)}) collective-permute-start(bf16[16,16,768]{2,1,0:T(8,128)(2,1)S(1)} %collective-permute-done.28.refs_4_), channel_id=1, source_target_pairs={{0,8},{2,10},{8,12},{10,14},{12,4},{14,6},{4,0},{6,2},{1,9},{3,11}... | collective-permute-start | bytes 1179656 | tf_op jit(solution)/shard_map/ppermute | solution.py:32
  130.5 19.9 %collective-permute-start.22 = (bf16[4,16,6144]{2,1,0:T(8,128)(2,1)S(1)}, bf16[4,16,6144]{2,1,0:T(8,128)(2,1)S(1)}, u32[]{:S(2)}, u32[]{:S(2)}) collective-permute-start(bf16[4,16,6144]{2,1,0:T(8,128)(2,1)S(1)} %copy-done.15), channel_id=1, source_target_pairs={{1,0},{0,1},{3,2},{2,3},{5,4},{4,5},{7,6},{6,7},{9,8},{8,9},{11,10... | collective-permute-start | bytes 2359304 | tf_op jit(solution)/shard_map/ppermute | solution.py:19
  131.1 8.5 %collective-permute-start.25 = (bf16[16,16,768]{2,1,0:T(8,128)(2,1)S(1)}, bf16[16,16,768]{2,1,0:T(8,128)(2,1)S(1)}, u32[]{:S(2)}, u32[]{:S(2)}) collective-permute-start(bf16[16,16,768]{2,1,0:T(8,128)(2,1)S(1)} %bitcast.25), channel_id=1, source_target_pairs={{0,2},{2,0},{4,6},{6,4},{8,10},{10,8},{12,14},{14,12},{1,3},{3,1},... | collective-permute-start | bytes 1179656 | tf_op jit(solution)/shard_map/ppermute | solution.py:37
  131.1 8.5 %collective-permute-start.27 = (bf16[16,16,768]{2,1,0:T(8,128)(2,1)S(1)}, bf16[16,16,768]{2,1,0:T(8,128)(2,1)S(1)}, u32[]{:S(2)}, u32[]{:S(2)}) collective-permute-start(bf16[16,16,768]{2,1,0:T(8,128)(2,1)S(1)} %collective-permute-done.26.refs_2_), channel_id=1, source_target_pairs={{0,2},{2,0},{4,6},{6,4},{8,10},{10,8},{12,14},{14,12},{1,3},{3,1},... | collective-permute-start | bytes 1179656 | tf_op jit(solution)/shard_map/ppermute | solution.py:37
  138.1 1.4 copy-start.19
  138.1 1.7 %collective-permute-start.29 = (bf16[16,16,768]{2,1,0:T(8,128)(2,1)S(1)}, bf16[16,16,768]{2,1,0:T(8,128)(2,1)S(1)}, u32[]{:S(2)}, u32[]{:S(2)}) collective-permute-start(bf16[16,16,768]{2,1,0:T(8,128)(2,1)S(1)} %collective-permute-done.28.refs_4_), channel_id=1, source_target_pairs={{0,2},{2,0},{4,6},{6,4},{8,10},{10,8},{12,14},{14,12},{1,3},{3,1},... | collective-permute-start | bytes 1179656 | tf_op jit(solution)/shard_map/ppermute | solution.py:37
  138.1 1.4 copy-start
  138.1 2.3 %collective-permute-start.31 = (bf16[16,16,768]{2,1,0:T(8,128)(2,1)S(1)}, bf16[16,16,768]{2,1,0:T(8,128)(2,1)S(1)}, u32[]{:S(2)}, u32[]{:S(2)}) collective-permute-start(bf16[16,16,768]{2,1,0:T(8,128)(2,1)S(1)} %collective-permute-done.30.refs_6_), channel_id=1, source_target_pairs={{0,2},{2,0},{4,6},{6,4},{8,10},{10,8},{12,14},{14,12},{1,3},{3,1},... | collective-permute-start | bytes 1179656 | tf_op jit(solution)/shard_map/ppermute | solution.py:37
  139.6 0.8 copy-start.20
  139.6 0.9 copy-start.22
  139.8 0.8 copy-start.24
  140.6 0.8 copy-start.25

commit v5 on v4

--- a/solution.py
+++ b/solution.py
@@ -507,10 +507,10 @@
     third_out = layer_blocks(me, rows, middle, last - middle, norm_gain, other, *maps, middle - end)
     third_sent = passed_along(tied(third_out, first_sent), "section", 1)
     ups.step()
-    ups.step(second_out)
+    ups.step()
     result = place_blocks(first_sent, at, None, rows.shape)
     ups.held, result = lax.optimization_barrier((ups.held, result))
-    ups.step(third_out)
+    ups.step(second_out, third_out)
 
     maps = [ups.pieces[0], core_swap(ups.pieces[0])] + ups.pieces[1:]
     result = place_blocks(second_sent, end, result, rows.shape)

time: 152 us -> 152 us (level)
  no operation moved by 1% of the time
where the time goes in v5:
time: 152 us; the launch traced here: 151 us
  waiting for transfers between devices  66.4 us (44%)
  Pallas kernels  43.3 us (28%)
  starting transfers between devices  34.3 us (23%)
  local copies, waits for them, and re-layouts  6.93 us (5%)
    ppermute x12, waiting for transfers between devices, ring_step(): return lax.ppermute(block, 'expert', route)  61.5 us
    ppermute x12, starting transfers between devices, ring_step(): return lax.ppermute(block, 'expert', route)  27.5 us
    pallas_call x1, Pallas kernels, generated(): pl.pallas_call(functools.partial(generator_kernel, chunks, rank), out_sha...  14 us
    pallas_call x3, Pallas kernels, layer_blocks(): pl.pallas_call(functools.partial(layer_kernel, len(pieces) // 2, rank, wi...  13.7 us
    pallas_call x1, Pallas kernels, low_blocks(): pl.pallas_call(functools.partial(low_kernel, len(pieces), rank, width), o...  6.49 us
    pallas_call x1, Pallas kernels, update_blocks(): pl.pallas_call(functools.partial(update_kernel, n, rank), out_shape=jax.S...  6.24 us
    ppermute x5, starting transfers between devices, passed_along(): return lax.ppermute(block, axis, route)  5.16 us
    unnamed x54, local copies, waits for them, and re-layouts  4.67 us
  transfers between devices with their start and end apart: 32, of which 16 were waited for; matrix products, arithmetic and copies ran while one was open for 1% of the time, Pallas kernels for 28%

profile of v5, /device:TPU:0, one launch (start us, length us, event | category | flops | bytes accessed | tf_op | source)
XLA Modules:
  0.0 151.3 jit_solution(16380956854632946188)
XLA Ops:
  0.0 1.2 slice_bitcast_fusion
  1.2 3.0 %collective-permute-start.3 = (bf16[4,16,6144]{2,1,0:T(8,128)(2,1)S(1)}, bf16[4,16,6144]{2,1,0:T(8,128)(2,1)S(1)}, u32[]{:S(2)}, u32[]{:S(2)}) collective-permute-start(bf16[4,16,6144]{2,1,0:T(8,128)(2,1)S(1)} %slice_bitcast_fusion), channel_id=1, source_target_pairs={{1,0},{0,1},{3,2},{2,3},{5,4},{4,5},{7,6},{6,7},{9,8},{8,9},{11,10... | collective-permute-start | bytes 2359304 | tf_op jit(solution)/shard_map/ppermute | solution.py:19
  4.2 14.0 %shard_map.82 = (bf16[2,32,16,768]{3,2,1,0:T(8,128)(2,1)}, bf16[16,16,768]{2,1,0:T(8,128)(2,1)}, bf16[14,16,6144]{2,1,0:T(8,128)(2,1)}, bf16[2,8,16,768]{3,2,1,0:T(8,128)(2,1)}, bf16[2,8,16,768]{3,2,1,0:T(8,128)(2,1)}) custom-call(s32[32]{0:T(128)} %bitcast.27, s32[8]{0:T(128)} %bitcast.28, bf16[8,256]{1,0:T(8,128)(2,1)} %task_embed_ref.1, ...), custom_call_target="tpu_custom_call" | custom-call | flops 1 | bytes 1 | tf_op jit(solution)/shard_map/pallas_call | solution.py:136
  18.2 2.6 %collective-permute-start.1 = (bf16[2,8,16,768]{3,2,1,0:T(8,128)(2,1)}, bf16[2,8,16,768]{3,2,1,0:T(8,128)(2,1)S(1)}, u32[]{:S(2)}, u32[]{:S(2)}) collective-permute-start(bf16[2,8,16,768]{3,2,1,0:T(8,128)(2,1)} %get-tuple-element.30.refs_0_.refs_8_), channel_id=1, source_target_pairs={{0,8},{2,10},{8,12},{10,14},{12,4},{14,6},{4,0},{6,2},{1,9},{3,11}... | collective-permute-start | bytes 1179656 | tf_op jit(solution)/shard_map/ppermute | solution.py:32
  20.8 0.5 collective-permute-start.23
  21.4 0.0 collective-permute-start
  21.4 7.9 %collective-permute-done.1.refs_2_.refs_10_ = bf16[2,8,16,768]{3,2,1,0:T(8,128)(2,1)S(1)} collective-permute-done((bf16[2,8,16,768]{3,2,1,0:T(8,128)(2,1)}, bf16[2,8,16,768]{3,2,1,0:T(8,128)(2,1)S(1)}, u32[]{:S(2)}, u32[]{:S(2)}) %collective-permute-start.1) | collective-permute-done | bytes 393248 | tf_op jit(solution)/shard_map/ppermute | solution.py:32
  29.3 0.0 collective-permute-done.3.early_ref
  29.3 3.3 %collective-permute-start.4 = (bf16[2,8,16,768]{3,2,1,0:T(8,128)(2,1)S(1)}, bf16[2,8,16,768]{3,2,1,0:T(8,128)(2,1)S(1)}, u32[]{:S(2)}, u32[]{:S(2)}) collective-permute-start(bf16[2,8,16,768]{3,2,1,0:T(8,128)(2,1)S(1)} %collective-permute-done.1.refs_2_.refs_10_), channel_id=1, source_target_pairs={{0,8},{2,10},{8,12},{10,14},{12,4},{14,6},{4,0},{6,2},{1,9},{3,11}... | collective-permute-start | bytes 1179656 | tf_op jit(solution)/shard_map/ppermute | solution.py:32
  32.6 0.0 collective-permute-start.8
  32.6 0.7 collective-permute-start.2
  33.3 8.9 %collective-permute-done.4.refs_4_.refs_12_ = bf16[2,8,16,768]{3,2,1,0:T(8,128)(2,1)S(1)} collective-permute-done((bf16[2,8,16,768]{3,2,1,0:T(8,128)(2,1)S(1)}, bf16[2,8,16,768]{3,2,1,0:T(8,128)(2,1)S(1)}, u32[]{:S(2)}, u32[]{:S(2)}) %collective-permute-start.4) | collective-permute-done | bytes 393248 | tf_op jit(solution)/shard_map/ppermute | solution.py:32
  42.2 0.0 collective-permute-done.8.refs_3_.refs_11_
  42.2 3.4 %collective-permute-start.9 = (bf16[2,8,16,768]{3,2,1,0:T(8,128)(2,1)S(1)}, bf16[2,8,16,768]{3,2,1,0:T(8,128)(2,1)}, u32[]{:S(2)}, u32[]{:S(2)}) collective-permute-start(bf16[2,8,16,768]{3,2,1,0:T(8,128)(2,1)S(1)} %collective-permute-done.4.refs_4_.refs_12_), channel_id=1, source_target_pairs={{0,8},{2,10},{8,12},{10,14},{12,4},{14,6},{4,0},{6,2},{1,9},{3,11}... | collective-permute-start | bytes 1179656 | tf_op jit(solution)/shard_map/ppermute | solution.py:32
  45.6 4.6 %collective-permute-done.2.refs_2_ = bf16[16,16,768]{2,1,0:T(8,128)(2,1)} collective-permute-done((bf16[16,16,768]{2,1,0:T(8,128)(2,1)}, bf16[16,16,768]{2,1,0:T(8,128)(2,1)}, u32[]{:S(2)}, u32[]{:S(2)}) %collective-permute-start.2) | collective-permute-done | bytes 393248 | tf_op jit(solution)/shard_map/ppermute | solution.py:32
  50.3 0.7 copy-done.11
  51.0 3.4 %collective-permute-start.6 = (bf16[2,8,16,768]{3,2,1,0:T(8,128)(2,1)}, bf16[2,8,16,768]{3,2,1,0:T(8,128)(2,1)S(1)}, u32[]{:S(2)}, u32[]{:S(2)}) collective-permute-start(bf16[2,8,16,768]{3,2,1,0:T(8,128)(2,1)} %get-tuple-element.33.refs_0_.refs_8_), channel_id=1, source_target_pairs={{0,8},{2,10},{8,12},{10,14},{12,4},{14,6},{4,0},{6,2},{1,9},{3,11}... | collective-permute-start | bytes 1179656 | tf_op jit(solution)/shard_map/ppermute | solution.py:32
  54.4 3.6 %collective-permute-done.9.refs_6_.refs_14_ = bf16[2,8,16,768]{3,2,1,0:T(8,128)(2,1)} collective-permute-done((bf16[2,8,16,768]{3,2,1,0:T(8,128)(2,1)S(1)}, bf16[2,8,16,768]{3,2,1,0:T(8,128)(2,1)}, u32[]{:S(2)}, u32[]{:S(2)}) %collective-permute-start.9) | collective-permute-done | bytes 393248 | tf_op jit(solution)/shard_map/ppermute | solution.py:32
  58.0 3.5 %collective-permute-start.11 = (bf16[16,16,768]{2,1,0:T(8,128)(2,1)}, bf16[16,16,768]{2,1,0:T(8,128)(2,1)}, u32[]{:S(2)}, u32[]{:S(2)}) collective-permute-start(bf16[16,16,768]{2,1,0:T(8,128)(2,1)} %collective-permute-done.2.refs_2_), channel_id=1, source_target_pairs={{0,8},{2,10},{8,12},{10,14},{12,4},{14,6},{4,0},{6,2},{1,9},{3,11}... | collective-permute-start | bytes 1179656 | tf_op jit(solution)/shard_map/ppermute | solution.py:32
  61.5 5.0 %collective-permute-done.6.refs_2_.refs_10_ = bf16[2,8,16,768]{3,2,1,0:T(8,128)(2,1)S(1)} collective-permute-done((bf16[2,8,16,768]{3,2,1,0:T(8,128)(2,1)}, bf16[2,8,16,768]{3,2,1,0:T(8,128)(2,1)S(1)}, u32[]{:S(2)}, u32[]{:S(2)}) %collective-permute-start.6) | collective-permute-done | bytes 393248 | tf_op jit(solution)/shard_map/ppermute | solution.py:32
  66.5 0.0 collective-permute-start.7
  66.5 0.0 collective-permute-done.14.refs_7_.refs_15_
  66.6 1.1 copy-done.1
  67.7 5.6 %shard_map.83 = bf16[8,16,6144]{2,1,0:T(8,128)(2,1)} custom-call(s32[1]{0:T(128)} %bitcast.me_ref, bf16[32,16,6144]{2,1,0:T(8,128)(2,1)} %bitcast.19, bf16[1,6144]{1,0:T(2,128)(2,1)} %gain_ref.7, bf16[2,8,16,768]{3,2,1,0:T(8,128)(2,1)} %get-tuple-element.30.refs_0_.refs_8_, bf16[2,32,16,768]{3,2,1,0:T(8,128)(2,1)} %copy-done.1, ...), custom_call_target="tpu_custom_call" | custom-call | flops 1 | bytes 1 | tf_op jit(solution)/shard_map/pallas_call | solution.py:313
  73.3 0.3 collective-permute-done.11.refs_4_
  73.6 3.4 %collective-permute-start.15 = (bf16[16,16,768]{2,1,0:T(8,128)(2,1)}, bf16[16,16,768]{2,1,0:T(8,128)(2,1)S(1)}, u32[]{:S(2)}, u32[]{:S(2)}) collective-permute-start(bf16[16,16,768]{2,1,0:T(8,128)(2,1)} %collective-permute-done.11.refs_4_), channel_id=1, source_target_pairs={{0,8},{2,10},{8,12},{10,14},{12,4},{14,6},{4,0},{6,2},{1,9},{3,11}... | collective-permute-start | bytes 1179656 | tf_op jit(solution)/shard_map/ppermute | solution.py:32
  77.0 0.2 collective-permute-start.12
  77.2 0.5 collective-permute-start.21
  77.7 9.0 %collective-permute-done.15.refs_6_ = bf16[16,16,768]{2,1,0:T(8,128)(2,1)S(1)} collective-permute-done((bf16[16,16,768]{2,1,0:T(8,128)(2,1)}, bf16[16,16,768]{2,1,0:T(8,128)(2,1)S(1)}, u32[]{:S(2)}, u32[]{:S(2)}) %collective-permute-start.15) | collective-permute-done | bytes 393248 | tf_op jit(solution)/shard_map/ppermute | solution.py:32
  86.8 0.0 collective-permute-start.16
  86.8 0.0 collective-permute-done.13.refs_5_
  86.8 7.5 %collective-permute-done.12.refs_4_.refs_12_ = bf16[2,8,16,768]{3,2,1,0:T(8,128)(2,1)S(1)} collective-permute-done((bf16[2,8,16,768]{3,2,1,0:T(8,128)(2,1)S(1)}, bf16[2,8,16,768]{3,2,1,0:T(8,128)(2,1)S(1)}, u32[]{:S(2)}, u32[]{:S(2)}) %collective-permute-start.12) | collective-permute-done | bytes 393248 | tf_op jit(solution)/shard_map/ppermute | solution.py:32
  94.2 3.4 %collective-permute-start.18 = (bf16[2,8,16,768]{3,2,1,0:T(8,128)(2,1)S(1)}, bf16[2,8,16,768]{3,2,1,0:T(8,128)(2,1)S(1)}, u32[]{:S(2)}, u32[]{:S(2)}) collective-permute-start(bf16[2,8,16,768]{3,2,1,0:T(8,128)(2,1)S(1)} %collective-permute-done.12.refs_4_.refs_12_), channel_id=1, source_target_pairs={{0,8},{2,10},{8,12},{10,14},{12,4},{14,6},{4,0},{6,2},{1,9},{3,11}... | collective-permute-start | bytes 1179656 | tf_op jit(solution)/shard_map/ppermute | solution.py:32
  97.6 0.7 copy-done.26
  98.4 6.5 %shard_map.84.refs_16_ = bf16[1,16,256]{2,1,0:T(8,128)(2,1)} custom-call(s32[1]{0:T(128)} %bitcast.me_ref, bf16[32,16,6144]{2,1,0:T(8,128)(2,1)} %bitcast.20, bf16[1,6144]{1,0:T(2,128)(2,1)} %gain_ref.7, bf16[16,16,768]{2,1,0:T(8,128)(2,1)} %get-tuple-element.31.refs_0_, bf16[2,32,16,768]{3,2,1,0:T(8,128)(2,1)} %copy-done.1, ...), custom_call_target="tpu_custom_call" | custom-call | flops 1 | bytes 1 | tf_op jit(solution)/shard_map/pallas_call | solution.py:340
  104.9 1.0 slice.12
  106.0 0.1 collective-permute-start.26
  106.1 0.5 collective-permute-start.20
  106.7 0.1 collective-permute-start.19
  106.7 1.0 collective-permute-done.20.refs_15_
  107.7 0.4 collective-permute-done.19.refs_7_
  108.1 0.3 copy-done.12
  108.4 0.7 copy-done.13
  109.1 4.1 %shard_map.86 = bf16[4,16,6272]{2,1,0:T(8,128)(2,1)} custom-call(s32[1]{0:T(128)} %bitcast.me_ref, bf16[32,16,6144]{2,1,0:T(8,128)(2,1)} %bitcast.21, bf16[1,6144]{1,0:T(2,128)(2,1)} %gain_ref.7, bf16[2,8,16,768]{3,2,1,0:T(8,128)(2,1)} %get-tuple-element.33.refs_0_.refs_8_, bf16[2,32,16,768]{3,2,1,0:T(8,128)(2,1)} %copy-done.1, ...), custom_call_target="tpu_custom_call" | custom-call | flops 1 | bytes 1 | tf_op jit(solution)/shard_map/pallas_call | solution.py:313
  113.2 0.6 collective-permute-start.24
  113.7 3.8 %collective-permute-done.26.refs_2_ = bf16[16,16,768]{2,1,0:T(8,128)(2,1)S(1)} collective-permute-done((bf16[16,16,768]{2,1,0:T(8,128)(2,1)S(1)}, bf16[16,16,768]{2,1,0:T(8,128)(2,1)S(1)}, u32[]{:S(2)}, u32[]{:S(2)}) %collective-permute-start.26) | collective-permute-done | bytes 393248 | tf_op jit(solution)/shard_map/ppermute | solution.py:32
  117.5 1.2 collective-permute-start.28
  118.7 4.0 %shard_map.85 = bf16[4,16,6144]{2,1,0:T(8,128)(2,1)} custom-call(s32[1]{0:T(128)} %bitcast.me_ref, bf16[32,16,6144]{2,1,0:T(8,128)(2,1)} %bitcast.22, bf16[1,6144]{1,0:T(2,128)(2,1)} %gain_ref.7, bf16[2,8,16,768]{3,2,1,0:T(8,128)(2,1)} %get-tuple-element.33.refs_0_.refs_8_, bf16[2,32,16,768]{3,2,1,0:T(8,128)(2,1)} %copy-done.1, ...), custom_call_target="tpu_custom_call" | custom-call | flops 1 | bytes 1 | tf_op jit(solution)/shard_map/pallas_call | solution.py:313
  122.8 1.2 shard_map.87.refs_0_
  123.9 4.3 %collective-permute-done.28.refs_4_ = bf16[16,16,768]{2,1,0:T(8,128)(2,1)S(1)} collective-permute-done((bf16[16,16,768]{2,1,0:T(8,128)(2,1)S(1)}, bf16[16,16,768]{2,1,0:T(8,128)(2,1)S(1)}, u32[]{:S(2)}, u32[]{:S(2)}) %collective-permute-start.28) | collective-permute-done | bytes 393248 | tf_op jit(solution)/shard_map/ppermute | solution.py:32
  128.3 2.2 %collective-permute-start.30 = (bf16[16,16,768]{2,1,0:T(8,128)(2,1)S(1)}, bf16[16,16,768]{2,1,0:T(8,128)(2,1)S(1)}, u32[]{:S(2)}, u32[]{:S(2)}) collective-permute-start(bf16[16,16,768]{2,1,0:T(8,128)(2,1)S(1)} %collective-permute-done.28.refs_4_), channel_id=1, source_target_pairs={{0,8},{2,10},{8,12},{10,14},{12,4},{14,6},{4,0},{6,2},{1,9},{3,11}... | collective-permute-start | bytes 1179656 | tf_op jit(solution)/shard_map/ppermute | solution.py:32
  130.5 0.5 collective-permute-start.22
  131.1 0.5 collective-permute-start.27
  131.6 6.5 %collective-permute-done.30.refs_6_ = bf16[16,16,768]{2,1,0:T(8,128)(2,1)S(1)} collective-permute-done((bf16[16,16,768]{2,1,0:T(8,128)(2,1)S(1)}, bf16[16,16,768]{2,1,0:T(8,128)(2,1)S(1)}, u32[]{:S(2)}, u32[]{:S(2)}) %collective-permute-start.30) | collective-permute-done | bytes 393248 | tf_op jit(solution)/shard_map/ppermute | solution.py:32
  138.1 0.5 collective-permute-start.31
  138.6 0.9 shard_map.88.refs_8_
  139.6 0.2 collective-permute-done.29.refs_5_
  139.8 0.6 collective-permute-done.31.refs_7_
  140.4 0.1 copy-done.22
  140.5 0.1 copy-done.24
  140.6 0.8 copy-done.25
  141.4 6.2 %shard_map.89.refs_0_ = bf16[32,16,6144]{2,1,0:T(8,128)(2,1)} custom-call(s32[1]{0:T(128)} %bitcast.me_ref, bf16[14,16,6144]{2,1,0:T(8,128)(2,1)} %collective-permute-done.23.carrier_ref, bf16[4,16,6144]{2,1,0:T(8,128)(2,1)} %copy-done.14, bf16[4,16,6272]{2,1,0:T(8,128)(2,1)} %copy-done, ...), custom_call_target="tpu_custom_call", output_to_operand_aliasing={{}: (12, {})} | custom-call | flops 1 | bytes 1 | tf_op jit(solution)/shard_map/pallas_call | solution.py:365
  147.6 2.8 %collective-permute-done.22.block_ref = bf16[4,16,6144]{2,1,0:T(8,128)(2,1)S(1)} collective-permute-done((bf16[4,16,6144]{2,1,0:T(8,128)(2,1)S(1)}, bf16[4,16,6144]{2,1,0:T(8,128)(2,1)S(1)}, u32[]{:S(2)}, u32[]{:S(2)}) %collective-permute-start.22) | collective-permute-done | bytes 786464 | tf_op jit(solution)/shard_map/ppermute | solution.py:19
  150.4 0.9 shard_map.90
  (67 shorter events, 0.2 us)
Async XLA Ops:
  1.2 28.1 %collective-permute-start.3 = (bf16[4,16,6144]{2,1,0:T(8,128)(2,1)S(1)}, bf16[4,16,6144]{2,1,0:T(8,128)(2,1)S(1)}, u32[]{:S(2)}, u32[]{:S(2)}) collective-permute-start(bf16[4,16,6144]{2,1,0:T(8,128)(2,1)S(1)} %slice_bitcast_fusion), channel_id=1, source_target_pairs={{1,0},{0,1},{3,2},{2,3},{5,4},{4,5},{7,6},{6,7},{9,8},{8,9},{11,10... | collective-permute-start | bytes 2359304 | tf_op jit(solution)/shard_map/ppermute | solution.py:19
  18.2 11.0 %collective-permute-start.1 = (bf16[2,8,16,768]{3,2,1,0:T(8,128)(2,1)}, bf16[2,8,16,768]{3,2,1,0:T(8,128)(2,1)S(1)}, u32[]{:S(2)}, u32[]{:S(2)}) collective-permute-start(bf16[2,8,16,768]{3,2,1,0:T(8,128)(2,1)} %get-tuple-element.30.refs_0_.refs_8_), channel_id=1, source_target_pairs={{0,8},{2,10},{8,12},{10,14},{12,4},{14,6},{4,0},{6,2},{1,9},{3,11}... | collective-permute-start | bytes 1179656 | tf_op jit(solution)/shard_map/ppermute | solution.py:32
  20.8 84.0 %collective-permute-start.23 = (bf16[14,16,6144]{2,1,0:T(8,128)(2,1)}, bf16[14,16,6144]{2,1,0:T(8,128)(2,1)}, u32[]{:S(2)}, u32[]{:S(2)}) collective-permute-start(bf16[14,16,6144]{2,1,0:T(8,128)(2,1)} %get-tuple-element.42), channel_id=1, source_target_pairs={{1,0},{0,1},{3,2},{2,3},{5,4},{4,5},{7,6},{6,7},{9,8},{8,9},{11,10... | collective-permute-start | bytes 8257544 | tf_op jit(solution)/shard_map/ppermute | solution.py:19
  21.4 45.1 %collective-permute-start = (bf16[2,32,16,768]{3,2,1,0:T(8,128)(2,1)}, bf16[2,32,16,768]{3,2,1,0:T(8,128)(2,1)S(1)}, u32[]{:S(2)}, u32[]{:S(2)}) collective-permute-start(bf16[2,32,16,768]{3,2,1,0:T(8,128)(2,1)} %get-tuple-element.28), channel_id=1, source_target_pairs={{0,2},{2,0},{4,6},{6,4},{8,10},{10,8},{12,14},{14,12},{1,3},{3,1},... | collective-permute-start | bytes 4718600 | tf_op jit(solution)/shard_map/ppermute | solution.py:37
  29.2 37.3 %copy-start.8 = (bf16[2,8,16,768]{3,2,1,0:T(8,128)(2,1)}, bf16[2,8,16,768]{3,2,1,0:T(8,128)(2,1)S(1)}, u32[]{:S(2)}) copy-start(bf16[2,8,16,768]{3,2,1,0:T(8,128)(2,1)S(1)} %collective-permute-done.1.refs_2_.refs_10_) | copy-start | bytes 1179652
  29.3 37.2 %copy-start.14 = (bf16[4,16,6144]{2,1,0:T(8,128)(2,1)}, bf16[4,16,6144]{2,1,0:T(8,128)(2,1)S(1)}, u32[]{:S(2)}) copy-start(bf16[4,16,6144]{2,1,0:T(8,128)(2,1)S(1)} %collective-permute-done.3.early_ref) | copy-start | bytes 2359300
  29.3 12.9 %collective-permute-start.4 = (bf16[2,8,16,768]{3,2,1,0:T(8,128)(2,1)S(1)}, bf16[2,8,16,768]{3,2,1,0:T(8,128)(2,1)S(1)}, u32[]{:S(2)}, u32[]{:S(2)}) collective-permute-start(bf16[2,8,16,768]{3,2,1,0:T(8,128)(2,1)S(1)} %collective-permute-done.1.refs_2_.refs_10_), channel_id=1, source_target_pairs={{0,8},{2,10},{8,12},{10,14},{12,4},{14,6},{4,0},{6,2},{1,9},{3,11}... | collective-permute-start | bytes 1179656 | tf_op jit(solution)/shard_map/ppermute | solution.py:32
  32.6 9.6 %collective-permute-start.8 = (bf16[2,8,16,768]{3,2,1,0:T(8,128)(2,1)S(1)}, bf16[2,8,16,768]{3,2,1,0:T(8,128)(2,1)S(1)}, u32[]{:S(2)}, u32[]{:S(2)}) collective-permute-start(bf16[2,8,16,768]{3,2,1,0:T(8,128)(2,1)S(1)} %collective-permute-done.1.refs_2_.refs_10_), channel_id=1, source_target_pairs={{0,2},{2,0},{4,6},{6,4},{8,10},{10,8},{12,14},{14,12},{1,3},{3,1},... | collective-permute-start | bytes 1179656 | tf_op jit(solution)/shard_map/ppermute | solution.py:37
  32.6 17.7 %collective-permute-start.2 = (bf16[16,16,768]{2,1,0:T(8,128)(2,1)}, bf16[16,16,768]{2,1,0:T(8,128)(2,1)}, u32[]{:S(2)}, u32[]{:S(2)}) collective-permute-start(bf16[16,16,768]{2,1,0:T(8,128)(2,1)} %get-tuple-element.31.refs_0_), channel_id=1, source_target_pairs={{0,8},{2,10},{8,12},{10,14},{12,4},{14,6},{4,0},{6,2},{1,9},{3,11}... | collective-permute-start | bytes 1179656 | tf_op jit(solution)/shard_map/ppermute | solution.py:32
  42.1 24.4 %copy-start.9 = (bf16[2,8,16,768]{3,2,1,0:T(8,128)(2,1)}, bf16[2,8,16,768]{3,2,1,0:T(8,128)(2,1)S(1)}, u32[]{:S(2)}) copy-start(bf16[2,8,16,768]{3,2,1,0:T(8,128)(2,1)S(1)} %collective-permute-done.4.refs_4_.refs_12_) | copy-start | bytes 1179652
  42.2 8.1 %collective-permute-start.5 = (bf16[2,8,16,768]{3,2,1,0:T(8,128)(2,1)S(1)}, bf16[2,8,16,768]{3,2,1,0:T(8,128)(2,1)S(1)}, u32[]{:S(2)}, u32[]{:S(2)}) collective-permute-start(bf16[2,8,16,768]{3,2,1,0:T(8,128)(2,1)S(1)} %collective-permute-done.4.refs_4_.refs_12_), channel_id=1, source_target_pairs={{0,2},{2,0},{4,6},{6,4},{8,10},{10,8},{12,14},{14,12},{1,3},{3,1},... | collective-permute-start | bytes 1179656 | tf_op jit(solution)/shard_map/ppermute | solution.py:37
  42.2 24.4 %copy-start.10 = (bf16[2,8,16,768]{3,2,1,0:T(8,128)(2,1)}, bf16[2,8,16,768]{3,2,1,0:T(8,128)(2,1)S(1)}, u32[]{:S(2)}) copy-start(bf16[2,8,16,768]{3,2,1,0:T(8,128)(2,1)S(1)} %collective-permute-done.8.refs_3_.refs_11_) | copy-start | bytes 1179652
  42.2 15.8 %collective-permute-start.9 = (bf16[2,8,16,768]{3,2,1,0:T(8,128)(2,1)S(1)}, bf16[2,8,16,768]{3,2,1,0:T(8,128)(2,1)}, u32[]{:S(2)}, u32[]{:S(2)}) collective-permute-start(bf16[2,8,16,768]{3,2,1,0:T(8,128)(2,1)S(1)} %collective-permute-done.4.refs_4_.refs_12_), channel_id=1, source_target_pairs={{0,8},{2,10},{8,12},{10,14},{12,4},{14,6},{4,0},{6,2},{1,9},{3,11}... | collective-permute-start | bytes 1179656 | tf_op jit(solution)/shard_map/ppermute | solution.py:32
  50.3 7.7 %collective-permute-start.10 = (bf16[16,16,768]{2,1,0:T(8,128)(2,1)}, bf16[16,16,768]{2,1,0:T(8,128)(2,1)S(1)}, u32[]{:S(2)}, u32[]{:S(2)}) collective-permute-start(bf16[16,16,768]{2,1,0:T(8,128)(2,1)} %collective-permute-done.2.refs_2_), channel_id=1, source_target_pairs={{0,2},{2,0},{4,6},{6,4},{8,10},{10,8},{12,14},{14,12},{1,3},{3,1},... | collective-permute-start | bytes 1179656 | tf_op jit(solution)/shard_map/ppermute | solution.py:37
  50.3 0.8 copy-start.11
  51.0 15.5 %collective-permute-start.6 = (bf16[2,8,16,768]{3,2,1,0:T(8,128)(2,1)}, bf16[2,8,16,768]{3,2,1,0:T(8,128)(2,1)S(1)}, u32[]{:S(2)}, u32[]{:S(2)}) collective-permute-start(bf16[2,8,16,768]{3,2,1,0:T(8,128)(2,1)} %get-tuple-element.33.refs_0_.refs_8_), channel_id=1, source_target_pairs={{0,8},{2,10},{8,12},{10,14},{12,4},{14,6},{4,0},{6,2},{1,9},{3,11}... | collective-permute-start | bytes 1179656 | tf_op jit(solution)/shard_map/ppermute | solution.py:32
  57.9 8.6 %collective-permute-start.14 = (bf16[2,8,16,768]{3,2,1,0:T(8,128)(2,1)}, bf16[2,8,16,768]{3,2,1,0:T(8,128)(2,1)}, u32[]{:S(2)}, u32[]{:S(2)}) collective-permute-start(bf16[2,8,16,768]{3,2,1,0:T(8,128)(2,1)} %collective-permute-done.9.refs_6_.refs_14_), channel_id=1, source_target_pairs={{0,2},{2,0},{4,6},{6,4},{8,10},{10,8},{12,14},{14,12},{1,3},{3,1},... | collective-permute-start | bytes 1179656 | tf_op jit(solution)/shard_map/ppermute | solution.py:37
  58.0 8.5 %copy-start.17 = (bf16[16,16,768]{2,1,0:T(8,128)(2,1)}, bf16[16,16,768]{2,1,0:T(8,128)(2,1)S(1)}, u32[]{:S(2)}) copy-start(bf16[16,16,768]{2,1,0:T(8,128)(2,1)S(1)} %collective-permute-done.10.refs_3_) | copy-start | bytes 1179652
  58.0 15.6 %collective-permute-start.11 = (bf16[16,16,768]{2,1,0:T(8,128)(2,1)}, bf16[16,16,768]{2,1,0:T(8,128)(2,1)}, u32[]{:S(2)}, u32[]{:S(2)}) collective-permute-start(bf16[16,16,768]{2,1,0:T(8,128)(2,1)} %collective-permute-done.2.refs_2_), channel_id=1, source_target_pairs={{0,8},{2,10},{8,12},{10,14},{12,4},{14,6},{4,0},{6,2},{1,9},{3,11}... | collective-permute-start | bytes 1179656 | tf_op jit(solution)/shard_map/ppermute | solution.py:32
  66.5 41.6 %copy-start.3 = (bf16[2,8,16,768]{3,2,1,0:T(8,128)(2,1)}, bf16[2,8,16,768]{3,2,1,0:T(8,128)(2,1)S(1)}, u32[]{:S(2)}) copy-start(bf16[2,8,16,768]{3,2,1,0:T(8,128)(2,1)S(1)} %collective-permute-done.6.refs_2_.refs_10_) | copy-start | bytes 1179652
  66.5 10.5 %collective-permute-start.7 = (bf16[2,8,16,768]{3,2,1,0:T(8,128)(2,1)S(1)}, bf16[2,8,16,768]{3,2,1,0:T(8,128)(2,1)S(1)}, u32[]{:S(2)}, u32[]{:S(2)}) collective-permute-start(bf16[2,8,16,768]{3,2,1,0:T(8,128)(2,1)S(1)} %collective-permute-done.6.refs_2_.refs_10_), channel_id=1, source_target_pairs={{0,2},{2,0},{4,6},{6,4},{8,10},{10,8},{12,14},{14,12},{1,3},{3,1},... | collective-permute-start | bytes 1179656 | tf_op jit(solution)/shard_map/ppermute | solution.py:37
  66.5 1.2 copy-start.1
  73.6 13.2 %collective-permute-start.15 = (bf16[16,16,768]{2,1,0:T(8,128)(2,1)}, bf16[16,16,768]{2,1,0:T(8,128)(2,1)S(1)}, u32[]{:S(2)}, u32[]{:S(2)}) collective-permute-start(bf16[16,16,768]{2,1,0:T(8,128)(2,1)} %collective-permute-done.11.refs_4_), channel_id=1, source_target_pairs={{0,8},{2,10},{8,12},{10,14},{12,4},{14,6},{4,0},{6,2},{1,9},{3,11}... | collective-permute-start | bytes 1179656 | tf_op jit(solution)/shard_map/ppermute | solution.py:32
  77.0 9.8 %collective-permute-start.13 = (bf16[16,16,768]{2,1,0:T(8,128)(2,1)}, bf16[16,16,768]{2,1,0:T(8,128)(2,1)S(1)}, u32[]{:S(2)}, u32[]{:S(2)}) collective-permute-start(bf16[16,16,768]{2,1,0:T(8,128)(2,1)} %collective-permute-done.11.refs_4_), channel_id=1, source_target_pairs={{0,2},{2,0},{4,6},{6,4},{8,10},{10,8},{12,14},{14,12},{1,3},{3,1},... | collective-permute-start | bytes 1179656 | tf_op jit(solution)/shard_map/ppermute | solution.py:37
  77.0 29.1 %copy-start.4 = (bf16[2,8,16,768]{3,2,1,0:T(8,128)(2,1)}, bf16[2,8,16,768]{3,2,1,0:T(8,128)(2,1)S(1)}, u32[]{:S(2)}) copy-start(bf16[2,8,16,768]{3,2,1,0:T(8,128)(2,1)S(1)} %collective-permute-done.7.refs_3_.refs_11_) | copy-start | bytes 1179652
  77.0 17.3 %collective-permute-start.12 = (bf16[2,8,16,768]{3,2,1,0:T(8,128)(2,1)S(1)}, bf16[2,8,16,768]{3,2,1,0:T(8,128)(2,1)S(1)}, u32[]{:S(2)}, u32[]{:S(2)}) collective-permute-start(bf16[2,8,16,768]{3,2,1,0:T(8,128)(2,1)S(1)} %collective-permute-done.6.refs_2_.refs_10_), channel_id=1, source_target_pairs={{0,8},{2,10},{8,12},{10,14},{12,4},{14,6},{4,0},{6,2},{1,9},{3,11}... | collective-permute-start | bytes 1179656 | tf_op jit(solution)/shard_map/ppermute | solution.py:32
  77.2 45.6 %collective-permute-start.21 = (bf16[8,16,6144]{2,1,0:T(8,128)(2,1)}, bf16[8,16,6144]{2,1,0:T(8,128)(2,1)S(1)}, u32[]{:S(2)}, u32[]{:S(2)}) collective-permute-start(bf16[8,16,6144]{2,1,0:T(8,128)(2,1)} %shard_map.83), channel_id=1, source_target_pairs={{1,0},{0,1},{3,2},{2,3},{5,4},{4,5},{7,6},{6,7},{9,8},{8,9},{11,10... | collective-permute-start | bytes 4718600 | tf_op jit(solution)/shard_map/ppermute | solution.py:19
  86.8 10.9 %copy-start.21 = (bf16[16,16,768]{2,1,0:T(8,128)(2,1)}, bf16[16,16,768]{2,1,0:T(8,128)(2,1)S(1)}, u32[]{:S(2)}) copy-start(bf16[16,16,768]{2,1,0:T(8,128)(2,1)S(1)} %collective-permute-done.15.refs_6_) | copy-start | bytes 1179652
  86.8 10.9 %collective-permute-start.16 = (bf16[16,16,768]{2,1,0:T(8,128)(2,1)S(1)}, bf16[16,16,768]{2,1,0:T(8,128)(2,1)S(1)}, u32[]{:S(2)}, u32[]{:S(2)}) collective-permute-start(bf16[16,16,768]{2,1,0:T(8,128)(2,1)S(1)} %collective-permute-done.15.refs_6_), channel_id=1, source_target_pairs={{0,2},{2,0},{4,6},{6,4},{8,10},{10,8},{12,14},{14,12},{1,3},{3,1},... | collective-permute-start | bytes 1179656 | tf_op jit(solution)/shard_map/ppermute | solution.py:37
  86.8 10.9 %copy-start.23 = (bf16[16,16,768]{2,1,0:T(8,128)(2,1)}, bf16[16,16,768]{2,1,0:T(8,128)(2,1)S(1)}, u32[]{:S(2)}) copy-start(bf16[16,16,768]{2,1,0:T(8,128)(2,1)S(1)} %collective-permute-done.13.refs_5_) | copy-start | bytes 1179652
  94.2 11.9 %copy-start.5 = (bf16[2,8,16,768]{3,2,1,0:T(8,128)(2,1)}, bf16[2,8,16,768]{3,2,1,0:T(8,128)(2,1)S(1)}, u32[]{:S(2)}) copy-start(bf16[2,8,16,768]{3,2,1,0:T(8,128)(2,1)S(1)} %collective-permute-done.12.refs_4_.refs_12_) | copy-start | bytes 1179652
  94.2 11.8 %collective-permute-start.18 = (bf16[2,8,16,768]{3,2,1,0:T(8,128)(2,1)S(1)}, bf16[2,8,16,768]{3,2,1,0:T(8,128)(2,1)S(1)}, u32[]{:S(2)}, u32[]{:S(2)}) collective-permute-start(bf16[2,8,16,768]{3,2,1,0:T(8,128)(2,1)S(1)} %collective-permute-done.12.refs_4_.refs_12_), channel_id=1, source_target_pairs={{0,8},{2,10},{8,12},{10,14},{12,4},{14,6},{4,0},{6,2},{1,9},{3,11}... | collective-permute-start | bytes 1179656 | tf_op jit(solution)/shard_map/ppermute | solution.py:32
  97.6 0.7 copy-start.26
  104.9 1.9 %collective-permute-start.17 = (bf16[2,8,16,768]{3,2,1,0:T(8,128)(2,1)S(1)}, bf16[2,8,16,768]{3,2,1,0:T(8,128)(2,1)S(1)}, u32[]{:S(2)}, u32[]{:S(2)}) collective-permute-start(bf16[2,8,16,768]{3,2,1,0:T(8,128)(2,1)S(1)} %collective-permute-done.12.refs_4_.refs_12_), channel_id=1, source_target_pairs={{0,2},{2,0},{4,6},{6,4},{8,10},{10,8},{12,14},{14,12},{1,3},{3,1},... | collective-permute-start | bytes 1179656 | tf_op jit(solution)/shard_map/ppermute | solution.py:37
  105.9 25.1 %copy-start.7 = (bf16[2,2,8,8,768]{4,3,1,2,0:T(8,128)(2,1)}, bf16[2,2,8,8,768]{4,3,1,2,0:T(8,128)(2,1)S(1)}, u32[]{:S(2)}) copy-start(bf16[2,2,8,8,768]{4,3,1,2,0:T(8,128)(2,1)S(1)} %copy.15) | copy-start | bytes 1179652
  106.0 11.6 %collective-permute-start.26 = (bf16[16,16,768]{2,1,0:T(8,128)(2,1)S(1)}, bf16[16,16,768]{2,1,0:T(8,128)(2,1)S(1)}, u32[]{:S(2)}, u32[]{:S(2)}) collective-permute-start(bf16[16,16,768]{2,1,0:T(8,128)(2,1)S(1)} %bitcast.24), channel_id=1, source_target_pairs={{0,8},{2,10},{8,12},{10,14},{12,4},{14,6},{4,0},{6,2},{1,9},{3,11}... | collective-permute-start | bytes 1179656 | tf_op jit(solution)/shard_map/ppermute | solution.py:32
  106.1 2.0 %copy-start.2 = (bf16[2,8,16,768]{3,2,1,0:T(8,128)(2,1)}, bf16[2,8,16,768]{3,2,1,0:T(8,128)(2,1)S(1)}, u32[]{:S(2)}) copy-start(bf16[2,8,16,768]{3,2,1,0:T(8,128)(2,1)S(1)} %collective-permute-done.18.refs_6_.refs_14_) | copy-start | bytes 1179652
  106.1 1.6 %collective-permute-start.20 = (bf16[8,16,768]{2,1,0:T(8,128)(2,1)S(1)}, bf16[8,16,768]{2,1,0:T(8,128)(2,1)S(1)}, u32[]{:S(2)}, u32[]{:S(2)}) collective-permute-start(bf16[8,16,768]{2,1,0:T(8,128)(2,1)S(1)} %get-tuple-element.49), channel_id=1, source_target_pairs={{0,2},{2,0},{4,6},{6,4},{8,10},{10,8},{12,14},{14,12},{1,3},{3,1},... | collective-permute-start | bytes 589832 | tf_op jit(solution)/shard_map/ppermute | solution.py:37
  106.7 1.4 collective-permute-start.19
  106.7 1.4 copy-start.6
  107.7 0.7 copy-start.12
  108.4 0.7 copy-start.13
  113.2 25.0 %collective-permute-start.24 = (bf16[4,16,6272]{2,1,0:T(8,128)(2,1)}, bf16[4,16,6272]{2,1,0:T(8,128)(2,1)S(1)}, u32[]{:S(2)}, u32[]{:S(2)}) collective-permute-start(bf16[4,16,6272]{2,1,0:T(8,128)(2,1)} %shard_map.86), channel_id=1, source_target_pairs={{1,0},{0,1},{3,2},{2,3},{5,4},{4,5},{7,6},{6,7},{9,8},{8,9},{11,10... | collective-permute-start | bytes 2408456 | tf_op jit(solution)/shard_map/ppermute | solution.py:19
  117.5 13.5 %copy-start.16 = (bf16[16,16,768]{2,1,0:T(8,128)(2,1)}, bf16[16,16,768]{2,1,0:T(8,128)(2,1)S(1)}, u32[]{:S(2)}) copy-start(bf16[16,16,768]{2,1,0:T(8,128)(2,1)S(1)} %collective-permute-done.26.refs_2_) | copy-start | bytes 1179652
  117.5 10.7 %collective-permute-start.28 = (bf16[16,16,768]{2,1,0:T(8,128)(2,1)S(1)}, bf16[16,16,768]{2,1,0:T(8,128)(2,1)S(1)}, u32[]{:S(2)}, u32[]{:S(2)}) collective-permute-start(bf16[16,16,768]{2,1,0:T(8,128)(2,1)S(1)} %collective-permute-done.26.refs_2_), channel_id=1, source_target_pairs={{0,8},{2,10},{8,12},{10,14},{12,4},{14,6},{4,0},{6,2},{1,9},{3,11}... | collective-permute-start | bytes 1179656 | tf_op jit(solution)/shard_map/ppermute | solution.py:32
  122.8 7.8 %copy-start.15 = (bf16[4,16,6144]{2,1,0:T(8,128)(2,1)S(1)}, bf16[4,16,6144]{2,1,0:T(8,128)(2,1)}, u32[]{:S(2)}) copy-start(bf16[4,16,6144]{2,1,0:T(8,128)(2,1)} %shard_map.85) | copy-start | bytes 2359300
  128.3 11.3 %copy-start.18 = (bf16[16,16,768]{2,1,0:T(8,128)(2,1)}, bf16[16,16,768]{2,1,0:T(8,128)(2,1)S(1)}, u32[]{:S(2)}) copy-start(bf16[16,16,768]{2,1,0:T(8,128)(2,1)S(1)} %collective-permute-done.28.refs_4_) | copy-start | bytes 1179652
  128.3 9.8 %collective-permute-start.30 = (bf16[16,16,768]{2,1,0:T(8,128)(2,1)S(1)}, bf16[16,16,768]{2,1,0:T(8,128)(2,1)S(1)}, u32[]{:S(2)}, u32[]{:S(2)}) collective-permute-start(bf16[16,16,768]{2,1,0:T(8,128)(2,1)S(1)} %collective-permute-done.28.refs_4_), channel_id=1, source_target_pairs={{0,8},{2,10},{8,12},{10,14},{12,4},{14,6},{4,0},{6,2},{1,9},{3,11}... | collective-permute-start | bytes 1179656 | tf_op jit(solution)/shard_map/ppermute | solution.py:32
  130.5 19.9 %collective-permute-start.22 = (bf16[4,16,6144]{2,1,0:T(8,128)(2,1)S(1)}, bf16[4,16,6144]{2,1,0:T(8,128)(2,1)S(1)}, u32[]{:S(2)}, u32[]{:S(2)}) collective-permute-start(bf16[4,16,6144]{2,1,0:T(8,128)(2,1)S(1)} %copy-done.15), channel_id=1, source_target_pairs={{1,0},{0,1},{3,2},{2,3},{5,4},{4,5},{7,6},{6,7},{9,8},{8,9},{11,10... | collective-permute-start | bytes 2359304 | tf_op jit(solution)/shard_map/ppermute | solution.py:19
  131.1 8.5 %collective-permute-start.25 = (bf16[16,16,768]{2,1,0:T(8,128)(2,1)S(1)}, bf16[16,16,768]{2,1,0:T(8,128)(2,1)S(1)}, u32[]{:S(2)}, u32[]{:S(2)}) collective-permute-start(bf16[16,16,768]{2,1,0:T(8,128)(2,1)S(1)} %bitcast.25), channel_id=1, source_target_pairs={{0,2},{2,0},{4,6},{6,4},{8,10},{10,8},{12,14},{14,12},{1,3},{3,1},... | collective-permute-start | bytes 1179656 | tf_op jit(solution)/shard_map/ppermute | solution.py:37
  131.1 8.5 %collective-permute-start.27 = (bf16[16,16,768]{2,1,0:T(8,128)(2,1)S(1)}, bf16[16,16,768]{2,1,0:T(8,128)(2,1)S(1)}, u32[]{:S(2)}, u32[]{:S(2)}) collective-permute-start(bf16[16,16,768]{2,1,0:T(8,128)(2,1)S(1)} %collective-permute-done.26.refs_2_), channel_id=1, source_target_pairs={{0,2},{2,0},{4,6},{6,4},{8,10},{10,8},{12,14},{14,12},{1,3},{3,1},... | collective-permute-start | bytes 1179656 | tf_op jit(solution)/shard_map/ppermute | solution.py:37
  138.1 1.4 copy-start.19
  138.1 1.7 %collective-permute-start.29 = (bf16[16,16,768]{2,1,0:T(8,128)(2,1)S(1)}, bf16[16,16,768]{2,1,0:T(8,128)(2,1)S(1)}, u32[]{:S(2)}, u32[]{:S(2)}) collective-permute-start(bf16[16,16,768]{2,1,0:T(8,128)(2,1)S(1)} %collective-permute-done.28.refs_4_), channel_id=1, source_target_pairs={{0,2},{2,0},{4,6},{6,4},{8,10},{10,8},{12,14},{14,12},{1,3},{3,1},... | collective-permute-start | bytes 1179656 | tf_op jit(solution)/shard_map/ppermute | solution.py:37
  138.1 1.4 copy-start
  138.1 2.3 %collective-permute-start.31 = (bf16[16,16,768]{2,1,0:T(8,128)(2,1)S(1)}, bf16[16,16,768]{2,1,0:T(8,128)(2,1)S(1)}, u32[]{:S(2)}, u32[]{:S(2)}) collective-permute-start(bf16[16,16,768]{2,1,0:T(8,128)(2,1)S(1)} %collective-permute-done.30.refs_6_), channel_id=1, source_target_pairs={{0,2},{2,0},{4,6},{6,4},{8,10},{10,8},{12,14},{14,12},{1,3},{3,1},... | collective-permute-start | bytes 1179656 | tf_op jit(solution)/shard_map/ppermute | solution.py:37
  139.6 0.8 copy-start.20
  139.6 0.9 copy-start.22
  139.8 0.8 copy-start.24
  140.6 0.8 copy-start.25

commit v6 on v4

--- a/solution.py
+++ b/solution.py
@@ -490,8 +490,8 @@
     (at, end), (middle, last) = chunks[0], (chunks[1][0] + n_blocks // 8, n_blocks)
     result = None
     first.step()
-    first.step(early_sent)
-    downs.step()
+    first.step()
+    downs.step(early_sent)
     first.step()
     first_out = layer_blocks(me, rows, at, end - at, norm_gain, other, first.pieces, first.pieces, 0)
     first_sent = passed_along(tied(first_out, early_sent), "section", 1)

time: 152 us -> 152 us (level)
  no operation moved by 1% of the time
where the time goes in v6:
time: 152 us
  waiting for transfers between devices  66.2 us (44%)
  Pallas kernels  43.4 us (29%)
  starting transfers between devices  34.3 us (23%)
  local copies, waits for them, and re-layouts  7.38 us (5%)
    ppermute x12, waiting for transfers between devices, ring_step(): return lax.ppermute(block, 'expert', route)  60.9 us
    ppermute x12, starting transfers between devices, ring_step(): return lax.ppermute(block, 'expert', route)  27.5 us
    pallas_call x1, Pallas kernels, generated(): pl.pallas_call(functools.partial(generator_kernel, chunks, rank), out_sha...  14 us
    pallas_call x3, Pallas kernels, layer_blocks(): pl.pallas_call(functools.partial(layer_kernel, len(pieces) // 2, rank, wi...  13.7 us
    pallas_call x1, Pallas kernels, low_blocks(): pl.pallas_call(functools.partial(low_kernel, len(pieces), rank, width), o...  6.49 us
    pallas_call x1, Pallas kernels, update_blocks(): pl.pallas_call(functools.partial(update_kernel, n, rank), out_shape=jax.S...  6.26 us
    ppermute x5, starting transfers between devices, passed_along(): return lax.ppermute(block, axis, route)  5.15 us
    unnamed x54, local copies, waits for them, and re-layouts  5.12 us
  transfers between devices with their start and end apart: 32, of which 16 were waited for; matrix products, arithmetic and copies ran while one was open for 1% of the time, Pallas kernels for 28%

profile of v6, /device:TPU:0, one launch (start us, length us, event | category | flops | bytes accessed | tf_op | source)
XLA Modules:
  0.0 151.6 jit_solution(6720244855010113585)
XLA Ops:
  0.0 1.2 slice_bitcast_fusion
  1.2 3.0 %collective-permute-start.1 = (bf16[4,16,6144]{2,1,0:T(8,128)(2,1)S(1)}, bf16[4,16,6144]{2,1,0:T(8,128)(2,1)S(1)}, u32[]{:S(2)}, u32[]{:S(2)}) collective-permute-start(bf16[4,16,6144]{2,1,0:T(8,128)(2,1)S(1)} %slice_bitcast_fusion), channel_id=1, source_target_pairs={{1,0},{0,1},{3,2},{2,3},{5,4},{4,5},{7,6},{6,7},{9,8},{8,9},{11,10... | collective-permute-start | bytes 2359304 | tf_op jit(solution)/shard_map/ppermute | solution.py:19
  4.2 14.0 %shard_map.82 = (bf16[2,32,16,768]{3,2,1,0:T(8,128)(2,1)}, bf16[16,16,768]{2,1,0:T(8,128)(2,1)}, bf16[14,16,6144]{2,1,0:T(8,128)(2,1)}, bf16[2,8,16,768]{3,2,1,0:T(8,128)(2,1)}, bf16[2,8,16,768]{3,2,1,0:T(8,128)(2,1)}) custom-call(s32[32]{0:T(128)} %bitcast.27, s32[8]{0:T(128)} %bitcast.28, bf16[8,256]{1,0:T(8,128)(2,1)} %task_embed_ref.1, ...), custom_call_target="tpu_custom_call" | custom-call | flops 1 | bytes 1 | tf_op jit(solution)/shard_map/pallas_call | solution.py:136
  18.2 2.6 %collective-permute-start.2 = (bf16[2,8,16,768]{3,2,1,0:T(8,128)(2,1)}, bf16[2,8,16,768]{3,2,1,0:T(8,128)(2,1)S(1)}, u32[]{:S(2)}, u32[]{:S(2)}) collective-permute-start(bf16[2,8,16,768]{3,2,1,0:T(8,128)(2,1)} %get-tuple-element.29.refs_0_.refs_8_), channel_id=1, source_target_pairs={{0,8},{2,10},{8,12},{10,14},{12,4},{14,6},{4,0},{6,2},{1,9},{3,11}... | collective-permute-start | bytes 1179656 | tf_op jit(solution)/shard_map/ppermute | solution.py:32
  20.8 0.5 collective-permute-start.23
  21.4 7.9 %collective-permute-done.2.refs_2_.refs_10_ = bf16[2,8,16,768]{3,2,1,0:T(8,128)(2,1)S(1)} collective-permute-done((bf16[2,8,16,768]{3,2,1,0:T(8,128)(2,1)}, bf16[2,8,16,768]{3,2,1,0:T(8,128)(2,1)S(1)}, u32[]{:S(2)}, u32[]{:S(2)}) %collective-permute-start.2) | collective-permute-done | bytes 393248 | tf_op jit(solution)/shard_map/ppermute | solution.py:32
  29.3 3.3 %collective-permute-start.4 = (bf16[2,8,16,768]{3,2,1,0:T(8,128)(2,1)S(1)}, bf16[2,8,16,768]{3,2,1,0:T(8,128)(2,1)S(1)}, u32[]{:S(2)}, u32[]{:S(2)}) collective-permute-start(bf16[2,8,16,768]{3,2,1,0:T(8,128)(2,1)S(1)} %collective-permute-done.2.refs_2_.refs_10_), channel_id=1, source_target_pairs={{0,8},{2,10},{8,12},{10,14},{12,4},{14,6},{4,0},{6,2},{1,9},{3,11}... | collective-permute-start | bytes 1179656 | tf_op jit(solution)/shard_map/ppermute | solution.py:32
  32.5 0.0 collective-permute-start.8
  32.5 0.0 collective-permute-done.1.early_ref
  32.5 0.7 collective-permute-start.3
  33.3 8.8 %collective-permute-done.4.refs_4_.refs_12_ = bf16[2,8,16,768]{3,2,1,0:T(8,128)(2,1)S(1)} collective-permute-done((bf16[2,8,16,768]{3,2,1,0:T(8,128)(2,1)S(1)}, bf16[2,8,16,768]{3,2,1,0:T(8,128)(2,1)S(1)}, u32[]{:S(2)}, u32[]{:S(2)}) %collective-permute-start.4) | collective-permute-done | bytes 393248 | tf_op jit(solution)/shard_map/ppermute | solution.py:32
  42.1 0.0 collective-permute-start.5
  42.1 0.0 collective-permute-done.8.refs_3_.refs_11_
  42.1 3.4 %collective-permute-start.9 = (bf16[2,8,16,768]{3,2,1,0:T(8,128)(2,1)S(1)}, bf16[2,8,16,768]{3,2,1,0:T(8,128)(2,1)}, u32[]{:S(2)}, u32[]{:S(2)}) collective-permute-start(bf16[2,8,16,768]{3,2,1,0:T(8,128)(2,1)S(1)} %collective-permute-done.4.refs_4_.refs_12_), channel_id=1, source_target_pairs={{0,8},{2,10},{8,12},{10,14},{12,4},{14,6},{4,0},{6,2},{1,9},{3,11}... | collective-permute-start | bytes 1179656 | tf_op jit(solution)/shard_map/ppermute | solution.py:32
  45.6 4.6 %collective-permute-done.3.refs_2_ = bf16[16,16,768]{2,1,0:T(8,128)(2,1)} collective-permute-done((bf16[16,16,768]{2,1,0:T(8,128)(2,1)}, bf16[16,16,768]{2,1,0:T(8,128)(2,1)}, u32[]{:S(2)}, u32[]{:S(2)}) %collective-permute-start.3) | collective-permute-done | bytes 393248 | tf_op jit(solution)/shard_map/ppermute | solution.py:32
  50.2 0.7 copy-done.11
  51.0 3.4 %collective-permute-start.6 = (bf16[2,8,16,768]{3,2,1,0:T(8,128)(2,1)}, bf16[2,8,16,768]{3,2,1,0:T(8,128)(2,1)S(1)}, u32[]{:S(2)}, u32[]{:S(2)}) collective-permute-start(bf16[2,8,16,768]{3,2,1,0:T(8,128)(2,1)} %get-tuple-element.31.refs_0_.refs_8_), channel_id=1, source_target_pairs={{0,8},{2,10},{8,12},{10,14},{12,4},{14,6},{4,0},{6,2},{1,9},{3,11}... | collective-permute-start | bytes 1179656 | tf_op jit(solution)/shard_map/ppermute | solution.py:32
  54.3 3.6 %collective-permute-done.9.refs_6_.refs_14_ = bf16[2,8,16,768]{3,2,1,0:T(8,128)(2,1)} collective-permute-done((bf16[2,8,16,768]{3,2,1,0:T(8,128)(2,1)S(1)}, bf16[2,8,16,768]{3,2,1,0:T(8,128)(2,1)}, u32[]{:S(2)}, u32[]{:S(2)}) %collective-permute-start.9) | collective-permute-done | bytes 393248 | tf_op jit(solution)/shard_map/ppermute | solution.py:32
  57.9 3.5 %collective-permute-start.11 = (bf16[16,16,768]{2,1,0:T(8,128)(2,1)}, bf16[16,16,768]{2,1,0:T(8,128)(2,1)}, u32[]{:S(2)}, u32[]{:S(2)}) collective-permute-start(bf16[16,16,768]{2,1,0:T(8,128)(2,1)} %collective-permute-done.3.refs_2_), channel_id=1, source_target_pairs={{0,8},{2,10},{8,12},{10,14},{12,4},{14,6},{4,0},{6,2},{1,9},{3,11}... | collective-permute-start | bytes 1179656 | tf_op jit(solution)/shard_map/ppermute | solution.py:32
  61.4 5.0 %collective-permute-done.6.refs_2_.refs_10_ = bf16[2,8,16,768]{3,2,1,0:T(8,128)(2,1)S(1)} collective-permute-done((bf16[2,8,16,768]{3,2,1,0:T(8,128)(2,1)}, bf16[2,8,16,768]{3,2,1,0:T(8,128)(2,1)S(1)}, u32[]{:S(2)}, u32[]{:S(2)}) %collective-permute-start.6) | collective-permute-done | bytes 393248 | tf_op jit(solution)/shard_map/ppermute | solution.py:32
  66.5 0.0 collective-permute-done.refs_1_.refs_9_
  66.5 1.2 copy-done.1
  67.7 5.6 %shard_map.83 = bf16[8,16,6144]{2,1,0:T(8,128)(2,1)} custom-call(s32[1]{0:T(128)} %bitcast.me_ref, bf16[32,16,6144]{2,1,0:T(8,128)(2,1)} %bitcast.19, bf16[1,6144]{1,0:T(2,128)(2,1)} %gain_ref.7, bf16[2,8,16,768]{3,2,1,0:T(8,128)(2,1)} %get-tuple-element.29.refs_0_.refs_8_, bf16[2,32,16,768]{3,2,1,0:T(8,128)(2,1)} %copy-done.1, ...), custom_call_target="tpu_custom_call" | custom-call | flops 1 | bytes 1 | tf_op jit(solution)/shard_map/pallas_call | solution.py:313
  73.2 0.3 collective-permute-done.11.refs_4_
  73.5 3.4 %collective-permute-start.15 = (bf16[16,16,768]{2,1,0:T(8,128)(2,1)}, bf16[16,16,768]{2,1,0:T(8,128)(2,1)S(1)}, u32[]{:S(2)}, u32[]{:S(2)}) collective-permute-start(bf16[16,16,768]{2,1,0:T(8,128)(2,1)} %collective-permute-done.11.refs_4_), channel_id=1, source_target_pairs={{0,8},{2,10},{8,12},{10,14},{12,4},{14,6},{4,0},{6,2},{1,9},{3,11}... | collective-permute-start | bytes 1179656 | tf_op jit(solution)/shard_map/ppermute | solution.py:32
  76.9 0.2 collective-permute-start.12
  77.1 0.5 collective-permute-start.21
  77.7 9.0 %collective-permute-done.15.refs_6_ = bf16[16,16,768]{2,1,0:T(8,128)(2,1)S(1)} collective-permute-done((bf16[16,16,768]{2,1,0:T(8,128)(2,1)}, bf16[16,16,768]{2,1,0:T(8,128)(2,1)S(1)}, u32[]{:S(2)}, u32[]{:S(2)}) %collective-permute-start.15) | collective-permute-done | bytes 393248 | tf_op jit(solution)/shard_map/ppermute | solution.py:32
  86.7 0.0 collective-permute-done.13.refs_5_
  86.7 7.5 %collective-permute-done.12.refs_4_.refs_12_ = bf16[2,8,16,768]{3,2,1,0:T(8,128)(2,1)S(1)} collective-permute-done((bf16[2,8,16,768]{3,2,1,0:T(8,128)(2,1)S(1)}, bf16[2,8,16,768]{3,2,1,0:T(8,128)(2,1)S(1)}, u32[]{:S(2)}, u32[]{:S(2)}) %collective-permute-start.12) | collective-permute-done | bytes 393248 | tf_op jit(solution)/shard_map/ppermute | solution.py:32
  94.2 3.4 %collective-permute-start.18 = (bf16[2,8,16,768]{3,2,1,0:T(8,128)(2,1)S(1)}, bf16[2,8,16,768]{3,2,1,0:T(8,128)(2,1)S(1)}, u32[]{:S(2)}, u32[]{:S(2)}) collective-permute-start(bf16[2,8,16,768]{3,2,1,0:T(8,128)(2,1)S(1)} %collective-permute-done.12.refs_4_.refs_12_), channel_id=1, source_target_pairs={{0,8},{2,10},{8,12},{10,14},{12,4},{14,6},{4,0},{6,2},{1,9},{3,11}... | collective-permute-start | bytes 1179656 | tf_op jit(solution)/shard_map/ppermute | solution.py:32
  97.6 0.0 collective-permute-done.16.refs_7_
  97.6 0.7 copy-done.26
  98.3 6.5 %shard_map.84.refs_16_ = bf16[1,16,256]{2,1,0:T(8,128)(2,1)} custom-call(s32[1]{0:T(128)} %bitcast.me_ref, bf16[32,16,6144]{2,1,0:T(8,128)(2,1)} %bitcast.20, bf16[1,6144]{1,0:T(2,128)(2,1)} %gain_ref.7, bf16[16,16,768]{2,1,0:T(8,128)(2,1)} %get-tuple-element.30.refs_0_, bf16[2,32,16,768]{3,2,1,0:T(8,128)(2,1)} %copy-done.1, ...), custom_call_target="tpu_custom_call" | custom-call | flops 1 | bytes 1 | tf_op jit(solution)/shard_map/pallas_call | solution.py:340
  104.8 1.0 slice.12
  105.9 0.1 collective-permute-start.26
  106.1 0.5 collective-permute-start.20
  106.6 0.1 collective-permute-start.19
  106.7 1.0 collective-permute-done.20.refs_15_
  107.7 0.4 collective-permute-done.19.refs_7_
  108.1 0.3 copy-done.12
  108.4 0.4 copy-done.13
  108.7 0.7 copy-done.6
  109.5 4.1 %shard_map.86 = bf16[4,16,6272]{2,1,0:T(8,128)(2,1)} custom-call(s32[1]{0:T(128)} %bitcast.me_ref, bf16[32,16,6144]{2,1,0:T(8,128)(2,1)} %bitcast.21, bf16[1,6144]{1,0:T(2,128)(2,1)} %gain_ref.7, bf16[2,8,16,768]{3,2,1,0:T(8,128)(2,1)} %get-tuple-element.31.refs_0_.refs_8_, bf16[2,32,16,768]{3,2,1,0:T(8,128)(2,1)} %copy-done.1, ...), custom_call_target="tpu_custom_call" | custom-call | flops 1 | bytes 1 | tf_op jit(solution)/shard_map/pallas_call | solution.py:313
  113.6 0.5 collective-permute-start.24
  114.1 3.4 %collective-permute-done.26.refs_2_ = bf16[16,16,768]{2,1,0:T(8,128)(2,1)S(1)} collective-permute-done((bf16[16,16,768]{2,1,0:T(8,128)(2,1)S(1)}, bf16[16,16,768]{2,1,0:T(8,128)(2,1)S(1)}, u32[]{:S(2)}, u32[]{:S(2)}) %collective-permute-start.26) | collective-permute-done | bytes 393248 | tf_op jit(solution)/shard_map/ppermute | solution.py:32
  117.5 1.2 collective-permute-start.28
  118.7 4.0 %shard_map.85 = bf16[4,16,6144]{2,1,0:T(8,128)(2,1)} custom-call(s32[1]{0:T(128)} %bitcast.me_ref, bf16[32,16,6144]{2,1,0:T(8,128)(2,1)} %bitcast.22, bf16[1,6144]{1,0:T(2,128)(2,1)} %gain_ref.7, bf16[2,8,16,768]{3,2,1,0:T(8,128)(2,1)} %get-tuple-element.31.refs_0_.refs_8_, bf16[2,32,16,768]{3,2,1,0:T(8,128)(2,1)} %copy-done.1, ...), custom_call_target="tpu_custom_call" | custom-call | flops 1 | bytes 1 | tf_op jit(solution)/shard_map/pallas_call | solution.py:313
  122.7 1.2 shard_map.87.refs_0_
  123.9 4.3 %collective-permute-done.28.refs_4_ = bf16[16,16,768]{2,1,0:T(8,128)(2,1)S(1)} collective-permute-done((bf16[16,16,768]{2,1,0:T(8,128)(2,1)S(1)}, bf16[16,16,768]{2,1,0:T(8,128)(2,1)S(1)}, u32[]{:S(2)}, u32[]{:S(2)}) %collective-permute-start.28) | collective-permute-done | bytes 393248 | tf_op jit(solution)/shard_map/ppermute | solution.py:32
  128.2 2.2 %collective-permute-start.30 = (bf16[16,16,768]{2,1,0:T(8,128)(2,1)S(1)}, bf16[16,16,768]{2,1,0:T(8,128)(2,1)S(1)}, u32[]{:S(2)}, u32[]{:S(2)}) collective-permute-start(bf16[16,16,768]{2,1,0:T(8,128)(2,1)S(1)} %collective-permute-done.28.refs_4_), channel_id=1, source_target_pairs={{0,8},{2,10},{8,12},{10,14},{12,4},{14,6},{4,0},{6,2},{1,9},{3,11}... | collective-permute-start | bytes 1179656 | tf_op jit(solution)/shard_map/ppermute | solution.py:32
  130.5 0.5 collective-permute-start.22
  131.0 0.5 collective-permute-start.27
  131.5 6.5 %collective-permute-done.30.refs_6_ = bf16[16,16,768]{2,1,0:T(8,128)(2,1)S(1)} collective-permute-done((bf16[16,16,768]{2,1,0:T(8,128)(2,1)S(1)}, bf16[16,16,768]{2,1,0:T(8,128)(2,1)S(1)}, u32[]{:S(2)}, u32[]{:S(2)}) %collective-permute-start.30) | collective-permute-done | bytes 393248 | tf_op jit(solution)/shard_map/ppermute | solution.py:32
  138.1 0.5 collective-permute-start.31
  138.6 0.9 shard_map.88.refs_8_
  139.5 0.2 collective-permute-done.29.refs_5_
  139.8 0.6 collective-permute-done.31.refs_7_
  140.4 0.1 copy-done.22
  140.4 0.1 copy-done.24
  140.6 0.8 copy-done.25
  141.3 6.3 %shard_map.89.refs_0_ = bf16[32,16,6144]{2,1,0:T(8,128)(2,1)} custom-call(s32[1]{0:T(128)} %bitcast.me_ref, bf16[14,16,6144]{2,1,0:T(8,128)(2,1)} %collective-permute-done.23.carrier_ref, bf16[4,16,6144]{2,1,0:T(8,128)(2,1)} %copy-done.14, bf16[4,16,6272]{2,1,0:T(8,128)(2,1)} %copy-done, ...), custom_call_target="tpu_custom_call", output_to_operand_aliasing={{}: (12, {})} | custom-call | flops 1 | bytes 1 | tf_op jit(solution)/shard_map/pallas_call | solution.py:365
  147.6 3.1 %collective-permute-done.22.block_ref = bf16[4,16,6144]{2,1,0:T(8,128)(2,1)S(1)} collective-permute-done((bf16[4,16,6144]{2,1,0:T(8,128)(2,1)S(1)}, bf16[4,16,6144]{2,1,0:T(8,128)(2,1)S(1)}, u32[]{:S(2)}, u32[]{:S(2)}) %collective-permute-start.22) | collective-permute-done | bytes 786464 | tf_op jit(solution)/shard_map/ppermute | solution.py:19
  150.7 0.9 shard_map.90
  (67 shorter events, 0.2 us)
Async XLA Ops:
  1.2 31.3 %collective-permute-start.1 = (bf16[4,16,6144]{2,1,0:T(8,128)(2,1)S(1)}, bf16[4,16,6144]{2,1,0:T(8,128)(2,1)S(1)}, u32[]{:S(2)}, u32[]{:S(2)}) collective-permute-start(bf16[4,16,6144]{2,1,0:T(8,128)(2,1)S(1)} %slice_bitcast_fusion), channel_id=1, source_target_pairs={{1,0},{0,1},{3,2},{2,3},{5,4},{4,5},{7,6},{6,7},{9,8},{8,9},{11,10... | collective-permute-start | bytes 2359304 | tf_op jit(solution)/shard_map/ppermute | solution.py:19
  18.2 11.0 %collective-permute-start.2 = (bf16[2,8,16,768]{3,2,1,0:T(8,128)(2,1)}, bf16[2,8,16,768]{3,2,1,0:T(8,128)(2,1)S(1)}, u32[]{:S(2)}, u32[]{:S(2)}) collective-permute-start(bf16[2,8,16,768]{3,2,1,0:T(8,128)(2,1)} %get-tuple-element.29.refs_0_.refs_8_), channel_id=1, source_target_pairs={{0,8},{2,10},{8,12},{10,14},{12,4},{14,6},{4,0},{6,2},{1,9},{3,11}... | collective-permute-start | bytes 1179656 | tf_op jit(solution)/shard_map/ppermute | solution.py:32
  20.8 84.0 %collective-permute-start.23 = (bf16[14,16,6144]{2,1,0:T(8,128)(2,1)}, bf16[14,16,6144]{2,1,0:T(8,128)(2,1)}, u32[]{:S(2)}, u32[]{:S(2)}) collective-permute-start(bf16[14,16,6144]{2,1,0:T(8,128)(2,1)} %get-tuple-element.40), channel_id=1, source_target_pairs={{1,0},{0,1},{3,2},{2,3},{5,4},{4,5},{7,6},{6,7},{9,8},{8,9},{11,10... | collective-permute-start | bytes 8257544 | tf_op jit(solution)/shard_map/ppermute | solution.py:19
  21.4 45.1 %collective-permute-start = (bf16[2,32,16,768]{3,2,1,0:T(8,128)(2,1)}, bf16[2,32,16,768]{3,2,1,0:T(8,128)(2,1)S(1)}, u32[]{:S(2)}, u32[]{:S(2)}) collective-permute-start(bf16[2,32,16,768]{3,2,1,0:T(8,128)(2,1)} %get-tuple-element.27), channel_id=1, source_target_pairs={{0,2},{2,0},{4,6},{6,4},{8,10},{10,8},{12,14},{14,12},{1,3},{3,1},... | collective-permute-start | bytes 4718600 | tf_op jit(solution)/shard_map/ppermute | solution.py:37
  29.2 37.2 %copy-start.8 = (bf16[2,8,16,768]{3,2,1,0:T(8,128)(2,1)}, bf16[2,8,16,768]{3,2,1,0:T(8,128)(2,1)S(1)}, u32[]{:S(2)}) copy-start(bf16[2,8,16,768]{3,2,1,0:T(8,128)(2,1)S(1)} %collective-permute-done.2.refs_2_.refs_10_) | copy-start | bytes 1179652
  29.3 12.8 %collective-permute-start.4 = (bf16[2,8,16,768]{3,2,1,0:T(8,128)(2,1)S(1)}, bf16[2,8,16,768]{3,2,1,0:T(8,128)(2,1)S(1)}, u32[]{:S(2)}, u32[]{:S(2)}) collective-permute-start(bf16[2,8,16,768]{3,2,1,0:T(8,128)(2,1)S(1)} %collective-permute-done.2.refs_2_.refs_10_), channel_id=1, source_target_pairs={{0,8},{2,10},{8,12},{10,14},{12,4},{14,6},{4,0},{6,2},{1,9},{3,11}... | collective-permute-start | bytes 1179656 | tf_op jit(solution)/shard_map/ppermute | solution.py:32
  32.5 9.6 %collective-permute-start.8 = (bf16[2,8,16,768]{3,2,1,0:T(8,128)(2,1)S(1)}, bf16[2,8,16,768]{3,2,1,0:T(8,128)(2,1)S(1)}, u32[]{:S(2)}, u32[]{:S(2)}) collective-permute-start(bf16[2,8,16,768]{3,2,1,0:T(8,128)(2,1)S(1)} %collective-permute-done.2.refs_2_.refs_10_), channel_id=1, source_target_pairs={{0,2},{2,0},{4,6},{6,4},{8,10},{10,8},{12,14},{14,12},{1,3},{3,1},... | collective-permute-start | bytes 1179656 | tf_op jit(solution)/shard_map/ppermute | solution.py:37
  32.5 33.9 %copy-start.14 = (bf16[4,16,6144]{2,1,0:T(8,128)(2,1)}, bf16[4,16,6144]{2,1,0:T(8,128)(2,1)S(1)}, u32[]{:S(2)}) copy-start(bf16[4,16,6144]{2,1,0:T(8,128)(2,1)S(1)} %collective-permute-done.1.early_ref) | copy-start | bytes 2359300
  32.5 17.7 %collective-permute-start.3 = (bf16[16,16,768]{2,1,0:T(8,128)(2,1)}, bf16[16,16,768]{2,1,0:T(8,128)(2,1)}, u32[]{:S(2)}, u32[]{:S(2)}) collective-permute-start(bf16[16,16,768]{2,1,0:T(8,128)(2,1)} %get-tuple-element.30.refs_0_), channel_id=1, source_target_pairs={{0,8},{2,10},{8,12},{10,14},{12,4},{14,6},{4,0},{6,2},{1,9},{3,11}... | collective-permute-start | bytes 1179656 | tf_op jit(solution)/shard_map/ppermute | solution.py:32
  42.1 24.4 %copy-start.9 = (bf16[2,8,16,768]{3,2,1,0:T(8,128)(2,1)}, bf16[2,8,16,768]{3,2,1,0:T(8,128)(2,1)S(1)}, u32[]{:S(2)}) copy-start(bf16[2,8,16,768]{3,2,1,0:T(8,128)(2,1)S(1)} %collective-permute-done.4.refs_4_.refs_12_) | copy-start | bytes 1179652
  42.1 8.1 %collective-permute-start.5 = (bf16[2,8,16,768]{3,2,1,0:T(8,128)(2,1)S(1)}, bf16[2,8,16,768]{3,2,1,0:T(8,128)(2,1)S(1)}, u32[]{:S(2)}, u32[]{:S(2)}) collective-permute-start(bf16[2,8,16,768]{3,2,1,0:T(8,128)(2,1)S(1)} %collective-permute-done.4.refs_4_.refs_12_), channel_id=1, source_target_pairs={{0,2},{2,0},{4,6},{6,4},{8,10},{10,8},{12,14},{14,12},{1,3},{3,1},... | collective-permute-start | bytes 1179656 | tf_op jit(solution)/shard_map/ppermute | solution.py:37
  42.1 24.4 %copy-start.10 = (bf16[2,8,16,768]{3,2,1,0:T(8,128)(2,1)}, bf16[2,8,16,768]{3,2,1,0:T(8,128)(2,1)S(1)}, u32[]{:S(2)}) copy-start(bf16[2,8,16,768]{3,2,1,0:T(8,128)(2,1)S(1)} %collective-permute-done.8.refs_3_.refs_11_) | copy-start | bytes 1179652
  42.1 15.8 %collective-permute-start.9 = (bf16[2,8,16,768]{3,2,1,0:T(8,128)(2,1)S(1)}, bf16[2,8,16,768]{3,2,1,0:T(8,128)(2,1)}, u32[]{:S(2)}, u32[]{:S(2)}) collective-permute-start(bf16[2,8,16,768]{3,2,1,0:T(8,128)(2,1)S(1)} %collective-permute-done.4.refs_4_.refs_12_), channel_id=1, source_target_pairs={{0,8},{2,10},{8,12},{10,14},{12,4},{14,6},{4,0},{6,2},{1,9},{3,11}... | collective-permute-start | bytes 1179656 | tf_op jit(solution)/shard_map/ppermute | solution.py:32
  50.2 7.7 %collective-permute-start.10 = (bf16[16,16,768]{2,1,0:T(8,128)(2,1)}, bf16[16,16,768]{2,1,0:T(8,128)(2,1)S(1)}, u32[]{:S(2)}, u32[]{:S(2)}) collective-permute-start(bf16[16,16,768]{2,1,0:T(8,128)(2,1)} %collective-permute-done.3.refs_2_), channel_id=1, source_target_pairs={{0,2},{2,0},{4,6},{6,4},{8,10},{10,8},{12,14},{14,12},{1,3},{3,1},... | collective-permute-start | bytes 1179656 | tf_op jit(solution)/shard_map/ppermute | solution.py:37
  50.2 0.8 copy-start.11
  51.0 15.5 %collective-permute-start.6 = (bf16[2,8,16,768]{3,2,1,0:T(8,128)(2,1)}, bf16[2,8,16,768]{3,2,1,0:T(8,128)(2,1)S(1)}, u32[]{:S(2)}, u32[]{:S(2)}) collective-permute-start(bf16[2,8,16,768]{3,2,1,0:T(8,128)(2,1)} %get-tuple-element.31.refs_0_.refs_8_), channel_id=1, source_target_pairs={{0,8},{2,10},{8,12},{10,14},{12,4},{14,6},{4,0},{6,2},{1,9},{3,11}... | collective-permute-start | bytes 1179656 | tf_op jit(solution)/shard_map/ppermute | solution.py:32
  57.9 8.6 %collective-permute-start.14 = (bf16[2,8,16,768]{3,2,1,0:T(8,128)(2,1)}, bf16[2,8,16,768]{3,2,1,0:T(8,128)(2,1)}, u32[]{:S(2)}, u32[]{:S(2)}) collective-permute-start(bf16[2,8,16,768]{3,2,1,0:T(8,128)(2,1)} %collective-permute-done.9.refs_6_.refs_14_), channel_id=1, source_target_pairs={{0,2},{2,0},{4,6},{6,4},{8,10},{10,8},{12,14},{14,12},{1,3},{3,1},... | collective-permute-start | bytes 1179656 | tf_op jit(solution)/shard_map/ppermute | solution.py:37
  57.9 8.5 %copy-start.17 = (bf16[16,16,768]{2,1,0:T(8,128)(2,1)}, bf16[16,16,768]{2,1,0:T(8,128)(2,1)S(1)}, u32[]{:S(2)}) copy-start(bf16[16,16,768]{2,1,0:T(8,128)(2,1)S(1)} %collective-permute-done.10.refs_3_) | copy-start | bytes 1179652
  57.9 15.6 %collective-permute-start.11 = (bf16[16,16,768]{2,1,0:T(8,128)(2,1)}, bf16[16,16,768]{2,1,0:T(8,128)(2,1)}, u32[]{:S(2)}, u32[]{:S(2)}) collective-permute-start(bf16[16,16,768]{2,1,0:T(8,128)(2,1)} %collective-permute-done.3.refs_2_), channel_id=1, source_target_pairs={{0,8},{2,10},{8,12},{10,14},{12,4},{14,6},{4,0},{6,2},{1,9},{3,11}... | collective-permute-start | bytes 1179656 | tf_op jit(solution)/shard_map/ppermute | solution.py:32
  66.4 41.6 %copy-start.3 = (bf16[2,8,16,768]{3,2,1,0:T(8,128)(2,1)}, bf16[2,8,16,768]{3,2,1,0:T(8,128)(2,1)S(1)}, u32[]{:S(2)}) copy-start(bf16[2,8,16,768]{3,2,1,0:T(8,128)(2,1)S(1)} %collective-permute-done.6.refs_2_.refs_10_) | copy-start | bytes 1179652
  66.4 10.5 %collective-permute-start.7 = (bf16[2,8,16,768]{3,2,1,0:T(8,128)(2,1)S(1)}, bf16[2,8,16,768]{3,2,1,0:T(8,128)(2,1)S(1)}, u32[]{:S(2)}, u32[]{:S(2)}) collective-permute-start(bf16[2,8,16,768]{3,2,1,0:T(8,128)(2,1)S(1)} %collective-permute-done.6.refs_2_.refs_10_), channel_id=1, source_target_pairs={{0,2},{2,0},{4,6},{6,4},{8,10},{10,8},{12,14},{14,12},{1,3},{3,1},... | collective-permute-start | bytes 1179656 | tf_op jit(solution)/shard_map/ppermute | solution.py:37
  66.5 1.2 copy-start.1
  73.5 13.2 %collective-permute-start.15 = (bf16[16,16,768]{2,1,0:T(8,128)(2,1)}, bf16[16,16,768]{2,1,0:T(8,128)(2,1)S(1)}, u32[]{:S(2)}, u32[]{:S(2)}) collective-permute-start(bf16[16,16,768]{2,1,0:T(8,128)(2,1)} %collective-permute-done.11.refs_4_), channel_id=1, source_target_pairs={{0,8},{2,10},{8,12},{10,14},{12,4},{14,6},{4,0},{6,2},{1,9},{3,11}... | collective-permute-start | bytes 1179656 | tf_op jit(solution)/shard_map/ppermute | solution.py:32
  76.9 29.2 %copy-start.4 = (bf16[2,8,16,768]{3,2,1,0:T(8,128)(2,1)}, bf16[2,8,16,768]{3,2,1,0:T(8,128)(2,1)S(1)}, u32[]{:S(2)}) copy-start(bf16[2,8,16,768]{3,2,1,0:T(8,128)(2,1)S(1)} %collective-permute-done.7.refs_3_.refs_11_) | copy-start | bytes 1179652
  76.9 9.8 %collective-permute-start.13 = (bf16[16,16,768]{2,1,0:T(8,128)(2,1)}, bf16[16,16,768]{2,1,0:T(8,128)(2,1)S(1)}, u32[]{:S(2)}, u32[]{:S(2)}) collective-permute-start(bf16[16,16,768]{2,1,0:T(8,128)(2,1)} %collective-permute-done.11.refs_4_), channel_id=1, source_target_pairs={{0,2},{2,0},{4,6},{6,4},{8,10},{10,8},{12,14},{14,12},{1,3},{3,1},... | collective-permute-start | bytes 1179656 | tf_op jit(solution)/shard_map/ppermute | solution.py:37
  76.9 17.3 %collective-permute-start.12 = (bf16[2,8,16,768]{3,2,1,0:T(8,128)(2,1)S(1)}, bf16[2,8,16,768]{3,2,1,0:T(8,128)(2,1)S(1)}, u32[]{:S(2)}, u32[]{:S(2)}) collective-permute-start(bf16[2,8,16,768]{3,2,1,0:T(8,128)(2,1)S(1)} %collective-permute-done.6.refs_2_.refs_10_), channel_id=1, source_target_pairs={{0,8},{2,10},{8,12},{10,14},{12,4},{14,6},{4,0},{6,2},{1,9},{3,11}... | collective-permute-start | bytes 1179656 | tf_op jit(solution)/shard_map/ppermute | solution.py:32
  77.1 45.6 %collective-permute-start.21 = (bf16[8,16,6144]{2,1,0:T(8,128)(2,1)}, bf16[8,16,6144]{2,1,0:T(8,128)(2,1)S(1)}, u32[]{:S(2)}, u32[]{:S(2)}) collective-permute-start(bf16[8,16,6144]{2,1,0:T(8,128)(2,1)} %shard_map.83), channel_id=1, source_target_pairs={{1,0},{0,1},{3,2},{2,3},{5,4},{4,5},{7,6},{6,7},{9,8},{8,9},{11,10... | collective-permute-start | bytes 4718600 | tf_op jit(solution)/shard_map/ppermute | solution.py:19
  86.7 10.9 %copy-start.21 = (bf16[16,16,768]{2,1,0:T(8,128)(2,1)}, bf16[16,16,768]{2,1,0:T(8,128)(2,1)S(1)}, u32[]{:S(2)}) copy-start(bf16[16,16,768]{2,1,0:T(8,128)(2,1)S(1)} %collective-permute-done.15.refs_6_) | copy-start | bytes 1179652
  86.7 10.9 %collective-permute-start.16 = (bf16[16,16,768]{2,1,0:T(8,128)(2,1)S(1)}, bf16[16,16,768]{2,1,0:T(8,128)(2,1)S(1)}, u32[]{:S(2)}, u32[]{:S(2)}) collective-permute-start(bf16[16,16,768]{2,1,0:T(8,128)(2,1)S(1)} %collective-permute-done.15.refs_6_), channel_id=1, source_target_pairs={{0,2},{2,0},{4,6},{6,4},{8,10},{10,8},{12,14},{14,12},{1,3},{3,1},... | collective-permute-start | bytes 1179656 | tf_op jit(solution)/shard_map/ppermute | solution.py:37
  86.7 10.9 %copy-start.23 = (bf16[16,16,768]{2,1,0:T(8,128)(2,1)}, bf16[16,16,768]{2,1,0:T(8,128)(2,1)S(1)}, u32[]{:S(2)}) copy-start(bf16[16,16,768]{2,1,0:T(8,128)(2,1)S(1)} %collective-permute-done.13.refs_5_) | copy-start | bytes 1179652
  94.2 11.9 %copy-start.5 = (bf16[2,8,16,768]{3,2,1,0:T(8,128)(2,1)}, bf16[2,8,16,768]{3,2,1,0:T(8,128)(2,1)S(1)}, u32[]{:S(2)}) copy-start(bf16[2,8,16,768]{3,2,1,0:T(8,128)(2,1)S(1)} %collective-permute-done.12.refs_4_.refs_12_) | copy-start | bytes 1179652
  94.2 11.8 %collective-permute-start.18 = (bf16[2,8,16,768]{3,2,1,0:T(8,128)(2,1)S(1)}, bf16[2,8,16,768]{3,2,1,0:T(8,128)(2,1)S(1)}, u32[]{:S(2)}, u32[]{:S(2)}) collective-permute-start(bf16[2,8,16,768]{3,2,1,0:T(8,128)(2,1)S(1)} %collective-permute-done.12.refs_4_.refs_12_), channel_id=1, source_target_pairs={{0,8},{2,10},{8,12},{10,14},{12,4},{14,6},{4,0},{6,2},{1,9},{3,11}... | collective-permute-start | bytes 1179656 | tf_op jit(solution)/shard_map/ppermute | solution.py:32
  97.6 0.7 copy-start.26
  104.8 3.2 %collective-permute-start.17 = (bf16[2,8,16,768]{3,2,1,0:T(8,128)(2,1)S(1)}, bf16[2,8,16,768]{3,2,1,0:T(8,128)(2,1)S(1)}, u32[]{:S(2)}, u32[]{:S(2)}) collective-permute-start(bf16[2,8,16,768]{3,2,1,0:T(8,128)(2,1)S(1)} %collective-permute-done.12.refs_4_.refs_12_), channel_id=1, source_target_pairs={{0,2},{2,0},{4,6},{6,4},{8,10},{10,8},{12,14},{14,12},{1,3},{3,1},... | collective-permute-start | bytes 1179656 | tf_op jit(solution)/shard_map/ppermute | solution.py:37
  105.9 25.1 %copy-start.7 = (bf16[2,2,8,8,768]{4,3,1,2,0:T(8,128)(2,1)}, bf16[2,2,8,8,768]{4,3,1,2,0:T(8,128)(2,1)S(1)}, u32[]{:S(2)}) copy-start(bf16[2,2,8,8,768]{4,3,1,2,0:T(8,128)(2,1)S(1)} %copy.15) | copy-start | bytes 1179652
  105.9 11.6 %collective-permute-start.26 = (bf16[16,16,768]{2,1,0:T(8,128)(2,1)S(1)}, bf16[16,16,768]{2,1,0:T(8,128)(2,1)S(1)}, u32[]{:S(2)}, u32[]{:S(2)}) collective-permute-start(bf16[16,16,768]{2,1,0:T(8,128)(2,1)S(1)} %bitcast.24), channel_id=1, source_target_pairs={{0,8},{2,10},{8,12},{10,14},{12,4},{14,6},{4,0},{6,2},{1,9},{3,11}... | collective-permute-start | bytes 1179656 | tf_op jit(solution)/shard_map/ppermute | solution.py:32
  106.0 2.0 %copy-start.2 = (bf16[2,8,16,768]{3,2,1,0:T(8,128)(2,1)}, bf16[2,8,16,768]{3,2,1,0:T(8,128)(2,1)S(1)}, u32[]{:S(2)}) copy-start(bf16[2,8,16,768]{3,2,1,0:T(8,128)(2,1)S(1)} %collective-permute-done.18.refs_6_.refs_14_) | copy-start | bytes 1179652
  106.1 1.6 %collective-permute-start.20 = (bf16[8,16,768]{2,1,0:T(8,128)(2,1)S(1)}, bf16[8,16,768]{2,1,0:T(8,128)(2,1)S(1)}, u32[]{:S(2)}, u32[]{:S(2)}) collective-permute-start(bf16[8,16,768]{2,1,0:T(8,128)(2,1)S(1)} %get-tuple-element.47), channel_id=1, source_target_pairs={{0,2},{2,0},{4,6},{6,4},{8,10},{10,8},{12,14},{14,12},{1,3},{3,1},... | collective-permute-start | bytes 589832 | tf_op jit(solution)/shard_map/ppermute | solution.py:37
  106.6 1.4 collective-permute-start.19
  107.7 0.7 copy-start.12
  108.1 0.7 copy-start.13
  108.7 0.7 copy-start.6
  113.6 24.5 %collective-permute-start.24 = (bf16[4,16,6272]{2,1,0:T(8,128)(2,1)}, bf16[4,16,6272]{2,1,0:T(8,128)(2,1)S(1)}, u32[]{:S(2)}, u32[]{:S(2)}) collective-permute-start(bf16[4,16,6272]{2,1,0:T(8,128)(2,1)} %shard_map.86), channel_id=1, source_target_pairs={{1,0},{0,1},{3,2},{2,3},{5,4},{4,5},{7,6},{6,7},{9,8},{8,9},{11,10... | collective-permute-start | bytes 2408456 | tf_op jit(solution)/shard_map/ppermute | solution.py:19
  117.5 13.5 %copy-start.16 = (bf16[16,16,768]{2,1,0:T(8,128)(2,1)}, bf16[16,16,768]{2,1,0:T(8,128)(2,1)S(1)}, u32[]{:S(2)}) copy-start(bf16[16,16,768]{2,1,0:T(8,128)(2,1)S(1)} %collective-permute-done.26.refs_2_) | copy-start | bytes 1179652
  117.5 10.7 %collective-permute-start.28 = (bf16[16,16,768]{2,1,0:T(8,128)(2,1)S(1)}, bf16[16,16,768]{2,1,0:T(8,128)(2,1)S(1)}, u32[]{:S(2)}, u32[]{:S(2)}) collective-permute-start(bf16[16,16,768]{2,1,0:T(8,128)(2,1)S(1)} %collective-permute-done.26.refs_2_), channel_id=1, source_target_pairs={{0,8},{2,10},{8,12},{10,14},{12,4},{14,6},{4,0},{6,2},{1,9},{3,11}... | collective-permute-start | bytes 1179656 | tf_op jit(solution)/shard_map/ppermute | solution.py:32
  122.7 7.8 %copy-start.15 = (bf16[4,16,6144]{2,1,0:T(8,128)(2,1)S(1)}, bf16[4,16,6144]{2,1,0:T(8,128)(2,1)}, u32[]{:S(2)}) copy-start(bf16[4,16,6144]{2,1,0:T(8,128)(2,1)} %shard_map.85) | copy-start | bytes 2359300
  128.2 11.3 %copy-start.18 = (bf16[16,16,768]{2,1,0:T(8,128)(2,1)}, bf16[16,16,768]{2,1,0:T(8,128)(2,1)S(1)}, u32[]{:S(2)}) copy-start(bf16[16,16,768]{2,1,0:T(8,128)(2,1)S(1)} %collective-permute-done.28.refs_4_) | copy-start | bytes 1179652
  128.2 9.8 %collective-permute-start.30 = (bf16[16,16,768]{2,1,0:T(8,128)(2,1)S(1)}, bf16[16,16,768]{2,1,0:T(8,128)(2,1)S(1)}, u32[]{:S(2)}, u32[]{:S(2)}) collective-permute-start(bf16[16,16,768]{2,1,0:T(8,128)(2,1)S(1)} %collective-permute-done.28.refs_4_), channel_id=1, source_target_pairs={{0,8},{2,10},{8,12},{10,14},{12,4},{14,6},{4,0},{6,2},{1,9},{3,11}... | collective-permute-start | bytes 1179656 | tf_op jit(solution)/shard_map/ppermute | solution.py:32
  130.5 20.2 %collective-permute-start.22 = (bf16[4,16,6144]{2,1,0:T(8,128)(2,1)S(1)}, bf16[4,16,6144]{2,1,0:T(8,128)(2,1)S(1)}, u32[]{:S(2)}, u32[]{:S(2)}) collective-permute-start(bf16[4,16,6144]{2,1,0:T(8,128)(2,1)S(1)} %copy-done.15), channel_id=1, source_target_pairs={{1,0},{0,1},{3,2},{2,3},{5,4},{4,5},{7,6},{6,7},{9,8},{8,9},{11,10... | collective-permute-start | bytes 2359304 | tf_op jit(solution)/shard_map/ppermute | solution.py:19
  131.0 8.5 %collective-permute-start.25 = (bf16[16,16,768]{2,1,0:T(8,128)(2,1)S(1)}, bf16[16,16,768]{2,1,0:T(8,128)(2,1)S(1)}, u32[]{:S(2)}, u32[]{:S(2)}) collective-permute-start(bf16[16,16,768]{2,1,0:T(8,128)(2,1)S(1)} %bitcast.25), channel_id=1, source_target_pairs={{0,2},{2,0},{4,6},{6,4},{8,10},{10,8},{12,14},{14,12},{1,3},{3,1},... | collective-permute-start | bytes 1179656 | tf_op jit(solution)/shard_map/ppermute | solution.py:37
  131.0 8.5 %collective-permute-start.27 = (bf16[16,16,768]{2,1,0:T(8,128)(2,1)S(1)}, bf16[16,16,768]{2,1,0:T(8,128)(2,1)S(1)}, u32[]{:S(2)}, u32[]{:S(2)}) collective-permute-start(bf16[16,16,768]{2,1,0:T(8,128)(2,1)S(1)} %collective-permute-done.26.refs_2_), channel_id=1, source_target_pairs={{0,2},{2,0},{4,6},{6,4},{8,10},{10,8},{12,14},{14,12},{1,3},{3,1},... | collective-permute-start | bytes 1179656 | tf_op jit(solution)/shard_map/ppermute | solution.py:37
  138.1 1.4 copy-start.19
  138.1 1.7 %collective-permute-start.29 = (bf16[16,16,768]{2,1,0:T(8,128)(2,1)S(1)}, bf16[16,16,768]{2,1,0:T(8,128)(2,1)S(1)}, u32[]{:S(2)}, u32[]{:S(2)}) collective-permute-start(bf16[16,16,768]{2,1,0:T(8,128)(2,1)S(1)} %collective-permute-done.28.refs_4_), channel_id=1, source_target_pairs={{0,2},{2,0},{4,6},{6,4},{8,10},{10,8},{12,14},{14,12},{1,3},{3,1},... | collective-permute-start | bytes 1179656 | tf_op jit(solution)/shard_map/ppermute | solution.py:37
  138.1 1.4 copy-start
  138.1 2.3 %collective-permute-start.31 = (bf16[16,16,768]{2,1,0:T(8,128)(2,1)S(1)}, bf16[16,16,768]{2,1,0:T(8,128)(2,1)S(1)}, u32[]{:S(2)}, u32[]{:S(2)}) collective-permute-start(bf16[16,16,768]{2,1,0:T(8,128)(2,1)S(1)} %collective-permute-done.30.refs_6_), channel_id=1, source_target_pairs={{0,2},{2,0},{4,6},{6,4},{8,10},{10,8},{12,14},{14,12},{1,3},{3,1},... | collective-permute-start | bytes 1179656 | tf_op jit(solution)/shard_map/ppermute | solution.py:37
  139.5 0.8 copy-start.20
  139.5 0.9 copy-start.22
  139.8 0.8 copy-start.24
  140.6 0.8 copy-start.25
